TPU v7x, 256 devices: a whole 4x4x8 slice. The times are simulated.
256 devices in a mesh: row: 16 (over y, x), col: 16 (over z, core).
Axes of the slice: x: 4, y: 4, z: 8, core: 2. Of those that a mesh axis runs over, the one named last changes fastest.
Arguments:
- ids: int32 [2048], replicated, may hold values from 0 to 31999, as said below
- alpha: bfloat16 [2048, 2048], P('col', 'row'), may hold values from 0.0099487305 to 1
- beta: bfloat16 [2048, 32768], P('row', 'col'), may hold values from 0.0099487305 to 1
- emission: bfloat16 [32000, 32768], P('row', 'col'), may hold values from 0.049804688 to 1
- transition: bfloat16 [2048, 32768], P('row', 'col'), may hold values from 0.001 to 30, as said below
Outputs:
- counts: float32 [2048, 32768], P('row', 'col')
- new_trans: bfloat16 [2048, 32768], P('row', 'col')
Inputs may be any that keep to these rules, and one draw needn't show every extreme that they name: Split the rows into 16 aligned blocks of 128 rows and the ids into 16 ranges of 2000 consecutive values: every block holds exactly 8 ids of every range. `transition`: positive weights.
All inputs are finite; a program needn't handle non-finite values.
Results may differ from a plain program's by a relative error of at most 0.0023.
Values may be sent and summed in bfloat16 or wider, within the bound.
No kernel may reach another device: no remote copies, remote signals or barrier semaphores. Data moves between devices by JAX's collectives and lax.ppermute only.
A program may use at most 128 MiB of HBM per device.

v0:
```python
import jax
import jax.numpy as jnp
from jax import lax
from jax.sharding import PartitionSpec as P

STATES = 32768


def per_device(ids, alpha, beta, emission, transition):
    vocab_dev = emission.shape[0]
    my_row = lax.axis_index("row")
    word_base = my_row * vocab_dev
    alpha_full = lax.all_gather(alpha, "col", axis=0, tiled=True)
    local = ids - word_base
    inside = (local >= 0) & (local < vocab_dev)
    picked = jnp.take(emission, jnp.clip(local, 0, vocab_dev - 1), axis=0)
    emitted = lax.psum(
        jnp.where(inside[:, None], picked.astype(jnp.float32), 0.0).astype(jnp.bfloat16), "row"
    ).astype(jnp.float32)
    beta_full = lax.all_gather(beta, "row", axis=0, tiled=True)
    scaled = (emitted * beta_full.astype(jnp.float32)).astype(jnp.bfloat16)
    expected = lax.dot_general(
        alpha_full, scaled, (((0,), (0,)), ((), ())), preferred_element_type=jnp.float32
    )
    counts = transition.astype(jnp.float32) * expected
    totals = lax.psum(jnp.sum(counts, axis=1), "col")
    new_trans = (STATES * counts / totals[:, None]).astype(jnp.bfloat16)
    return (counts, new_trans)


def solution(mesh):
    in_specs = (P(), P("col", "row"), P("row", "col"), P("row", "col"), P("row", "col"))
    out_specs = (P("row", "col"), P("row", "col"))
    return jax.shard_map(
        per_device, mesh=mesh, in_specs=in_specs, out_specs=out_specs, check_vma=False
    )
```

profile of v0, /device:TPU:2, one launch (start us, length us, event | category | flops | bytes accessed | tf_op | source)
XLA Modules:
  0.0 314.9 jit_solution(6593720873610163947)
XLA Ops:
  7.2 0.0 all-reduce.2.cloned.1.call-start
  7.2 0.7 compare_and_fusion.1
  7.9 0.7 fusion.3
  8.6 20.7 %gather_fusion = bf16[2048,2048]{1,0:T(8,128)(2,1)} fusion(bf16[2000,2048]{1,0:T(8,128)(2,1)} %param.8, s32[2048]{0:T(1024)S(1)} %fusion.3), kind=kCustom, calls=%fused_computation | custom fusion | bytes 16785408 | tf_op jit(solution)/shard_map/jit(_take)/gather | solution.py:16
  29.4 8.3 %select_convert_fusion = bf16[2048,2048]{1,0:T(8,128)(2,1)} fusion(bf16[2048,2048]{1,0:T(8,128)(2,1)} %gather_fusion, pred[2048]{0:T(1024)(128)(4,1)S(1)} %get-tuple-element.5, pred[2048]{0:T(1024)(128)(4,1)S(1)} %get-tuple-element.4), kind=kLoop, calls=%fused_computation.2 | loop fusion | flops 16777216 | bytes 16781312 | tf_op jit(solution)/shard_map/convert_element_type | solution.py:18
  37.7 0.0 copy-start
  37.7 0.0 copy-start.1
  37.7 0.0 all-reduce.2.cloned.1.call-update
  37.7 0.0 all-gather.2.cloned.1.call-start
  37.8 0.7 all-gather.2.cloned.1.call-update
  38.5 0.3 copy-done
  38.7 0.3 copy.7
  39.0 0.0 copy-done.1
  39.0 21.4 %all_gather.7 = bf16[2048,128]{1,0:T(8,128)(2,1)S(1)} all-gather(bf16[128,128]{1,0:T(8,128)(2,1)S(1)} %copy-done.1), channel_id=1, replica_groups=mesh['row'=16,'col'=16] {'col'}, dimensions={0}, use_global_device_ids=true | all-gather | bytes 557056 | tf_op jit(solution)/shard_map/all_gather | solution.py:13
  60.4 130.8 %all-reduce.2.cloned.1.call-done = bf16[2048,2048]{1,0:T(8,128)(2,1)} async-done(((bf16[2048,2048]{1,0:T(8,128)(2,1)}), bf16[2048,2048]{1,0:T(8,128)(2,1)}) %all-reduce.2.cloned.1.call-update) | async-done | bytes 8388624 | tf_op jit(solution)/shard_map/psum | solution.py:17
  191.3 78.7 %all-gather.2.cloned.1.call-done = bf16[2048,2048]{1,0:T(8,128)(2,1)} async-done(((bf16[128,2048]{1,0:T(8,128)(2,1)}), bf16[2048,2048]{1,0:T(8,128)(2,1)}) %all-gather.2.cloned.1.call-update) | async-done | bytes 8388624 | tf_op jit(solution)/shard_map/all_gather | solution.py:20
  269.9 9.5 %fusion.4 = (f32[128]{0:T(128)S(1)}, f32[128,2048]{0,1:T(8,128)S(1)}) fusion(bf16[2048,128]{1,0:T(8,128)(2,1)S(1)} %all_gather.7, bf16[2048,2048]{1,0:T(8,128)(2,1)} %all-gather.2.cloned.1.call-done, bf16[2048,2048]{1,0:T(8,128)(2,1)} %all-reduce.2.cloned.1.call-done, bf16[128,2048]{0,1:T(8,128)(2,1)S(1)} %copy.7), kind=kOutput, calls=%fused_computation.11 | convolution fusion | flops 1091305344 | bytes 18874880 | tf_op jit(solution)/shard_map/dot_general | solution.py:22
  279.4 26.2 %psum.15 = f32[128]{0:T(128)S(1)} all-reduce(f32[128]{0:T(128)S(1)} %get-tuple-element.6), channel_id=1, replica_groups=mesh['row'=16,'col'=16] {'col'}, use_global_device_ids=true, to_apply=%region_2.3 | all-reduce | flops 128 | bytes 1024 | tf_op jit(solution)/shard_map/psum | solution.py:26
  305.7 1.3 copy.8
  307.0 0.1 divide_convert_fusion
  307.1 1.0 copy.9
Async XLA Ops:
  7.2 184.1 %all-reduce.2.cloned.1.call-start = ((), (), s32[]{:S(2)}) async-start(), calls=%async_computation | async-start | bytes 16777216 | tf_op jit(solution)/shard_map/psum | solution.py:17
  37.7 1.0 copy-start
  37.7 1.3 copy-start.1
  37.7 232.2 %all-gather.2.cloned.1.call-start = ((), (), s32[]{:S(2)}) async-start(), calls=%async_computation.1 | async-start | bytes 8912896 | tf_op jit(solution)/shard_map/all_gather | solution.py:20
Sparse Core Ops, SparseCore 0:
  37.8 153.3 all-reduce.1
  194.0 75.9 all-gather.1
where the time goes:
time: 315 us
  waiting for transfers between devices  210 us (67%)
  blocking collectives  47.7 us (15%)
  local copies, waits for them, and re-layouts  23.6 us (7%)
  between operations  14.1 us (4%)
  other arithmetic  9.85 us (3%)
  matrix products  9.47 us (3%)
    psum x1, waiting for transfers between devices, per_device(): lax.psum(jnp.where(inside[:, None], picked.astype(jnp.float32), 0.0).asty...  131 us
    all_gather x1, waiting for transfers between devices, per_device(): beta_full = lax.all_gather(beta, 'row', axis=0, tiled=True)  78.7 us
    psum x1, blocking collectives, per_device(): totals = lax.psum(jnp.sum(counts, axis=1), 'col')  26.2 us
    all_gather x1, blocking collectives, per_device(): alpha_full = lax.all_gather(alpha, 'col', axis=0, tiled=True)  21.4 us
    gather x1, local copies, waits for them, and re-layouts, per_device(): picked = jnp.take(emission, jnp.clip(local, 0, vocab_dev - 1), axis=0)  20.7 us
    dot_general x1, matrix products, per_device(): lax.dot_general(alpha_full, scaled, (((0,), (0,)), ((), ())), preferred_e...  9.47 us
    convert_element_type x1, other arithmetic, per_device(): jnp.where(inside[:, None], picked.astype(jnp.float32), 0.0)  8.33 us
  transfers between devices with their start and end apart: 2, of which 2 were waited for; matrix products, arithmetic and copies ran while one was open for 0% of the time, Pallas kernels for 0%

commit v1 on v0

v1 whole, which is shorter than its diff:
```python
import jax
import jax.numpy as jnp
import numpy as np
from jax import lax
from jax.experimental import pallas as pl
from jax.experimental.pallas import tpu as pltpu
from jax.sharding import Mesh, PartitionSpec as P

STATES = 32768
RANGE = 2000
F32, BF16 = jnp.float32, jnp.bfloat16
VM = pl.BlockSpec(memory_space=pltpu.VMEM)
SM = pl.BlockSpec(memory_space=pltpu.SMEM)


def iota(shape, dim):
    return lax.broadcasted_iota(jnp.int32, shape, dim)


def params(mib):
    return pltpu.CompilerParams(vmem_limit_bytes=mib << 20)


def pick_kernel(pos, ids, table, out, hot):
    @pl.when(pl.program_id(0) == 0)
    def _():
        local = ids[...] - pos[0] * RANGE
        mine = (local >= 0) & (local < RANGE)
        upto = (iota((128, 128), 0) <= iota((128, 128), 1)).astype(BF16)
        count = jnp.dot(mine.astype(F32).astype(BF16), upto, preferred_element_type=F32)
        value = jnp.where(mine, local, 0).astype(F32)
        count = jnp.where(mine, count, 0.0)
        wide = lambda a: jnp.broadcast_to(a[:, None, :], (16, 8, 128)).reshape(128, 128)
        order = ((iota((128, 128), 0) & 7) + 1).astype(F32)
        word = jnp.sum(jnp.where(wide(count) == order, wide(value), 0.0), axis=1, keepdims=True)
        hot[...] = (iota((128, RANGE), 1) == word.astype(jnp.int32)).astype(F32).astype(BF16)

    rows = jnp.dot(hot[...], table[...], preferred_element_type=F32)
    out[...] = rows.astype(BF16).reshape(4, 1, 32, 512)


def pick(pos, ids, emission):
    return pl.pallas_call(
        pick_kernel,
        grid=(4,),
        in_specs=[SM, pl.BlockSpec((16, 128), lambda j: (0, 0)), pl.BlockSpec((RANGE, 512), lambda j: (0, j))],
        out_specs=pl.BlockSpec((4, 1, 32, 512), lambda j: (0, j, 0, 0)),
        out_shape=jax.ShapeDtypeStruct((4, 4, 32, 512), BF16),
        scratch_shapes=[pltpu.VMEM((128, RANGE), BF16)],
        compiler_params=params(32),
        name="pick",
    )(pos, ids, emission)


def scale_kernel(pos, ids, rows, b0, b1, b2, b3, out, wide):
    wide[...] = rows[...].astype(F32)
    before = (iota((128, 128), 0) < iota((128, 128), 1)).astype(BF16)
    for d, beta in enumerate((b0, b1, b2, b3)):
        block = (pos[2] - d + 4) & 3
        word = ids[pl.ds(pos[1] * 4 + block, 1), :]
        wordb = jnp.broadcast_to(word, (16, 128))
        owner_at = iota((16, 128), 0)
        owns = (wordb >= owner_at * RANGE) & (wordb < (owner_at + 1) * RANGE)
        ownf = owns.astype(F32)
        earlier = jnp.dot(ownf.astype(BF16), before, preferred_element_type=F32)
        place = ownf * (earlier + (owner_at * 8).astype(F32))
        slot = jnp.sum(place, axis=0, keepdims=True).astype(jnp.int32)
        move = (iota((128, 128), 0) == slot).astype(F32).astype(BF16)
        given = wide[:, pl.ds(pl.multiple_of(block * 8, 8), 8), :].reshape(128, 512).astype(BF16)
        emitted = lax.dot_general(move, given, (((0,), (0,)), ((), ())), preferred_element_type=F32)
        out[block] = (emitted * beta[...].astype(F32)).astype(BF16)


def scale(pos, ids, rows, betas):
    return pl.pallas_call(
        scale_kernel,
        in_specs=[SM] + [VM] * 6,
        out_specs=VM,
        out_shape=jax.ShapeDtypeStruct((4, 128, 512), BF16),
        scratch_shapes=[pltpu.VMEM((16, 32, 512), F32)],
        compiler_params=params(32),
        name="scale",
    )(pos, ids, rows, *betas)


def turn_kernel(alpha, out):
    for x in range(4):
        out[0, x * 128 : (x + 1) * 128, :] = alpha[x].T


def turn(alpha):
    return pl.pallas_call(
        turn_kernel,
        grid=(4,),
        in_specs=[pl.BlockSpec((4, 512, 128), lambda g: (0, g, 0))],
        out_specs=pl.BlockSpec((1, 512, 512), lambda g: (g, 0, 0)),
        out_shape=jax.ShapeDtypeStruct((4, 512, 512), BF16),
        compiler_params=params(32),
        name="turn",
    )(alpha)


def expect_kernel(pos, alpha, s0, s1, s2, s3, out):
    step = 1 - 2 * pos[3]
    groups = (pos[1], (pos[1] - step + 4) & 3, (pos[1] + step + 4) & 3, (pos[1] + 2) & 3)
    total = jnp.zeros((512, 512), F32)
    for group, part in zip(groups, (s0, s1, s2, s3)):
        total += jnp.dot(alpha[group], part[...], preferred_element_type=F32)
    out[...] = total.astype(F32).reshape(4, 128, 512)


def expect(pos, alpha, parts):
    return pl.pallas_call(
        expect_kernel,
        in_specs=[SM] + [VM] * 5,
        out_specs=VM,
        out_shape=jax.ShapeDtypeStruct((4, 128, 512), F32),
        compiler_params=params(32),
        name="expect",
    )(pos, alpha, *parts)


def count_kernel(transition, expected, counts, total):
    sums = jnp.zeros((128, 128), F32)
    for x in range(4):
        part = transition[:, x * 512 : (x + 1) * 512].astype(F32) * expected[x].astype(F32)
        counts[:, x * 512 : (x + 1) * 512] = part
        for i in range(4):
            sums += part[:, i * 128 : (i + 1) * 128]
    total[...] = jnp.sum(sums.T, axis=0, keepdims=True)


def count(transition, expected):
    return pl.pallas_call(
        count_kernel,
        in_specs=[VM] * 2,
        out_specs=[VM] * 2,
        out_shape=[jax.ShapeDtypeStruct((128, 2048), F32), jax.ShapeDtypeStruct((1, 128), F32)],
        compiler_params=params(32),
        name="count",
    )(transition, expected)


def divide_kernel(counts, totals, out):
    total = jnp.sum(totals[...].reshape(16, 128), axis=0, keepdims=True)
    column = jnp.broadcast_to(total, (128, 128)).T[:, :1]
    out[...] = (STATES * counts[...] / column).astype(BF16)


def divide(counts, totals):
    return pl.pallas_call(
        divide_kernel,
        in_specs=[VM] * 2,
        out_specs=VM,
        out_shape=jax.ShapeDtypeStruct((128, 2048), BF16),
        compiler_params=params(32),
        name="divide",
    )(counts, totals)


def ring(step, size=4):
    return [(i, (i + step) % size) for i in range(size)]


def per_device(ids, alpha, beta, emission, transition):
    y, x, z, k = (lax.axis_index(a) for a in ("y", "x", "z", "k"))
    pos = jnp.stack([y * 4 + x, y, x, k]).astype(jnp.int32)
    ids = ids.reshape(16, 128)

    alpha_all = lax.all_to_all(jnp.broadcast_to(alpha[None], (16, 128, 128)), ("z", "k"), 0, 0).reshape(2048, 128)
    alpha_all = lax.all_to_all(jnp.broadcast_to(alpha_all[None], (4, 2048, 128)), "x", 0, 0)
    alpha_t = turn(alpha_all)

    betas = []
    for d in range(4):
        piece = lax.dynamic_slice(beta, (0, ((x + d) & 3) * 512), (128, 512))
        betas.append(piece if d == 0 else lax.ppermute(piece, "x", ring(d)))

    picked = pick(pos, ids, emission).reshape(16, 32, 512)
    rows = lax.all_to_all(picked, ("y", "x"), 0, 0)
    own = scale(pos, ids, rows, betas).reshape(512, 512)

    ahead = [(a * 2 + c, ((a + (1 - 2 * c)) % 4) * 2 + c) for a in range(4) for c in range(2)]
    behind = [(b, a) for a, b in ahead]
    one = lax.ppermute(own, ("y", "k"), ahead)
    two = lax.ppermute(own, ("y", "k"), behind)
    far = lax.ppermute(one, ("y", "k"), ahead)

    expected = expect(pos, alpha_t, (own, one, two, far))
    expected = lax.all_to_all(expected, "x", 0, 0)
    counts, total = count(transition, expected)
    totals = lax.all_to_all(jnp.broadcast_to(total[None], (16, 1, 128)), ("z", "k"), 0, 0)
    return counts, divide(counts, totals)


def solution(mesh):
    fine = Mesh(np.asarray(mesh.devices).reshape(4, 4, 8, 2), ("y", "x", "z", "k"))
    row, col = ("y", "x"), ("z", "k")
    in_specs = (P(), P(col, row), P(row, col), P(row, col), P(row, col))
    out_specs = (P(row, col), P(row, col))
    return jax.shard_map(per_device, mesh=fine, in_specs=in_specs, out_specs=out_specs, check_vma=False)
```

time: 315 us -> 148 us (0.47)
  waiting for transfers between devices: 210 us -> 48 us
  blocking collectives: 47.7 us -> 66.9 us
  local copies, waits for them, and re-layouts: 23.6 us -> 7 us
  between operations: 14.1 us -> 0.72 us
  starting transfers between devices: 0.08 us -> 13.3 us
  Pallas kernels: 0 us -> 10.4 us
  other arithmetic: 9.85 us -> 0.08 us
  matrix products: 9.47 us -> 0 us
    psum x1 -> x0, waiting for transfers between devices: 131 us -> none  [per_device(): lax.psum(jnp.where(inside[:, None], picked.astype(jnp.float32), 0.0).asty...]
    all_gather x1 -> x0, waiting for transfers between devices: 78.7 us -> none  [per_device(): beta_full = lax.all_gather(beta, 'row', axis=0, tiled=True)]
    all_to_all x0 -> x4, blocking collectives: none -> 66.9 us  [the longest x1 24.4 us: per_device(): lax.all_to_all(jnp.broadcast_to(alpha[None], (16, 128, 128)), ('z', 'k'),...]
    ppermute x0 -> x6, waiting for transfers between devices: none -> 47.9 us  [the longest x3 25.8 us: per_device(): betas.append(piece if d == 0 else lax.ppermute(piece, 'x', ring(d)))]
    psum x1 -> x0, blocking collectives: 26.2 us -> none  [per_device(): totals = lax.psum(jnp.sum(counts, axis=1), 'col')]
    all_gather x1 -> x0, blocking collectives: 21.4 us -> none  [per_device(): alpha_full = lax.all_gather(alpha, 'col', axis=0, tiled=True)]
    gather x1 -> x0, local copies, waits for them, and re-layouts: 20.7 us -> none  [per_device(): picked = jnp.take(emission, jnp.clip(local, 0, vocab_dev - 1), axis=0)]
    pallas_call x0 -> x6, Pallas kernels: none -> 10.4 us  [the longest x1 3.27 us: pick(): pl.pallas_call(pick_kernel, grid=(4,), in_specs=[SM, pl.BlockSpec((16, 12...]
  transfers between devices with their start and end apart: 2 -> 7, of which waited for: 2 -> 5; matrix products, arithmetic and copies ran while one was open for 0% -> 0% of each run, Pallas kernels for 0% -> 2%
where the time goes in v1:
time: 148 us; the launch traced here: 146 us
  blocking collectives  66.9 us (45%)
  waiting for transfers between devices  48 us (32%)
  starting transfers between devices  13.3 us (9%)
  Pallas kernels  10.4 us (7%)
  local copies, waits for them, and re-layouts  7 us (5%)
    ppermute x3, waiting for transfers between devices, per_device(): betas.append(piece if d == 0 else lax.ppermute(piece, 'x', ring(d)))  25.8 us
    all_to_all x1, blocking collectives, per_device(): lax.all_to_all(jnp.broadcast_to(alpha[None], (16, 128, 128)), ('z', 'k'),...  24.4 us
    all_to_all x1, blocking collectives, per_device(): rows = lax.all_to_all(picked, ('y', 'x'), 0, 0)  17.4 us
    all_to_all x1, blocking collectives, per_device(): expected = lax.all_to_all(expected, 'x', 0, 0)  14.9 us
    ppermute x1, waiting for transfers between devices, per_device(): one = lax.ppermute(own, ('y', 'k'), ahead)  12.6 us
    all_to_all x1, blocking collectives, per_device(): lax.all_to_all(jnp.broadcast_to(total[None], (16, 1, 128)), ('z', 'k'), 0...  10.1 us
    ppermute x1, waiting for transfers between devices, per_device(): far = lax.ppermute(one, ('y', 'k'), ahead)  9.53 us
    unnamed x14, local copies, waits for them, and re-layouts  5.27 us
  transfers between devices with their start and end apart: 7, of which 5 were waited for; matrix products, arithmetic and copies ran while one was open for 0% of the time, Pallas kernels for 2%

profile of v1, /device:TPU:2, one launch (start us, length us, event | category | flops | bytes accessed | tf_op | source)
XLA Modules:
  0.0 146.2 jit_solution(829896249988915677)
XLA Ops:
  0.6 0.1 pad_add_fusion.pos
  0.7 0.0 copy-start
  0.7 3.3 %copy-done = bf16[2000,2048]{1,0:T(8,128)(2,1)S(1)} copy-done((bf16[2000,2048]{1,0:T(8,128)(2,1)S(1)}, bf16[2000,2048]{1,0:T(8,128)(2,1)}, u32[]{:S(2)}) %copy-start) | copy-done | bytes 8192024
  4.0 0.0 copy-start.3
  4.0 0.7 copy-done.3
  4.7 0.0 copy-start.6
  4.7 3.3 %pick.1 = bf16[4,4,32,512]{3,2,1,0:T(8,128)(2,1)S(1)} custom-call(s32[4]{0:T(128)S(1)} %pad_add_fusion.pos, s32[16,128]{1,0:T(8,128)S(1)} %bitcast.13, bf16[2000,2048]{1,0:T(8,128)(2,1)S(1)} %copy-done), custom_call_target="tpu_custom_call" | custom-call | tf_op jit(solution)/shard_map/pick/pallas_call | solution.py:43
  8.0 17.4 %all_to_all.25.rows = bf16[16,32,512]{2,1,0:T(8,128)(2,1)S(1)} all-to-all(bf16[16,32,512]{2,1,0:T(8,128)(2,1)S(1)} %bitcast.9), channel_id=1, replica_groups=mesh['y'=4,'x'=4,'z'=8,'k'=2] {'y','x'}, dimensions={0} | all-to-all | bytes 1048576 | tf_op jit(solution)/shard_map/all_to_all | solution.py:180
  25.4 0.0 copy-done.6
  25.5 0.1 broadcast_in_dim.10
  25.6 24.4 %all_to_all.26 = bf16[16,128,128]{2,1,0:T(8,128)(2,1)S(1)} all-to-all(bf16[16,128,128]{2,1,0:T(8,128)(2,1)S(1)} %broadcast_in_dim.10), channel_id=1, replica_groups=mesh['y'=4,'x'=4,'z'=8,'k'=2] {'z','k'}, dimensions={0} | all-to-all | bytes 1048576 | tf_op jit(solution)/shard_map/all_to_all | solution.py:170
  50.0 1.6 %broadcast_in_dim.23 = bf16[4,2048,128]{2,1,0:T(8,128)(2,1)} broadcast(bf16[2048,128]{1,0:T(8,128)(2,1)S(1)} %bitcast.16), dimensions={1,2} | broadcast | bytes 2621440 | tf_op jit(solution)/shard_map/broadcast_in_dim | solution.py:171
  51.6 0.0 copy-start.5
  51.6 0.0 copy-start.4
  51.6 5.2 %all-to-all-start.1 = ((bf16[4,2048,128]{2,1,0:T(8,128)(2,1)}), bf16[4,2048,128]{2,1,0:T(8,128)(2,1)S(1)}, u32[]{:S(2)}, u32[]{:S(2)}) async-start(bf16[4,2048,128]{2,1,0:T(8,128)(2,1)} %broadcast_in_dim.23), calls=%async_computation.1 | async-start | bytes 4194304 | tf_op jit(solution)/shard_map/all_to_all | solution.py:171
  56.7 0.0 copy-done.5
  56.8 1.5 %collective-permute-start = (bf16[128,512]{1,0:T(8,128)(2,1)S(1)}, bf16[128,512]{1,0:T(8,128)(2,1)S(1)}, u32[]{:S(2)}, u32[]{:S(2)}) collective-permute-start(bf16[128,512]{1,0:T(8,128)(2,1)S(1)} %get-tuple-element.7), channel_id=1, source_target_pairs={{0,16},{16,32},{32,48},{48,0},{1,17},{17,33},{33,49},{49,1},{2,18}... | collective-permute-start | bytes 393224 | tf_op jit(solution)/shard_map/ppermute | solution.py:177
  58.3 0.7 collective-permute-start.1
  59.0 2.5 %collective-permute-start.2 = (bf16[128,512]{1,0:T(8,128)(2,1)S(1)}, bf16[128,512]{1,0:T(8,128)(2,1)S(1)}, u32[]{:S(2)}, u32[]{:S(2)}) collective-permute-start(bf16[128,512]{1,0:T(8,128)(2,1)S(1)} %get-tuple-element.6), channel_id=1, source_target_pairs={{0,48},{16,0},{32,16},{48,32},{1,49},{17,1},{33,17},{49,33},{2,50}... | collective-permute-start | bytes 393224 | tf_op jit(solution)/shard_map/ppermute | solution.py:177
  61.6 21.4 %collective-permute-done.b1 = bf16[128,512]{1,0:T(8,128)(2,1)S(1)} collective-permute-done((bf16[128,512]{1,0:T(8,128)(2,1)S(1)}, bf16[128,512]{1,0:T(8,128)(2,1)S(1)}, u32[]{:S(2)}, u32[]{:S(2)}) %collective-permute-start) | collective-permute-done | bytes 131104 | tf_op jit(solution)/shard_map/ppermute | solution.py:177
  82.9 2.3 %collective-permute-done.1.b2 = bf16[128,512]{1,0:T(8,128)(2,1)S(1)} collective-permute-done((bf16[128,512]{1,0:T(8,128)(2,1)S(1)}, bf16[128,512]{1,0:T(8,128)(2,1)S(1)}, u32[]{:S(2)}, u32[]{:S(2)}) %collective-permute-start.1) | collective-permute-done | bytes 131104 | tf_op jit(solution)/shard_map/ppermute | solution.py:177
  85.2 2.1 %collective-permute-done.2.b3 = bf16[128,512]{1,0:T(8,128)(2,1)S(1)} collective-permute-done((bf16[128,512]{1,0:T(8,128)(2,1)S(1)}, bf16[128,512]{1,0:T(8,128)(2,1)S(1)}, u32[]{:S(2)}, u32[]{:S(2)}) %collective-permute-start.2) | collective-permute-done | bytes 131104 | tf_op jit(solution)/shard_map/ppermute | solution.py:177
  87.3 0.0 copy-done.4
  87.3 1.6 %scale.1 = bf16[4,128,512]{2,1,0:T(8,128)(2,1)S(1)} custom-call(s32[4]{0:T(128)S(1)} %pad_add_fusion.pos, s32[16,128]{1,0:T(8,128)S(1)} %bitcast.14, bf16[16,32,512]{2,1,0:T(8,128)(2,1)S(1)} %all_to_all.25.rows, bf16[128,512]{1,0:T(8,128)(2,1)S(1)} %get-tuple-element.8.b0, bf16[128,512]{1,0:T(8,128)(2,1)S(1)} %collective-permute-done.b1, ...), custom_call_target="tpu_custom_call" | custom-call | tf_op jit(solution)/shard_map/scale/pallas_call | solution.py:75
  88.9 0.1 collective-permute-start.3
  89.0 3.2 %collective-permute-start.4 = (bf16[512,512]{1,0:T(8,128)(2,1)S(1)}, bf16[512,512]{1,0:T(8,128)(2,1)}, u32[]{:S(2)}, u32[]{:S(2)}) collective-permute-start(bf16[512,512]{1,0:T(8,128)(2,1)S(1)} %bitcast.11), channel_id=1, source_target_pairs={{64,0},{193,1},{128,64},{1,65},{192,128},{65,129},{0,192},{129,193... | collective-permute-start | bytes 1572872 | tf_op jit(solution)/shard_map/ppermute | solution.py:186
  92.2 12.6 %collective-permute-done.3.s1 = bf16[512,512]{1,0:T(8,128)(2,1)S(1)} collective-permute-done((bf16[512,512]{1,0:T(8,128)(2,1)S(1)}, bf16[512,512]{1,0:T(8,128)(2,1)S(1)}, u32[]{:S(2)}, u32[]{:S(2)}) %collective-permute-start.3) | collective-permute-done | bytes 524320 | tf_op jit(solution)/shard_map/ppermute | solution.py:185
  104.9 0.0 collective-permute-start.5
  104.9 0.0 all-to-all-done.1.alpha
  104.9 0.9 turn.1.alpha
  105.8 0.0 collective-permute-done.4.s2
  105.8 9.5 %collective-permute-done.5.s3 = bf16[512,512]{1,0:T(8,128)(2,1)} collective-permute-done((bf16[512,512]{1,0:T(8,128)(2,1)S(1)}, bf16[512,512]{1,0:T(8,128)(2,1)}, u32[]{:S(2)}, u32[]{:S(2)}) %collective-permute-start.5) | collective-permute-done | bytes 524320 | tf_op jit(solution)/shard_map/ppermute | solution.py:187
  115.4 2.5 %expect.1 = f32[4,128,512]{2,1,0:T(8,128)S(1)} custom-call(s32[4]{0:T(128)S(1)} %pad_add_fusion.pos, bf16[4,512,512]{2,1,0:T(8,128)(2,1)S(1)} %turn.1.alpha, bf16[512,512]{1,0:T(8,128)(2,1)S(1)} %bitcast.12, bf16[512,512]{1,0:T(8,128)(2,1)S(1)} %collective-permute-done.3.s1, bf16[512,512]{1,0:T(8,128)(2,1)} %collective-permute-done.4.s2, ...), custom_call_target="tpu_custom_call" | custom-call | tf_op jit(solution)/shard_map/expect/pallas_call | solution.py:113
  117.8 0.0 copy-start.2
  117.8 14.9 %all_to_all.27.expected = f32[4,128,512]{2,1,0:T(8,128)S(1)} all-to-all(f32[4,128,512]{2,1,0:T(8,128)S(1)} %expect.1), channel_id=1, replica_groups=mesh['y'=4,'x'=4,'z'=8,'k'=2] {'x'}, dimensions={0} | all-to-all | bytes 2097152 | tf_op jit(solution)/shard_map/all_to_all | solution.py:190
  132.8 0.0 copy-done.2
  132.8 1.1 count.1
  133.8 10.1 %all_to_all.28.totals = f32[16,1,128]{2,1,0:T(1,128)S(1)} all-to-all(f32[16,1,128]{2,1,0:T(1,128)S(1)} %broadcast_in_dim.25), channel_id=1, replica_groups=mesh['y'=4,'x'=4,'z'=8,'k'=2] {'z','k'}, dimensions={0} | all-to-all | bytes 16384 | tf_op jit(solution)/shard_map/all_to_all | solution.py:192
  143.9 0.0 copy-start.1
  143.9 1.2 copy-done.1
  145.2 1.0 divide.1
  (2 shorter events, 0.0 us)
Async XLA Ops:
  0.7 3.3 %copy-start = (bf16[2000,2048]{1,0:T(8,128)(2,1)S(1)}, bf16[2000,2048]{1,0:T(8,128)(2,1)}, u32[]{:S(2)}) copy-start(bf16[2000,2048]{1,0:T(8,128)(2,1)} %table.1) | copy-start | bytes 24576004
  4.0 0.7 copy-start.3
  4.7 20.7 %copy-start.6 = (bf16[128,128]{1,0:T(8,128)(2,1)S(1)}, bf16[128,128]{1,0:T(8,128)(2,1)}, u32[]{:S(2)}) copy-start(bf16[128,128]{1,0:T(8,128)(2,1)} %param.6) | copy-start | bytes 98308
  51.6 5.2 %copy-start.5 = (bf16[128,2048]{1,0:T(8,128)(2,1)S(1)}, bf16[128,2048]{1,0:T(8,128)(2,1)}, u32[]{:S(2)}) copy-start(bf16[128,2048]{1,0:T(8,128)(2,1)} %param.7) | copy-start | bytes 1572868
  51.6 35.8 %copy-start.4 = (s32[2048]{0:T(1024)S(1)}, s32[2048]{0:T(1024)}, u32[]{:S(2)}) copy-start(s32[2048]{0:T(1024)} %param.5) | copy-start | bytes 24580
  51.6 53.3 %all-to-all-start.1 = ((bf16[4,2048,128]{2,1,0:T(8,128)(2,1)}), bf16[4,2048,128]{2,1,0:T(8,128)(2,1)S(1)}, u32[]{:S(2)}, u32[]{:S(2)}) async-start(bf16[4,2048,128]{2,1,0:T(8,128)(2,1)} %broadcast_in_dim.23), calls=%async_computation.1 | async-start | bytes 4194304 | tf_op jit(solution)/shard_map/all_to_all | solution.py:171
  56.8 26.1 %collective-permute-start = (bf16[128,512]{1,0:T(8,128)(2,1)S(1)}, bf16[128,512]{1,0:T(8,128)(2,1)S(1)}, u32[]{:S(2)}, u32[]{:S(2)}) collective-permute-start(bf16[128,512]{1,0:T(8,128)(2,1)S(1)} %get-tuple-element.7), channel_id=1, source_target_pairs={{0,16},{16,32},{32,48},{48,0},{1,17},{17,33},{33,49},{49,1},{2,18}... | collective-permute-start | bytes 393224 | tf_op jit(solution)/shard_map/ppermute | solution.py:177
  58.3 26.9 %collective-permute-start.1 = (bf16[128,512]{1,0:T(8,128)(2,1)S(1)}, bf16[128,512]{1,0:T(8,128)(2,1)S(1)}, u32[]{:S(2)}, u32[]{:S(2)}) collective-permute-start(bf16[128,512]{1,0:T(8,128)(2,1)S(1)} %get-tuple-element.9), channel_id=1, source_target_pairs={{0,32},{16,48},{32,0},{48,16},{1,33},{17,49},{33,1},{49,17},{2,34}... | collective-permute-start | bytes 393224 | tf_op jit(solution)/shard_map/ppermute | solution.py:177
  59.0 28.3 %collective-permute-start.2 = (bf16[128,512]{1,0:T(8,128)(2,1)S(1)}, bf16[128,512]{1,0:T(8,128)(2,1)S(1)}, u32[]{:S(2)}, u32[]{:S(2)}) collective-permute-start(bf16[128,512]{1,0:T(8,128)(2,1)S(1)} %get-tuple-element.6), channel_id=1, source_target_pairs={{0,48},{16,0},{32,16},{48,32},{1,49},{17,1},{33,17},{49,33},{2,50}... | collective-permute-start | bytes 393224 | tf_op jit(solution)/shard_map/ppermute | solution.py:177
  88.9 16.0 %collective-permute-start.3 = (bf16[512,512]{1,0:T(8,128)(2,1)S(1)}, bf16[512,512]{1,0:T(8,128)(2,1)S(1)}, u32[]{:S(2)}, u32[]{:S(2)}) collective-permute-start(bf16[512,512]{1,0:T(8,128)(2,1)S(1)} %bitcast.10), channel_id=1, source_target_pairs={{0,64},{1,193},{64,128},{65,1},{128,192},{129,65},{192,0},{193,129... | collective-permute-start | bytes 1572872 | tf_op jit(solution)/shard_map/ppermute | solution.py:185
  89.0 16.8 %collective-permute-start.4 = (bf16[512,512]{1,0:T(8,128)(2,1)S(1)}, bf16[512,512]{1,0:T(8,128)(2,1)}, u32[]{:S(2)}, u32[]{:S(2)}) collective-permute-start(bf16[512,512]{1,0:T(8,128)(2,1)S(1)} %bitcast.11), channel_id=1, source_target_pairs={{64,0},{193,1},{128,64},{1,65},{192,128},{65,129},{0,192},{129,193... | collective-permute-start | bytes 1572872 | tf_op jit(solution)/shard_map/ppermute | solution.py:186
  104.9 10.5 %collective-permute-start.5 = (bf16[512,512]{1,0:T(8,128)(2,1)S(1)}, bf16[512,512]{1,0:T(8,128)(2,1)}, u32[]{:S(2)}, u32[]{:S(2)}) collective-permute-start(bf16[512,512]{1,0:T(8,128)(2,1)S(1)} %collective-permute-done.3.s1), channel_id=1, source_target_pairs={{0,64},{1,193},{64,128},{65,1},{128,192},{129,65},{192,0},{193,129... | collective-permute-start | bytes 1572872 | tf_op jit(solution)/shard_map/ppermute | solution.py:187
  117.8 14.9 %copy-start.2 = (bf16[128,2048]{1,0:T(8,128)(2,1)S(1)}, bf16[128,2048]{1,0:T(8,128)(2,1)}, u32[]{:S(2)}) copy-start(bf16[128,2048]{1,0:T(8,128)(2,1)} %transition.1) | copy-start | bytes 1572868
  143.9 1.2 copy-start.1

commit v2 on v1

v2 whole, which is shorter than its diff:
```python
import jax
import jax.numpy as jnp
import numpy as np
from jax import lax
from jax.experimental import pallas as pl
from jax.experimental.pallas import tpu as pltpu
from jax.sharding import Mesh, PartitionSpec as P

STATES = 32768
RANGE = 2000
F32, BF16 = jnp.float32, jnp.bfloat16
VM = pl.BlockSpec(memory_space=pltpu.VMEM)
SM = pl.BlockSpec(memory_space=pltpu.SMEM)


SMALL = pl.CostEstimate(flops=1, bytes_accessed=1, transcendentals=0)


def iota(shape, dim):
    return lax.broadcasted_iota(jnp.int32, shape, dim)


def params(mib):
    return pltpu.CompilerParams(vmem_limit_bytes=mib << 20)


def cut_kernel(pos, a, o0, o1, o2, o3):
    for d, o in enumerate((o0, o1, o2, o3)):
        o[...] = a[:, pl.ds(pl.multiple_of(((pos[2] + d) & 3) * 512, 512), 512)]


def cut(pos, a):
    return pl.pallas_call(
        cut_kernel,
        in_specs=[SM, VM],
        out_specs=[VM] * 4,
        out_shape=[jax.ShapeDtypeStruct((128, 512), BF16)] * 4,
        compiler_params=params(8),
        cost_estimate=SMALL,
        name="cut",
    )(pos, a)


def pick_kernel(pos, ids, table, out, slab, sems):
    parts = ((0, 512), (512, 512), (1024, 512), (1536, 464))
    copies = [
        pltpu.make_async_copy(table.at[pl.ds(start, size)], slab.at[pl.ds(start, size)], sems.at[n])
        for n, (start, size) in enumerate(parts)
    ]
    for copy in copies:
        copy.start()
    local = ids[...] - pos[0] * RANGE
    mine = (local >= 0) & (local < RANGE)
    upto = (iota((128, 128), 0) <= iota((128, 128), 1)).astype(BF16)
    count = jnp.dot(mine.astype(F32).astype(BF16), upto, preferred_element_type=F32)
    value = jnp.where(mine, local, 0).astype(F32)
    count = jnp.where(mine, count, 0.0)
    wide = lambda a: jnp.broadcast_to(a[:, None, :], (16, 8, 128)).reshape(128, 128)
    order = ((iota((128, 128), 0) & 7) + 1).astype(F32)
    word = jnp.sum(jnp.where(wide(count) == order, wide(value), 0.0), axis=1, keepdims=True).astype(jnp.int32)
    rows = jnp.zeros((128, 2048), F32)
    for copy, (start, size) in zip(copies, parts):
        hot = (iota((128, size), 1) + start == word).astype(F32).astype(BF16)
        copy.wait()
        rows += jnp.dot(hot, slab[start : start + size, :], preferred_element_type=F32)
    for x in range(4):
        out[:, x] = rows[:, x * 512 : (x + 1) * 512].astype(BF16).reshape(4, 32, 512)


def pick(pos, ids, emission):
    return pl.pallas_call(
        pick_kernel,
        in_specs=[SM, VM, pl.BlockSpec(memory_space=pl.ANY)],
        out_specs=VM,
        out_shape=jax.ShapeDtypeStruct((4, 4, 32, 512), BF16),
        scratch_shapes=[pltpu.VMEM((RANGE, 2048), BF16), pltpu.SemaphoreType.DMA((4,))],
        compiler_params=params(58),
        cost_estimate=SMALL,
        name="pick",
    )(pos, ids, emission)


def scale_kernel(pos, ids, rows, c0, c1, c2, c3, out, wide):
    wide[...] = rows[...].astype(F32)
    before = (iota((128, 128), 0) < iota((128, 128), 1)).astype(BF16)
    for d, c in enumerate((c0, c1, c2, c3)):
        block = (pos[2] - d + 4) & 3
        word = ids[pl.ds(pos[1] * 4 + block, 1), :]
        wordb = jnp.broadcast_to(word, (16, 128))
        owner_at = iota((16, 128), 0)
        owns = (wordb >= owner_at * RANGE) & (wordb < (owner_at + 1) * RANGE)
        ownf = owns.astype(F32)
        earlier = jnp.dot(ownf.astype(BF16), before, preferred_element_type=F32)
        place = ownf * (earlier + (owner_at * 8).astype(F32))
        slot = jnp.sum(place, axis=0, keepdims=True).astype(jnp.int32)
        move = (iota((128, 128), 0) == slot).astype(F32).astype(BF16)
        given = wide[:, pl.ds(pl.multiple_of(block * 8, 8), 8), :].reshape(128, 512).astype(BF16)
        emitted = lax.dot_general(move, given, (((0,), (0,)), ((), ())), preferred_element_type=F32)
        out[block] = (emitted * c[...].astype(F32)).astype(BF16)


def scale(pos, ids, rows, cuts):
    return pl.pallas_call(
        scale_kernel,
        in_specs=[SM] + [VM] * 6,
        out_specs=VM,
        out_shape=jax.ShapeDtypeStruct((4, 128, 512), BF16),
        scratch_shapes=[pltpu.VMEM((16, 32, 512), F32)],
        compiler_params=params(16),
        cost_estimate=SMALL,
        name="scale",
    )(pos, ids, rows, *cuts)


def quarter(pos, transition, away):
    return transition[:, pl.ds(pl.multiple_of(((pos[2] + away + 4) & 3) * 512, 512), 512)]


def pack_kernel(pos, l0, l1, l2, l3, transition, ahead, behind):
    step = 1 - 2 * pos[3]
    near, far, back = (quarter(pos, transition, away) for away in (step, 2, -step))
    for n in range(4):
        lanes = slice(n * 128, (n + 1) * 128)
        ahead[n] = near[:, lanes]
        ahead[12 + n] = far[:, lanes]
        behind[n] = back[:, lanes]
    m = 0
    for part in (l0, l1, l2, l3):
        for n in range(part.shape[0]):
            ahead[4 + m] = part[n]
            behind[4 + m] = part[n]
            m += 1


def pack(pos, line, transition):
    return pl.pallas_call(
        pack_kernel,
        in_specs=[SM] + [VM] * 5,
        out_specs=[VM] * 2,
        out_shape=[jax.ShapeDtypeStruct((16, 128, 128), BF16), jax.ShapeDtypeStruct((12, 128, 128), BF16)],
        compiler_params=params(8),
        cost_estimate=SMALL,
        name="pack",
    )(pos, *line, transition)


def turn_kernel(pos, *refs):
    out = refs[8]
    for c in range(2):
        core = pos[3] ^ c
        step = 1 - 2 * core
        for n, (away, first) in enumerate(((0, 4), (-step, 4), (step, 4), (2, 0))):
            x = (pos[2] + away + 4) & 3
            for m, flip in enumerate((0, 1, 2, 3, 7, 6, 5, 4)):
                block = (pos[4] ^ flip) * 2 + core
                rows = pl.ds(pl.multiple_of(x * 128, 128), 128)
                times = pl.ds(pl.multiple_of((block & 3) * 128, 128), 128)
                out[block >> 2, rows, times] = refs[c * 4 + n][first + m].T


def turn(pos, parts):
    return pl.pallas_call(
        turn_kernel,
        in_specs=[SM] + [VM] * 8,
        out_specs=VM,
        out_shape=jax.ShapeDtypeStruct((4, 512, 512), BF16),
        compiler_params=params(16),
        cost_estimate=SMALL,
        name="turn",
    )(pos, *parts)


def expect_kernel(pos, alpha, s0, s1, s2, s3, transition, t1, t2, t3, total, sums):
    step = 1 - 2 * pos[3]
    groups = (pos[1], (pos[1] - step + 4) & 3, (pos[1] + step + 4) & 3, (pos[1] + 2) & 3)
    acc = jnp.zeros((512, 512), F32)
    for group, part in zip(groups, (s0, s1, s2, s3)):
        acc += jnp.dot(alpha[group], part[...], preferred_element_type=F32)
    total[...] = acc.reshape(4, 128, 512)
    for t, first, away in ((None, 0, 0), (t1, 0, -step), (t2, 0, step), (t3, 8, 2)):
        block = (pos[2] + away + 4) & 3
        lanes = jnp.zeros((128, 128), F32)
        if t is None:
            mine = quarter(pos, transition, 0)
        for n in range(4):
            part = slice(n * 128, (n + 1) * 128)
            weight = mine[:, part] if t is None else t[first + n]
            lanes += weight.astype(F32) * total[block, :, part]
        line = jnp.sum(lanes.T, axis=0, keepdims=True)
        sums[pl.ds(block * 16, 16)] = jnp.broadcast_to(line[None], (16, 1, 128))


def expect(pos, alpha, parts, transition, quarters):
    return pl.pallas_call(
        expect_kernel,
        in_specs=[SM] + [VM] * 9,
        out_specs=[VM] * 2,
        out_shape=[jax.ShapeDtypeStruct((4, 128, 512), F32), jax.ShapeDtypeStruct((64, 1, 128), F32)],
        compiler_params=params(24),
        cost_estimate=SMALL,
        name="expect",
    )(pos, alpha, *parts, transition, *quarters)


def code_kernel(pos, total, *outs):
    for d, out in enumerate(outs, 1):
        power = total[(pos[2] + d) & 3]
        power = power * power
        power = power * power
        out[...] = (power * power).astype(BF16)


def code(pos, total):
    return pl.pallas_call(
        code_kernel,
        in_specs=[SM, VM],
        out_specs=[VM] * 3,
        out_shape=[jax.ShapeDtypeStruct((128, 512), BF16)] * 3,
        compiler_params=params(8),
        cost_estimate=pl.CostEstimate(flops=10**9, bytes_accessed=10**7, transcendentals=0),
        name="code",
    )(pos, total)


def column_kernel(sums, out):
    whole = jnp.sum(sums[...].reshape(64, 128), axis=0, keepdims=True)
    out[...] = STATES / jnp.broadcast_to(whole, (128, 128)).T


def column(sums):
    return pl.pallas_call(
        column_kernel,
        in_specs=[VM],
        out_specs=VM,
        out_shape=jax.ShapeDtypeStruct((128, 128), F32),
        compiler_params=params(8),
        cost_estimate=pl.CostEstimate(flops=int(2 * 10**9), bytes_accessed=10**6, transcendentals=0),
        name="column",
    )(sums)


def finish_kernel(pos, transition, total, e1, e2, e3, rate, counts, out):
    for d, e in enumerate((None, e1, e2, e3)):
        part = pl.ds(pl.multiple_of(((pos[2] - d + 4) & 3) * 512, 512), 512)
        if d:
            expected = jnp.sqrt(jnp.sqrt(jnp.sqrt(e[...].astype(F32))))
        else:
            expected = total[pos[2]]
        count = transition[:, part].astype(F32) * expected
        counts[:, part] = count
        out[:, part] = (count * jnp.concatenate([rate[...]] * 4, axis=1)).astype(BF16)


def finish(pos, transition, total, parts, rate):
    return pl.pallas_call(
        finish_kernel,
        in_specs=[SM] + [VM] * 6,
        out_specs=[VM] * 2,
        out_shape=[jax.ShapeDtypeStruct((128, 2048), F32), jax.ShapeDtypeStruct((128, 2048), BF16)],
        compiler_params=params(16),
        cost_estimate=SMALL,
        name="finish",
    )(pos, transition, total, *parts, rate)


def ring(step, size=4):
    return [(i, (i + step) % size) for i in range(size)]


def per_device(ids, alpha, beta, emission, transition):
    y, x, z, k = (lax.axis_index(a) for a in ("y", "x", "z", "k"))
    pos = jnp.stack([y * 4 + x, y, x, k, z]).astype(jnp.int32)
    ids = ids.reshape(16, 128)
    ahead = [(a * 2 + c, ((a + 1 - 2 * c) % 4) * 2 + c) for a in range(4) for c in range(2)]
    behind = [(b, a) for a, b in ahead]
    swap = [(0, 1), (1, 0)]

    together = lax.optimization_barrier
    flip = lambda a, by: lax.ppermute(a, "z", [(i, i ^ by) for i in range(8)])

    line = [alpha[None], flip(alpha[None], 1)]
    betas = [c if d == 0 else lax.ppermute(c, "x", ring(d)) for d, c in enumerate(cut(pos, beta))]
    picked = pick(pos, ids, emission)
    picked, line, betas = together((picked, line, betas))

    rows = lax.all_to_all(picked.reshape(16, 32, 512), ("y", "x"), 0, 0)
    line.append(flip(jnp.concatenate(line), 2))
    line.append(flip(jnp.concatenate(line), 7))
    rows, line = together((rows, line))
    own = scale(pos, ids, rows, betas).reshape(512, 512)

    own, line = together((own, line))
    one = lax.ppermute(own, ("y", "k"), ahead)
    two = lax.ppermute(own, ("y", "k"), behind)
    to_a, to_b = pack(pos, line, transition)
    one_a = lax.ppermute(to_a, ("x", "k"), ahead)
    two_a = lax.ppermute(to_b, ("x", "k"), behind)

    one, two, one_a, two_a, to_b = together((one, two, one_a, two_a, to_b))
    far = lax.ppermute(one, ("y", "k"), ahead)
    far_a = lax.ppermute(one_a[4:], ("x", "k"), ahead)
    sources = [to_b, one_a, two_a, far_a]
    sources += [lax.ppermute(a, "k", swap) for a in sources]
    alpha_t = turn(pos, sources)

    total, sums = expect(pos, alpha_t, (own, one, two, far), transition, (one_a, two_a, far_a))
    sums = lax.all_to_all(sums, ("x", "z", "k"), 0, 0)
    parts = [lax.ppermute(e, "x", ring(d)) for d, e in enumerate(code(pos, total), 1)]
    return finish(pos, transition, total, parts, column(sums))


def solution(mesh):
    fine = Mesh(np.asarray(mesh.devices).reshape(4, 4, 8, 2), ("y", "x", "z", "k"))
    row, col = ("y", "x"), ("z", "k")
    in_specs = (P(), P(col, row), P(row, col), P(row, col), P(row, col))
    out_specs = (P(row, col), P(row, col))
    return jax.shard_map(per_device, mesh=fine, in_specs=in_specs, out_specs=out_specs, check_vma=False)
```

time: 148 us -> 92.7 us (0.63)
  blocking collectives: 66.9 us -> 0 us
  starting transfers between devices: 13.3 us -> 44.7 us
  waiting for transfers between devices: 48 us -> 29.2 us
  local copies, waits for them, and re-layouts: 7 us -> 1.88 us
  Pallas kernels: 10.4 us -> 15.1 us
    all_to_all x4 -> x0, blocking collectives: 66.9 us -> none  [the longest x1 24.4 us: per_device(): lax.all_to_all(jnp.broadcast_to(alpha[None], (16, 128, 128)), ('z', 'k'),...]
    ppermute x3 -> x16, starting transfers between devices: 4.78 us -> 25.5 us  [the longest x3 10.9 us: per_device(): flip = lambda a, by: lax.ppermute(a, 'z', [(i, i ^ by) for i in range(8)])]
    ppermute x1, waiting for transfers between devices: 12.6 us -> 1.49 us  [per_device(): one = lax.ppermute(own, ('y', 'k'), ahead)]
    all_to_all x1 -> x2, starting transfers between devices: 5.17 us -> 16 us  [the longest x1 9.99 us: per_device(): sums = lax.all_to_all(sums, ('x', 'z', 'k'), 0, 0)]
    ppermute x1, waiting for transfers between devices: 9.53 us -> 0.6 us  [per_device(): far = lax.ppermute(one, ('y', 'k'), ahead)]
    pallas_call x5 -> x8, Pallas kernels: 8.78 us -> 13.5 us  [the longest x1 5.38 us: pick(): pl.pallas_call(pick_kernel, in_specs=[SM, VM, pl.BlockSpec(memory_space=p...]
    unnamed x14, local copies, waits for them, and re-layouts: 5.27 us -> 1.77 us
    all_to_all x1 -> x2, waiting for transfers between devices: 0.01 us -> 2.9 us  [the longest x1 2.9 us: per_device(): sums = lax.all_to_all(sums, ('x', 'z', 'k'), 0, 0)]
  transfers between devices with their start and end apart: 7 -> 21, of which waited for: 5 -> 11; matrix products, arithmetic and copies ran while one was open for 0% -> 0% of each run, Pallas kernels for 2% -> 8%
where the time goes in v2:
time: 92.7 us; the launch traced here: 91.7 us
  starting transfers between devices  44.7 us (48%)
  waiting for transfers between devices  29.2 us (31%)
  Pallas kernels  15.1 us (16%)
  local copies, waits for them, and re-layouts  1.88 us (2%)
    ppermute x3, starting transfers between devices, per_device(): flip = lambda a, by: lax.ppermute(a, 'z', [(i, i ^ by) for i in range(8)])  10.9 us
    all_to_all x1, starting transfers between devices, per_device(): sums = lax.all_to_all(sums, ('x', 'z', 'k'), 0, 0)  9.99 us
    ppermute x1, waiting for transfers between devices, per_device(): two_a = lax.ppermute(to_b, ('x', 'k'), behind)  7.21 us
    ppermute x3, waiting for transfers between devices, per_device(): flip = lambda a, by: lax.ppermute(a, 'z', [(i, i ^ by) for i in range(8)])  6.36 us
    ppermute x1, waiting for transfers between devices, per_device(): far_a = lax.ppermute(one_a[4:], ('x', 'k'), ahead)  6.07 us
    all_to_all x1, starting transfers between devices, per_device(): rows = lax.all_to_all(picked.reshape(16, 32, 512), ('y', 'x'), 0, 0)  5.96 us
    pallas_call x1, Pallas kernels, pick(): pl.pallas_call(pick_kernel, in_specs=[SM, VM, pl.BlockSpec(memory_space=p...  5.38 us
    ppermute x3, starting transfers between devices, per_device(): lax.ppermute(e, 'x', ring(d))  4.98 us
  transfers between devices with their start and end apart: 21, of which 11 were waited for; matrix products, arithmetic and copies ran while one was open for 0% of the time, Pallas kernels for 8%

profile of v2, /device:TPU:2, one launch (start us, length us, event | category | flops | bytes accessed | tf_op | source)
XLA Modules:
  0.0 91.7 jit_solution(15527991108741069410)
XLA Ops:
  0.6 0.1 stack.23.pos
  0.7 1.1 %copy-done.1 = bf16[128,2048]{1,0:T(8,128)(2,1)S(1)} copy-done((bf16[128,2048]{1,0:T(8,128)(2,1)S(1)}, bf16[128,2048]{1,0:T(8,128)(2,1)}, u32[]{:S(2)}) %copy-start.1) | copy-done | bytes 524312
  1.8 0.6 cut.1
  2.4 1.6 %collective-permute-start.1 = (bf16[128,512]{1,0:T(8,128)(2,1)S(1)}, bf16[128,512]{1,0:T(8,128)(2,1)S(1)}, u32[]{:S(2)}, u32[]{:S(2)}) collective-permute-start(bf16[128,512]{1,0:T(8,128)(2,1)S(1)} %get-tuple-element.36), channel_id=1, source_target_pairs={{0,16},{16,32},{32,48},{48,0},{1,17},{17,33},{33,49},{49,1},{2,18}... | collective-permute-start | bytes 393224 | tf_op jit(solution)/shard_map/ppermute | solution.py:282
  4.0 2.8 %collective-permute-start.2 = (bf16[128,512]{1,0:T(8,128)(2,1)S(1)}, bf16[128,512]{1,0:T(8,128)(2,1)S(1)}, u32[]{:S(2)}, u32[]{:S(2)}) collective-permute-start(bf16[128,512]{1,0:T(8,128)(2,1)S(1)} %get-tuple-element.37), channel_id=1, source_target_pairs={{0,32},{16,48},{32,0},{48,16},{1,33},{17,49},{33,1},{49,17},{2,34}... | collective-permute-start | bytes 393224 | tf_op jit(solution)/shard_map/ppermute | solution.py:282
  6.8 0.4 collective-permute-start.3
  7.3 1.9 %collective-permute-start = (bf16[1,128,128]{2,1,0:T(8,128)(2,1)}, bf16[1,128,128]{2,1,0:T(8,128)(2,1)S(1)}, u32[]{:S(2)}, u32[]{:S(2)}) collective-permute-start(bf16[1,128,128]{2,1,0:T(8,128)(2,1)} %bitcast.12), channel_id=1, source_target_pairs={{0,2},{2,0},{4,6},{6,4},{8,10},{10,8},{12,14},{14,12},{1,3},{3,1},... | collective-permute-start | bytes 98312 | tf_op jit(solution)/shard_map/ppermute | solution.py:279
  9.2 5.4 %pick.1 = bf16[4,4,32,512]{3,2,1,0:T(8,128)(2,1)} custom-call(s32[5]{0:T(128)} %copy-done.4, s32[16,128]{1,0:T(8,128)} %bitcast.16, bf16[2000,2048]{1,0:T(8,128)(2,1)} %table.1), custom_call_target="tpu_custom_call" | custom-call | flops 1 | bytes 1 | tf_op jit(solution)/shard_map/pick/pallas_call | solution.py:71
  14.6 0.0 copy-start.6
  14.6 0.0 collective-permute-done.1.c1
  14.6 0.0 collective-permute-done.2.c2
  14.6 6.0 %all-to-all-start = ((bf16[16,32,512]{2,1,0:T(8,128)(2,1)}), bf16[16,32,512]{2,1,0:T(8,128)(2,1)S(1)}, u32[]{:S(2)}, u32[]{:S(2)}) async-start(bf16[16,32,512]{2,1,0:T(8,128)(2,1)} %bitcast.18), calls=%async_computation | async-start | bytes 1048576 | tf_op jit(solution)/shard_map/all_to_all | solution.py:286
  20.6 3.4 %collective-permute-start.4 = (bf16[2,128,128]{2,1,0:T(8,128)(2,1)S(1)}, bf16[2,128,128]{2,1,0:T(8,128)(2,1)S(1)}, u32[]{:S(2)}, u32[]{:S(2)}) collective-permute-start(bf16[2,128,128]{2,1,0:T(8,128)(2,1)S(1)} %pad_maximum_fusion.1), channel_id=1, source_target_pairs={{0,4},{2,6},{4,0},{6,2},{8,12},{10,14},{12,8},{14,10},{1,5},{3,7},... | collective-permute-start | bytes 196616 | tf_op jit(solution)/shard_map/ppermute | solution.py:279
  24.0 2.3 %collective-permute-done.4.l2 = bf16[2,128,128]{2,1,0:T(8,128)(2,1)S(1)} collective-permute-done((bf16[2,128,128]{2,1,0:T(8,128)(2,1)S(1)}, bf16[2,128,128]{2,1,0:T(8,128)(2,1)S(1)}, u32[]{:S(2)}, u32[]{:S(2)}) %collective-permute-start.4) | collective-permute-done | bytes 65568 | tf_op jit(solution)/shard_map/ppermute | solution.py:279
  26.2 5.7 %collective-permute-start.5 = (bf16[4,128,128]{2,1,0:T(8,128)(2,1)S(1)}, bf16[4,128,128]{2,1,0:T(8,128)(2,1)S(1)}, u32[]{:S(2)}, u32[]{:S(2)}) collective-permute-start(bf16[4,128,128]{2,1,0:T(8,128)(2,1)S(1)} %pad_maximum_fusion), channel_id=1, source_target_pairs={{0,14},{2,12},{4,10},{6,8},{8,6},{10,4},{12,2},{14,0},{1,15},{3,13... | collective-permute-start | bytes 393224 | tf_op jit(solution)/shard_map/ppermute | solution.py:279
  31.9 4.1 %collective-permute-done.5.l3 = bf16[4,128,128]{2,1,0:T(8,128)(2,1)S(1)} collective-permute-done((bf16[4,128,128]{2,1,0:T(8,128)(2,1)S(1)}, bf16[4,128,128]{2,1,0:T(8,128)(2,1)S(1)}, u32[]{:S(2)}, u32[]{:S(2)}) %collective-permute-start.5) | collective-permute-done | bytes 131104 | tf_op jit(solution)/shard_map/ppermute | solution.py:279
  36.0 0.0 all-to-all-done.rows
  36.0 0.7 copy-done.5
  36.7 1.6 %scale.1 = bf16[4,128,512]{2,1,0:T(8,128)(2,1)S(1)} custom-call(s32[5]{0:T(128)S(1)} %copy-done.5, s32[16,128]{1,0:T(8,128)S(1)} %bitcast.17, bf16[16,32,512]{2,1,0:T(8,128)(2,1)S(1)} %all-to-all-done.rows, bf16[128,512]{1,0:T(8,128)(2,1)S(1)} %get-tuple-element.43.c0, bf16[128,512]{1,0:T(8,128)(2,1)S(1)} %collective-permute-done.1.c1, ...), custom_call_target="tpu_custom_call" | custom-call | flops 1 | bytes 1 | tf_op jit(solution)/shard_map/scale/pallas_call | solution.py:103
  38.3 0.7 pack.1
  38.9 1.5 %collective-permute-start.8 = (bf16[16,128,128]{2,1,0:T(8,128)(2,1)S(1)}, bf16[16,128,128]{2,1,0:T(8,128)(2,1)S(1)}, u32[]{:S(2)}, u32[]{:S(2)}) collective-permute-start(bf16[16,128,128]{2,1,0:T(8,128)(2,1)S(1)} %get-tuple-element.56), channel_id=1, source_target_pairs={{0,16},{1,49},{16,32},{17,1},{32,48},{33,17},{48,0},{49,33},{2,18}... | collective-permute-start | bytes 1572872 | tf_op jit(solution)/shard_map/ppermute | solution.py:296
  40.5 1.5 %collective-permute-start.6 = (bf16[512,512]{1,0:T(8,128)(2,1)S(1)}, bf16[512,512]{1,0:T(8,128)(2,1)S(1)}, u32[]{:S(2)}, u32[]{:S(2)}) collective-permute-start(bf16[512,512]{1,0:T(8,128)(2,1)S(1)} %bitcast.9), channel_id=1, source_target_pairs={{0,64},{1,193},{64,128},{65,1},{128,192},{129,65},{192,0},{193,129... | collective-permute-start | bytes 1572872 | tf_op jit(solution)/shard_map/ppermute | solution.py:293
  41.9 1.8 %collective-permute-start.7 = (bf16[512,512]{1,0:T(8,128)(2,1)S(1)}, bf16[512,512]{1,0:T(8,128)(2,1)S(1)}, u32[]{:S(2)}, u32[]{:S(2)}) collective-permute-start(bf16[512,512]{1,0:T(8,128)(2,1)S(1)} %bitcast.10), channel_id=1, source_target_pairs={{64,0},{193,1},{128,64},{1,65},{192,128},{65,129},{0,192},{129,193... | collective-permute-start | bytes 1572872 | tf_op jit(solution)/shard_map/ppermute | solution.py:294
  43.7 0.6 collective-permute-start.9
  44.3 7.2 %collective-permute-done.9.refs_2_.t2 = bf16[12,128,128]{2,1,0:T(8,128)(2,1)S(1)} collective-permute-done((bf16[12,128,128]{2,1,0:T(8,128)(2,1)S(1)}, bf16[12,128,128]{2,1,0:T(8,128)(2,1)S(1)}, u32[]{:S(2)}, u32[]{:S(2)}) %collective-permute-start.9) | collective-permute-done | bytes 393248 | tf_op jit(solution)/shard_map/ppermute | solution.py:297
  51.5 0.2 collective-permute-done.8.refs_1_.t1
  51.7 1.5 %collective-permute-done.6.s1 = bf16[512,512]{1,0:T(8,128)(2,1)S(1)} collective-permute-done((bf16[512,512]{1,0:T(8,128)(2,1)S(1)}, bf16[512,512]{1,0:T(8,128)(2,1)S(1)}, u32[]{:S(2)}, u32[]{:S(2)}) %collective-permute-start.6) | collective-permute-done | bytes 524320 | tf_op jit(solution)/shard_map/ppermute | solution.py:293
  53.2 1.7 %collective-permute-start.10 = (bf16[12,128,128]{2,1,0:T(8,128)(2,1)S(1)}, bf16[12,128,128]{2,1,0:T(8,128)(2,1)S(1)}, u32[]{:S(2)}, u32[]{:S(2)}) collective-permute-start(bf16[12,128,128]{2,1,0:T(8,128)(2,1)S(1)} %slice.3), channel_id=1, source_target_pairs={{0,16},{1,49},{16,32},{17,1},{32,48},{33,17},{48,0},{49,33},{2,18}... | collective-permute-start | bytes 1179656 | tf_op jit(solution)/shard_map/ppermute | solution.py:301
  54.9 0.0 collective-permute-start.12
  55.0 0.0 collective-permute-start.15
  55.0 0.8 collective-permute-start.11
  55.8 0.0 collective-permute-start.13
  55.8 6.1 %collective-permute-done.10.refs_3_.t3 = bf16[12,128,128]{2,1,0:T(8,128)(2,1)S(1)} collective-permute-done((bf16[12,128,128]{2,1,0:T(8,128)(2,1)S(1)}, bf16[12,128,128]{2,1,0:T(8,128)(2,1)S(1)}, u32[]{:S(2)}, u32[]{:S(2)}) %collective-permute-start.10) | collective-permute-done | bytes 393248 | tf_op jit(solution)/shard_map/ppermute | solution.py:301
  61.9 0.0 collective-permute-done.13.refs_6_
  61.9 1.7 %collective-permute-done.14.refs_7_ = bf16[12,128,128]{2,1,0:T(8,128)(2,1)S(1)} collective-permute-done((bf16[12,128,128]{2,1,0:T(8,128)(2,1)S(1)}, bf16[12,128,128]{2,1,0:T(8,128)(2,1)S(1)}, u32[]{:S(2)}, u32[]{:S(2)}) %collective-permute-start.14) | collective-permute-done | bytes 393248 | tf_op jit(solution)/shard_map/ppermute | solution.py:303
  63.6 1.1 %turn.1.alpha = bf16[4,512,512]{2,1,0:T(8,128)(2,1)S(1)} custom-call(s32[5]{0:T(128)S(1)} %copy-done.5, bf16[12,128,128]{2,1,0:T(8,128)(2,1)S(1)} %get-tuple-element.58.refs_0_, bf16[16,128,128]{2,1,0:T(8,128)(2,1)S(1)} %collective-permute-done.8.refs_1_.t1, bf16[12,128,128]{2,1,0:T(8,128)(2,1)S(1)} %collective-permute-done.9.refs_2_.t2, ...), custom_call_target="tpu_custom_call" | custom-call | flops 1 | bytes 1 | tf_op jit(solution)/shard_map/turn/pallas_call | solution.py:162
  64.8 0.6 collective-permute-done.15.s3
  65.4 2.6 %expect.1 = (f32[4,128,512]{2,1,0:T(8,128)S(1)}, f32[64,1,128]{2,1,0:T(1,128)}) custom-call(s32[5]{0:T(128)S(1)} %copy-done.6, bf16[4,512,512]{2,1,0:T(8,128)(2,1)S(1)} %turn.1.alpha, bf16[512,512]{1,0:T(8,128)(2,1)S(1)} %bitcast.11, bf16[512,512]{1,0:T(8,128)(2,1)S(1)} %collective-permute-done.6.s1, bf16[512,512]{1,0:T(8,128)(2,1)S(1)} %collective-permute-done.7.s2, ...), custom_call_target="tpu_custom_call" | custom-call | flops 1 | bytes 1 | tf_op jit(solution)/shard_map/expect/pallas_call | solution.py:194
  68.0 10.0 %all-to-all-start.1 = ((f32[64,1,128]{2,1,0:T(1,128)}), f32[64,1,128]{2,1,0:T(1,128)S(1)}, u32[]{:S(2)}, u32[]{:S(2)}) async-start(f32[64,1,128]{2,1,0:T(1,128)} %get-tuple-element.67), calls=%async_computation.1 | async-start | bytes 65536 | tf_op jit(solution)/shard_map/all_to_all | solution.py:307
  78.0 0.6 code.1
  78.6 1.6 %collective-permute-start.16 = (bf16[128,512]{1,0:T(8,128)(2,1)S(1)}, bf16[128,512]{1,0:T(8,128)(2,1)S(1)}, u32[]{:S(2)}, u32[]{:S(2)}) collective-permute-start(bf16[128,512]{1,0:T(8,128)(2,1)S(1)} %get-tuple-element.64), channel_id=1, source_target_pairs={{0,16},{16,32},{32,48},{48,0},{1,17},{17,33},{33,49},{49,1},{2,18}... | collective-permute-start | bytes 393224 | tf_op jit(solution)/shard_map/ppermute | solution.py:308
  80.3 1.0 %collective-permute-start.17 = (bf16[128,512]{1,0:T(8,128)(2,1)S(1)}, bf16[128,512]{1,0:T(8,128)(2,1)S(1)}, u32[]{:S(2)}, u32[]{:S(2)}) collective-permute-start(bf16[128,512]{1,0:T(8,128)(2,1)S(1)} %get-tuple-element.65), channel_id=1, source_target_pairs={{0,32},{16,48},{32,0},{48,16},{1,33},{17,49},{33,1},{49,17},{2,34}... | collective-permute-start | bytes 393224 | tf_op jit(solution)/shard_map/ppermute | solution.py:308
  81.2 2.4 %collective-permute-start.18 = (bf16[128,512]{1,0:T(8,128)(2,1)S(1)}, bf16[128,512]{1,0:T(8,128)(2,1)S(1)}, u32[]{:S(2)}, u32[]{:S(2)}) collective-permute-start(bf16[128,512]{1,0:T(8,128)(2,1)S(1)} %get-tuple-element.66), channel_id=1, source_target_pairs={{0,48},{16,0},{32,16},{48,32},{1,49},{17,1},{33,17},{49,33},{2,50}... | collective-permute-start | bytes 393224 | tf_op jit(solution)/shard_map/ppermute | solution.py:308
  83.6 2.9 %all-to-all-done.1.sums = f32[64,1,128]{2,1,0:T(1,128)S(1)} async-done(((f32[64,1,128]{2,1,0:T(1,128)}), f32[64,1,128]{2,1,0:T(1,128)S(1)}, u32[]{:S(2)}, u32[]{:S(2)}) %all-to-all-start.1) | async-done | bytes 32800 | tf_op jit(solution)/shard_map/all_to_all | solution.py:307
  86.5 0.1 column.1.rate
  86.7 1.6 %collective-permute-done.17.e2 = bf16[128,512]{1,0:T(8,128)(2,1)S(1)} collective-permute-done((bf16[128,512]{1,0:T(8,128)(2,1)S(1)}, bf16[128,512]{1,0:T(8,128)(2,1)S(1)}, u32[]{:S(2)}, u32[]{:S(2)}) %collective-permute-start.17) | collective-permute-done | bytes 131104 | tf_op jit(solution)/shard_map/ppermute | solution.py:308
  88.2 1.1 %collective-permute-done.18.e3 = bf16[128,512]{1,0:T(8,128)(2,1)S(1)} collective-permute-done((bf16[128,512]{1,0:T(8,128)(2,1)S(1)}, bf16[128,512]{1,0:T(8,128)(2,1)S(1)}, u32[]{:S(2)}, u32[]{:S(2)}) %collective-permute-start.18) | collective-permute-done | bytes 131104 | tf_op jit(solution)/shard_map/ppermute | solution.py:308
  89.4 2.4 %finish.1 = (f32[128,2048]{1,0:T(8,128)}, bf16[128,2048]{1,0:T(8,128)(2,1)}) custom-call(s32[5]{0:T(128)S(1)} %copy-done.6, bf16[128,2048]{1,0:T(8,128)(2,1)S(1)} %copy-done, f32[4,128,512]{2,1,0:T(8,128)S(1)} %get-tuple-element.63.total, bf16[128,512]{1,0:T(8,128)(2,1)S(1)} %collective-permute-done.16.e1, bf16[128,512]{1,0:T(8,128)(2,1)S(1)} %collective-permute-done.17.e2, ...), custom_call_target="tpu_custom_call" | custom-call | flops 1 | bytes 1 | tf_op jit(solution)/shard_map/finish/pallas_call | solution.py:255
  (21 shorter events, 0.1 us)
Async XLA Ops:
  0.6 37.6 %copy-start = (bf16[128,2048]{1,0:T(8,128)(2,1)S(1)}, bf16[128,2048]{1,0:T(8,128)(2,1)}, u32[]{:S(2)}) copy-start(bf16[128,2048]{1,0:T(8,128)(2,1)} %transition.5) | copy-start | bytes 1572868
  0.7 1.1 %copy-start.1 = (bf16[128,2048]{1,0:T(8,128)(2,1)S(1)}, bf16[128,2048]{1,0:T(8,128)(2,1)}, u32[]{:S(2)}) copy-start(bf16[128,2048]{1,0:T(8,128)(2,1)} %a.1) | copy-start | bytes 1572868
  1.8 7.3 %copy-start.4 = (s32[5]{0:T(128)}, s32[5]{0:T(128)S(1)}, u32[]{:S(2)}) copy-start(s32[5]{0:T(128)S(1)} %stack.23.pos) | copy-start | bytes 64
  1.8 18.7 %copy-start.2 = (bf16[128,128]{1,0:T(8,128)(2,1)S(1)}, bf16[128,128]{1,0:T(8,128)(2,1)}, u32[]{:S(2)}) copy-start(bf16[128,128]{1,0:T(8,128)(2,1)} %param.6) | copy-start | bytes 98308
  1.8 34.2 %copy-start.3 = (s32[2048]{0:T(1024)S(1)}, s32[2048]{0:T(1024)}, u32[]{:S(2)}) copy-start(s32[2048]{0:T(1024)} %param.5) | copy-start | bytes 24580
  2.4 12.2 %collective-permute-start.1 = (bf16[128,512]{1,0:T(8,128)(2,1)S(1)}, bf16[128,512]{1,0:T(8,128)(2,1)S(1)}, u32[]{:S(2)}, u32[]{:S(2)}) collective-permute-start(bf16[128,512]{1,0:T(8,128)(2,1)S(1)} %get-tuple-element.36), channel_id=1, source_target_pairs={{0,16},{16,32},{32,48},{48,0},{1,17},{17,33},{33,49},{49,1},{2,18}... | collective-permute-start | bytes 393224 | tf_op jit(solution)/shard_map/ppermute | solution.py:282
  4.0 10.6 %collective-permute-start.2 = (bf16[128,512]{1,0:T(8,128)(2,1)S(1)}, bf16[128,512]{1,0:T(8,128)(2,1)S(1)}, u32[]{:S(2)}, u32[]{:S(2)}) collective-permute-start(bf16[128,512]{1,0:T(8,128)(2,1)S(1)} %get-tuple-element.37), channel_id=1, source_target_pairs={{0,32},{16,48},{32,0},{48,16},{1,33},{17,49},{33,1},{49,17},{2,34}... | collective-permute-start | bytes 393224 | tf_op jit(solution)/shard_map/ppermute | solution.py:282
  6.8 7.8 %collective-permute-start.3 = (bf16[128,512]{1,0:T(8,128)(2,1)S(1)}, bf16[128,512]{1,0:T(8,128)(2,1)S(1)}, u32[]{:S(2)}, u32[]{:S(2)}) collective-permute-start(bf16[128,512]{1,0:T(8,128)(2,1)S(1)} %get-tuple-element.38), channel_id=1, source_target_pairs={{0,48},{16,0},{32,16},{48,32},{1,49},{17,1},{33,17},{49,33},{2,50}... | collective-permute-start | bytes 393224 | tf_op jit(solution)/shard_map/ppermute | solution.py:282
  7.3 7.3 %collective-permute-start = (bf16[1,128,128]{2,1,0:T(8,128)(2,1)}, bf16[1,128,128]{2,1,0:T(8,128)(2,1)S(1)}, u32[]{:S(2)}, u32[]{:S(2)}) collective-permute-start(bf16[1,128,128]{2,1,0:T(8,128)(2,1)} %bitcast.12), channel_id=1, source_target_pairs={{0,2},{2,0},{4,6},{6,4},{8,10},{10,8},{12,14},{14,12},{1,3},{3,1},... | collective-permute-start | bytes 98312 | tf_op jit(solution)/shard_map/ppermute | solution.py:279
  14.6 50.8 %copy-start.6 = (s32[5]{0:T(128)S(1)}, s32[5]{0:T(128)}, u32[]{:S(2)}) copy-start(s32[5]{0:T(128)} %copy-done.4) | copy-start | bytes 64
  14.6 21.4 %all-to-all-start = ((bf16[16,32,512]{2,1,0:T(8,128)(2,1)}), bf16[16,32,512]{2,1,0:T(8,128)(2,1)S(1)}, u32[]{:S(2)}, u32[]{:S(2)}) async-start(bf16[16,32,512]{2,1,0:T(8,128)(2,1)} %bitcast.18), calls=%async_computation | async-start | bytes 1048576 | tf_op jit(solution)/shard_map/all_to_all | solution.py:286
  20.6 5.6 %collective-permute-start.4 = (bf16[2,128,128]{2,1,0:T(8,128)(2,1)S(1)}, bf16[2,128,128]{2,1,0:T(8,128)(2,1)S(1)}, u32[]{:S(2)}, u32[]{:S(2)}) collective-permute-start(bf16[2,128,128]{2,1,0:T(8,128)(2,1)S(1)} %pad_maximum_fusion.1), channel_id=1, source_target_pairs={{0,4},{2,6},{4,0},{6,2},{8,12},{10,14},{12,8},{14,10},{1,5},{3,7},... | collective-permute-start | bytes 196616 | tf_op jit(solution)/shard_map/ppermute | solution.py:279
  26.2 9.8 %collective-permute-start.5 = (bf16[4,128,128]{2,1,0:T(8,128)(2,1)S(1)}, bf16[4,128,128]{2,1,0:T(8,128)(2,1)S(1)}, u32[]{:S(2)}, u32[]{:S(2)}) collective-permute-start(bf16[4,128,128]{2,1,0:T(8,128)(2,1)S(1)} %pad_maximum_fusion), channel_id=1, source_target_pairs={{0,14},{2,12},{4,10},{6,8},{8,6},{10,4},{12,2},{14,0},{1,15},{3,13... | collective-permute-start | bytes 393224 | tf_op jit(solution)/shard_map/ppermute | solution.py:279
  36.0 0.7 copy-start.5
  38.9 12.8 %collective-permute-start.8 = (bf16[16,128,128]{2,1,0:T(8,128)(2,1)S(1)}, bf16[16,128,128]{2,1,0:T(8,128)(2,1)S(1)}, u32[]{:S(2)}, u32[]{:S(2)}) collective-permute-start(bf16[16,128,128]{2,1,0:T(8,128)(2,1)S(1)} %get-tuple-element.56), channel_id=1, source_target_pairs={{0,16},{1,49},{16,32},{17,1},{32,48},{33,17},{48,0},{49,33},{2,18}... | collective-permute-start | bytes 1572872 | tf_op jit(solution)/shard_map/ppermute | solution.py:296
  40.5 12.7 %collective-permute-start.6 = (bf16[512,512]{1,0:T(8,128)(2,1)S(1)}, bf16[512,512]{1,0:T(8,128)(2,1)S(1)}, u32[]{:S(2)}, u32[]{:S(2)}) collective-permute-start(bf16[512,512]{1,0:T(8,128)(2,1)S(1)} %bitcast.9), channel_id=1, source_target_pairs={{0,64},{1,193},{64,128},{65,1},{128,192},{129,65},{192,0},{193,129... | collective-permute-start | bytes 1572872 | tf_op jit(solution)/shard_map/ppermute | solution.py:293
  41.9 11.2 %collective-permute-start.7 = (bf16[512,512]{1,0:T(8,128)(2,1)S(1)}, bf16[512,512]{1,0:T(8,128)(2,1)S(1)}, u32[]{:S(2)}, u32[]{:S(2)}) collective-permute-start(bf16[512,512]{1,0:T(8,128)(2,1)S(1)} %bitcast.10), channel_id=1, source_target_pairs={{64,0},{193,1},{128,64},{1,65},{192,128},{65,129},{0,192},{129,193... | collective-permute-start | bytes 1572872 | tf_op jit(solution)/shard_map/ppermute | solution.py:294
  43.7 7.8 %collective-permute-start.9 = (bf16[12,128,128]{2,1,0:T(8,128)(2,1)S(1)}, bf16[12,128,128]{2,1,0:T(8,128)(2,1)S(1)}, u32[]{:S(2)}, u32[]{:S(2)}) collective-permute-start(bf16[12,128,128]{2,1,0:T(8,128)(2,1)S(1)} %get-tuple-element.58.refs_0_), channel_id=1, source_target_pairs={{16,0},{49,1},{32,16},{1,17},{48,32},{17,33},{0,48},{33,49},{18,2}... | collective-permute-start | bytes 1179656 | tf_op jit(solution)/shard_map/ppermute | solution.py:297
  53.2 8.7 %collective-permute-start.10 = (bf16[12,128,128]{2,1,0:T(8,128)(2,1)S(1)}, bf16[12,128,128]{2,1,0:T(8,128)(2,1)S(1)}, u32[]{:S(2)}, u32[]{:S(2)}) collective-permute-start(bf16[12,128,128]{2,1,0:T(8,128)(2,1)S(1)} %slice.3), channel_id=1, source_target_pairs={{0,16},{1,49},{16,32},{17,1},{32,48},{33,17},{48,0},{49,33},{2,18}... | collective-permute-start | bytes 1179656 | tf_op jit(solution)/shard_map/ppermute | solution.py:301
  54.9 7.0 %collective-permute-start.12 = (bf16[16,128,128]{2,1,0:T(8,128)(2,1)S(1)}, bf16[16,128,128]{2,1,0:T(8,128)(2,1)S(1)}, u32[]{:S(2)}, u32[]{:S(2)}) collective-permute-start(bf16[16,128,128]{2,1,0:T(8,128)(2,1)S(1)} %collective-permute-done.8.refs_1_.t1), channel_id=1, source_target_pairs={{0,1},{1,0},{2,3},{3,2},{4,5},{5,4},{6,7},{7,6},{8,9},{9,8},{10,11... | collective-permute-start | bytes 1572872 | tf_op jit(solution)/shard_map/ppermute | solution.py:303
  55.0 10.4 %collective-permute-start.15 = (bf16[512,512]{1,0:T(8,128)(2,1)S(1)}, bf16[512,512]{1,0:T(8,128)(2,1)S(1)}, u32[]{:S(2)}, u32[]{:S(2)}) collective-permute-start(bf16[512,512]{1,0:T(8,128)(2,1)S(1)} %collective-permute-done.6.s1), channel_id=1, source_target_pairs={{0,64},{1,193},{64,128},{65,1},{128,192},{129,65},{192,0},{193,129... | collective-permute-start | bytes 1572872 | tf_op jit(solution)/shard_map/ppermute | solution.py:300
  55.0 6.9 %collective-permute-start.11 = (bf16[12,128,128]{2,1,0:T(8,128)(2,1)S(1)}, bf16[12,128,128]{2,1,0:T(8,128)(2,1)S(1)}, u32[]{:S(2)}, u32[]{:S(2)}) collective-permute-start(bf16[12,128,128]{2,1,0:T(8,128)(2,1)S(1)} %get-tuple-element.58.refs_0_), channel_id=1, source_target_pairs={{0,1},{1,0},{2,3},{3,2},{4,5},{5,4},{6,7},{7,6},{8,9},{9,8},{10,11... | collective-permute-start | bytes 1179656 | tf_op jit(solution)/shard_map/ppermute | solution.py:303
  55.8 6.1 %collective-permute-start.13 = (bf16[12,128,128]{2,1,0:T(8,128)(2,1)S(1)}, bf16[12,128,128]{2,1,0:T(8,128)(2,1)S(1)}, u32[]{:S(2)}, u32[]{:S(2)}) collective-permute-start(bf16[12,128,128]{2,1,0:T(8,128)(2,1)S(1)} %collective-permute-done.9.refs_2_.t2), channel_id=1, source_target_pairs={{0,1},{1,0},{2,3},{3,2},{4,5},{5,4},{6,7},{7,6},{8,9},{9,8},{10,11... | collective-permute-start | bytes 1179656 | tf_op jit(solution)/shard_map/ppermute | solution.py:303
  61.9 1.7 %collective-permute-start.14 = (bf16[12,128,128]{2,1,0:T(8,128)(2,1)S(1)}, bf16[12,128,128]{2,1,0:T(8,128)(2,1)S(1)}, u32[]{:S(2)}, u32[]{:S(2)}) collective-permute-start(bf16[12,128,128]{2,1,0:T(8,128)(2,1)S(1)} %collective-permute-done.10.refs_3_.t3), channel_id=1, source_target_pairs={{0,1},{1,0},{2,3},{3,2},{4,5},{5,4},{6,7},{7,6},{8,9},{9,8},{10,11... | collective-permute-start | bytes 1179656 | tf_op jit(solution)/shard_map/ppermute | solution.py:303
  68.0 18.5 %all-to-all-start.1 = ((f32[64,1,128]{2,1,0:T(1,128)}), f32[64,1,128]{2,1,0:T(1,128)S(1)}, u32[]{:S(2)}, u32[]{:S(2)}) async-start(f32[64,1,128]{2,1,0:T(1,128)} %get-tuple-element.67), calls=%async_computation.1 | async-start | bytes 65536 | tf_op jit(solution)/shard_map/all_to_all | solution.py:307
  78.6 8.0 %collective-permute-start.16 = (bf16[128,512]{1,0:T(8,128)(2,1)S(1)}, bf16[128,512]{1,0:T(8,128)(2,1)S(1)}, u32[]{:S(2)}, u32[]{:S(2)}) collective-permute-start(bf16[128,512]{1,0:T(8,128)(2,1)S(1)} %get-tuple-element.64), channel_id=1, source_target_pairs={{0,16},{16,32},{32,48},{48,0},{1,17},{17,33},{33,49},{49,1},{2,18}... | collective-permute-start | bytes 393224 | tf_op jit(solution)/shard_map/ppermute | solution.py:308
  80.3 8.0 %collective-permute-start.17 = (bf16[128,512]{1,0:T(8,128)(2,1)S(1)}, bf16[128,512]{1,0:T(8,128)(2,1)S(1)}, u32[]{:S(2)}, u32[]{:S(2)}) collective-permute-start(bf16[128,512]{1,0:T(8,128)(2,1)S(1)} %get-tuple-element.65), channel_id=1, source_target_pairs={{0,32},{16,48},{32,0},{48,16},{1,33},{17,49},{33,1},{49,17},{2,34}... | collective-permute-start | bytes 393224 | tf_op jit(solution)/shard_map/ppermute | solution.py:308
  81.2 8.1 %collective-permute-start.18 = (bf16[128,512]{1,0:T(8,128)(2,1)S(1)}, bf16[128,512]{1,0:T(8,128)(2,1)S(1)}, u32[]{:S(2)}, u32[]{:S(2)}) collective-permute-start(bf16[128,512]{1,0:T(8,128)(2,1)S(1)} %get-tuple-element.66), channel_id=1, source_target_pairs={{0,48},{16,0},{32,16},{48,32},{1,49},{17,1},{33,17},{49,33},{2,50}... | collective-permute-start | bytes 393224 | tf_op jit(solution)/shard_map/ppermute | solution.py:308

commit v3 on v2

--- a/solution.py
+++ b/solution.py
@@ -107,13 +107,31 @@
         out_shape=jax.ShapeDtypeStruct((4, 128, 512), BF16),
         scratch_shapes=[pltpu.VMEM((16, 32, 512), F32)],
         compiler_params=params(16),
-        cost_estimate=SMALL,
+        cost_estimate=pl.CostEstimate(flops=10**10, bytes_accessed=10**7, transcendentals=0),
         name="scale",
     )(pos, ids, rows, *cuts)
 
 
 def quarter(pos, transition, away):
     return transition[:, pl.ds(pl.multiple_of(((pos[2] + away + 4) & 3) * 512, 512), 512)]
+
+
+def join_kernel(l0, l1, l2, out):
+    out[0:1] = l0[...]
+    out[1:2] = l1[...]
+    out[2:4] = l2[...]
+
+
+def join(line):
+    return pl.pallas_call(
+        join_kernel,
+        in_specs=[VM] * 3,
+        out_specs=VM,
+        out_shape=jax.ShapeDtypeStruct((4, 128, 128), BF16),
+        compiler_params=params(8),
+        cost_estimate=pl.CostEstimate(flops=3 * 10**10, bytes_accessed=10**6, transcendentals=0),
+        name="join",
+    )(*line)
 
 
 def pack_kernel(pos, l0, l1, l2, l3, transition, ahead, behind):
@@ -170,13 +188,18 @@
     )(pos, *parts)
 
 
-def expect_kernel(pos, alpha, s0, s1, s2, s3, transition, t1, t2, t3, total, sums):
+def expect_kernel(pos, alpha, s0, s1, s2, s3, transition, t1, t2, t3, total, sums, e1, e2, e3):
     step = 1 - 2 * pos[3]
     groups = (pos[1], (pos[1] - step + 4) & 3, (pos[1] + step + 4) & 3, (pos[1] + 2) & 3)
     acc = jnp.zeros((512, 512), F32)
     for group, part in zip(groups, (s0, s1, s2, s3)):
         acc += jnp.dot(alpha[group], part[...], preferred_element_type=F32)
     total[...] = acc.reshape(4, 128, 512)
+    for d, e in enumerate((e1, e2, e3), 1):
+        power = total[(pos[2] + d) & 3]
+        power = power * power
+        power = power * power
+        e[...] = (power * power).astype(BF16)
     for t, first, away in ((None, 0, 0), (t1, 0, -step), (t2, 0, step), (t3, 8, 2)):
         block = (pos[2] + away + 4) & 3
         lanes = jnp.zeros((128, 128), F32)
@@ -187,43 +210,27 @@
             weight = mine[:, part] if t is None else t[first + n]
             lanes += weight.astype(F32) * total[block, :, part]
         line = jnp.sum(lanes.T, axis=0, keepdims=True)
-        sums[pl.ds(block * 16, 16)] = jnp.broadcast_to(line[None], (16, 1, 128))
+        sums[pl.ds(block, 1)] = line[None]
 
 
 def expect(pos, alpha, parts, transition, quarters):
     return pl.pallas_call(
         expect_kernel,
         in_specs=[SM] + [VM] * 9,
-        out_specs=[VM] * 2,
-        out_shape=[jax.ShapeDtypeStruct((4, 128, 512), F32), jax.ShapeDtypeStruct((64, 1, 128), F32)],
+        out_specs=[VM] * 5,
+        out_shape=[
+            jax.ShapeDtypeStruct((4, 128, 512), F32),
+            jax.ShapeDtypeStruct((4, 1, 128), F32),
+            *[jax.ShapeDtypeStruct((128, 512), BF16)] * 3,
+        ],
         compiler_params=params(24),
         cost_estimate=SMALL,
         name="expect",
     )(pos, alpha, *parts, transition, *quarters)
 
 
-def code_kernel(pos, total, *outs):
-    for d, out in enumerate(outs, 1):
-        power = total[(pos[2] + d) & 3]
-        power = power * power
-        power = power * power
-        out[...] = (power * power).astype(BF16)
-
-
-def code(pos, total):
-    return pl.pallas_call(
-        code_kernel,
-        in_specs=[SM, VM],
-        out_specs=[VM] * 3,
-        out_shape=[jax.ShapeDtypeStruct((128, 512), BF16)] * 3,
-        compiler_params=params(8),
-        cost_estimate=pl.CostEstimate(flops=10**9, bytes_accessed=10**7, transcendentals=0),
-        name="code",
-    )(pos, total)
-
-
 def column_kernel(sums, out):
-    whole = jnp.sum(sums[...].reshape(64, 128), axis=0, keepdims=True)
+    whole = jnp.sum(sums[...].reshape(32, 128), axis=0, keepdims=True)
     out[...] = STATES / jnp.broadcast_to(whole, (128, 128)).T
 
 
@@ -239,24 +246,37 @@
     )(sums)
 
 
-def finish_kernel(pos, transition, total, e1, e2, e3, rate, counts, out):
+def finish_kernel(pos, transition, total, e1, e2, e3, rate, counts, out, kept, rounded, sems):
+    copies = []
     for d, e in enumerate((None, e1, e2, e3)):
         part = pl.ds(pl.multiple_of(((pos[2] - d + 4) & 3) * 512, 512), 512)
         if d:
-            expected = jnp.sqrt(jnp.sqrt(jnp.sqrt(e[...].astype(F32))))
+            root = lax.rsqrt(lax.rsqrt(e[...].astype(F32)))
+            expected = root * lax.rsqrt(root)
         else:
             expected = total[pos[2]]
         count = transition[:, part].astype(F32) * expected
-        counts[:, part] = count
-        out[:, part] = (count * jnp.concatenate([rate[...]] * 4, axis=1)).astype(BF16)
+        kept[d] = count
+        rounded[d] = (count * jnp.concatenate([rate[...]] * 4, axis=1)).astype(BF16)
+        copies.append(pltpu.make_async_copy(kept.at[d], counts.at[:, part], sems.at[2 * d]))
+        copies.append(pltpu.make_async_copy(rounded.at[d], out.at[:, part], sems.at[2 * d + 1]))
+        copies[-2].start()
+        copies[-1].start()
+    for copy in copies:
+        copy.wait()
 
 
 def finish(pos, transition, total, parts, rate):
     return pl.pallas_call(
         finish_kernel,
         in_specs=[SM] + [VM] * 6,
-        out_specs=[VM] * 2,
+        out_specs=[pl.BlockSpec(memory_space=pl.ANY)] * 2,
         out_shape=[jax.ShapeDtypeStruct((128, 2048), F32), jax.ShapeDtypeStruct((128, 2048), BF16)],
+        scratch_shapes=[
+            pltpu.VMEM((4, 128, 512), F32),
+            pltpu.VMEM((4, 128, 512), BF16),
+            pltpu.SemaphoreType.DMA((8,)),
+        ],
         compiler_params=params(16),
         cost_estimate=SMALL,
         name="finish",
@@ -285,27 +305,27 @@
 
     rows = lax.all_to_all(picked.reshape(16, 32, 512), ("y", "x"), 0, 0)
     line.append(flip(jnp.concatenate(line), 2))
-    line.append(flip(jnp.concatenate(line), 7))
-    rows, line = together((rows, line))
+    line.append(flip(join(line), 7))
     own = scale(pos, ids, rows, betas).reshape(512, 512)
 
-    own, line = together((own, line))
     one = lax.ppermute(own, ("y", "k"), ahead)
     two = lax.ppermute(own, ("y", "k"), behind)
     to_a, to_b = pack(pos, line, transition)
     one_a = lax.ppermute(to_a, ("x", "k"), ahead)
     two_a = lax.ppermute(to_b, ("x", "k"), behind)
 
-    one, two, one_a, two_a, to_b = together((one, two, one_a, two_a, to_b))
     far = lax.ppermute(one, ("y", "k"), ahead)
     far_a = lax.ppermute(one_a[4:], ("x", "k"), ahead)
+    far_a, two = together((far_a, two))
     sources = [to_b, one_a, two_a, far_a]
     sources += [lax.ppermute(a, "k", swap) for a in sources]
     alpha_t = turn(pos, sources)
 
-    total, sums = expect(pos, alpha_t, (own, one, two, far), transition, (one_a, two_a, far_a))
-    sums = lax.all_to_all(sums, ("x", "z", "k"), 0, 0)
-    parts = [lax.ppermute(e, "x", ring(d)) for d, e in enumerate(code(pos, total), 1)]
+    total, sums, *parts = expect(pos, alpha_t, (own, one, two, far), transition, (one_a, two_a, far_a))
+    sums = sums + lax.ppermute(sums, "k", swap)
+    sums = jnp.broadcast_to(sums[:, None], (4, 8, 1, 128)).reshape(32, 1, 128)
+    sums = lax.all_to_all(sums, ("x", "z"), 0, 0)
+    parts = [lax.ppermute(e, "x", ring(d)) for d, e in enumerate(parts, 1)]
     return finish(pos, transition, total, parts, column(sums))
 
 

time: 92.7 us -> 84.5 us (0.912)
  waiting for transfers between devices: 29.2 us -> 25.8 us
  starting transfers between devices: 44.7 us -> 42.3 us
  Pallas kernels: 15.1 us -> 13.3 us
    ppermute x1, waiting for transfers between devices: 7.21 us -> 0.06 us  [per_device(): two_a = lax.ppermute(to_b, ('x', 'k'), behind)]
    ppermute x1, waiting for transfers between devices: 0.6 us -> 5.02 us  [per_device(): far = lax.ppermute(one, ('y', 'k'), ahead)]
    ppermute x1, waiting for transfers between devices: 6.07 us -> 1.93 us  [per_device(): far_a = lax.ppermute(one_a[4:], ('x', 'k'), ahead)]
    ppermute x1, waiting for transfers between devices: 0.2 us -> 3.83 us  [per_device(): one_a = lax.ppermute(to_a, ('x', 'k'), ahead)]
    ppermute x3, waiting for transfers between devices: 6.36 us -> 3.03 us  [per_device(): flip = lambda a, by: lax.ppermute(a, 'z', [(i, i ^ by) for i in range(8)])]
    ppermute x1, waiting for transfers between devices: 1.49 us -> 3.88 us  [per_device(): one = lax.ppermute(own, ('y', 'k'), ahead)]
    ppermute x3, starting transfers between devices: 10.9 us -> 8.69 us  [per_device(): flip = lambda a, by: lax.ppermute(a, 'z', [(i, i ^ by) for i in range(8)])]
    all_to_all x1, starting transfers between devices: 9.99 us -> 8.66 us  [per_device(): sums = lax.all_to_all(sums, ('x', 'z'), 0, 0)]
  transfers between devices with their start and end apart: 21 -> 22, of which waited for: 11 -> 12; matrix products, arithmetic and copies ran while one was open for 0% -> 0% of each run, Pallas kernels for 8% -> 11%
where the time goes in v3:
time: 84.5 us; the launch traced here: 84.2 us
  starting transfers between devices  42.3 us (50%)
  waiting for transfers between devices  25.8 us (31%)
  Pallas kernels  13.3 us (16%)
  local copies, waits for them, and re-layouts  1.79 us (2%)
  between operations  1 us (1%)
    ppermute x3, starting transfers between devices, per_device(): flip = lambda a, by: lax.ppermute(a, 'z', [(i, i ^ by) for i in range(8)])  8.69 us
    all_to_all x1, starting transfers between devices, per_device(): sums = lax.all_to_all(sums, ('x', 'z'), 0, 0)  8.66 us
    all_to_all x1, starting transfers between devices, per_device(): rows = lax.all_to_all(picked.reshape(16, 32, 512), ('y', 'x'), 0, 0)  5.95 us
    pallas_call x1, Pallas kernels, pick(): pl.pallas_call(pick_kernel, in_specs=[SM, VM, pl.BlockSpec(memory_space=p...  5.38 us
    ppermute x1, waiting for transfers between devices, per_device(): far = lax.ppermute(one, ('y', 'k'), ahead)  5.02 us
    ppermute x3, starting transfers between devices, per_device(): lax.ppermute(c, 'x', ring(d))  4.83 us
    ppermute x3, starting transfers between devices, per_device(): parts = [lax.ppermute(e, 'x', ring(d)) for d, e in enumerate(parts, 1)]  4.82 us
    ppermute x1, waiting for transfers between devices, per_device(): one = lax.ppermute(own, ('y', 'k'), ahead)  3.88 us
  transfers between devices with their start and end apart: 22, of which 12 were waited for; matrix products, arithmetic and copies ran while one was open for 0% of the time, Pallas kernels for 11%

profile of v3, /device:TPU:2, one launch (start us, length us, event | category | flops | bytes accessed | tf_op | source)
XLA Modules:
  0.0 84.2 jit_solution(2329562727968245613)
XLA Ops:
  0.6 0.0 copy-start.2
  0.6 0.1 stack.23.pos
  0.7 1.0 %copy-done.1 = bf16[128,2048]{1,0:T(8,128)(2,1)S(1)} copy-done((bf16[128,2048]{1,0:T(8,128)(2,1)S(1)}, bf16[128,2048]{1,0:T(8,128)(2,1)}, u32[]{:S(2)}) %copy-start.1) | copy-done | bytes 524312
  1.8 0.6 cut.1
  2.4 1.6 %collective-permute-start.1 = (bf16[128,512]{1,0:T(8,128)(2,1)S(1)}, bf16[128,512]{1,0:T(8,128)(2,1)S(1)}, u32[]{:S(2)}, u32[]{:S(2)}) collective-permute-start(bf16[128,512]{1,0:T(8,128)(2,1)S(1)} %get-tuple-element.23), channel_id=1, source_target_pairs={{0,16},{16,32},{32,48},{48,0},{1,17},{17,33},{33,49},{49,1},{2,18}... | collective-permute-start | bytes 393224 | tf_op jit(solution)/shard_map/ppermute | solution.py:302
  3.9 2.8 %collective-permute-start.2 = (bf16[128,512]{1,0:T(8,128)(2,1)S(1)}, bf16[128,512]{1,0:T(8,128)(2,1)S(1)}, u32[]{:S(2)}, u32[]{:S(2)}) collective-permute-start(bf16[128,512]{1,0:T(8,128)(2,1)S(1)} %get-tuple-element.24), channel_id=1, source_target_pairs={{0,32},{16,48},{32,0},{48,16},{1,33},{17,49},{33,1},{49,17},{2,34}... | collective-permute-start | bytes 393224 | tf_op jit(solution)/shard_map/ppermute | solution.py:302
  6.8 0.4 collective-permute-start.3
  7.2 1.9 %collective-permute-start = (bf16[1,128,128]{2,1,0:T(8,128)(2,1)}, bf16[1,128,128]{2,1,0:T(8,128)(2,1)S(1)}, u32[]{:S(2)}, u32[]{:S(2)}) collective-permute-start(bf16[1,128,128]{2,1,0:T(8,128)(2,1)} %bitcast.14), channel_id=1, source_target_pairs={{0,2},{2,0},{4,6},{6,4},{8,10},{10,8},{12,14},{14,12},{1,3},{3,1},... | collective-permute-start | bytes 98312 | tf_op jit(solution)/shard_map/ppermute | solution.py:299
  9.1 5.4 %pick.1 = bf16[4,4,32,512]{3,2,1,0:T(8,128)(2,1)} custom-call(s32[5]{0:T(128)} %copy-done.3, s32[16,128]{1,0:T(8,128)} %bitcast.18, bf16[2000,2048]{1,0:T(8,128)(2,1)} %table.1), custom_call_target="tpu_custom_call" | custom-call | flops 1 | bytes 1 | tf_op jit(solution)/shard_map/pick/pallas_call | solution.py:71
  14.5 0.0 collective-permute-done.l1
  14.5 0.0 collective-permute-done.3.c3
  14.6 3.4 %collective-permute-start.4 = (bf16[2,128,128]{2,1,0:T(8,128)(2,1)S(1)}, bf16[2,128,128]{2,1,0:T(8,128)(2,1)S(1)}, u32[]{:S(2)}, u32[]{:S(2)}) collective-permute-start(bf16[2,128,128]{2,1,0:T(8,128)(2,1)S(1)} %pad_maximum_fusion), channel_id=1, source_target_pairs={{0,4},{2,6},{4,0},{6,2},{8,12},{10,14},{12,8},{14,10},{1,5},{3,7},... | collective-permute-start | bytes 196616 | tf_op jit(solution)/shard_map/ppermute | solution.py:299
  17.9 5.9 %all-to-all-start = ((bf16[16,32,512]{2,1,0:T(8,128)(2,1)}), bf16[16,32,512]{2,1,0:T(8,128)(2,1)S(1)}, u32[]{:S(2)}, u32[]{:S(2)}) async-start(bf16[16,32,512]{2,1,0:T(8,128)(2,1)} %bitcast.20), calls=%async_computation | async-start | bytes 1048576 | tf_op jit(solution)/shard_map/all_to_all | solution.py:306
  23.9 0.0 copy-start.4
  23.9 0.0 copy-start.5
  23.9 0.0 collective-permute-done.4.l2
  23.9 3.4 %collective-permute-start.5 = (bf16[4,128,128]{2,1,0:T(8,128)(2,1)S(1)}, bf16[4,128,128]{2,1,0:T(8,128)(2,1)S(1)}, u32[]{:S(2)}, u32[]{:S(2)}) collective-permute-start(bf16[4,128,128]{2,1,0:T(8,128)(2,1)S(1)} %join.1), channel_id=1, source_target_pairs={{0,14},{2,12},{4,10},{6,8},{8,6},{10,4},{12,2},{14,0},{1,15},{3,13... | collective-permute-start | bytes 393224 | tf_op jit(solution)/shard_map/ppermute | solution.py:299
  27.4 3.0 %collective-permute-done.5.l3 = bf16[4,128,128]{2,1,0:T(8,128)(2,1)S(1)} collective-permute-done((bf16[4,128,128]{2,1,0:T(8,128)(2,1)S(1)}, bf16[4,128,128]{2,1,0:T(8,128)(2,1)S(1)}, u32[]{:S(2)}, u32[]{:S(2)}) %collective-permute-start.5) | collective-permute-done | bytes 131104 | tf_op jit(solution)/shard_map/ppermute | solution.py:299
  30.4 0.7 pack.1
  31.1 1.5 %collective-permute-start.6 = (bf16[16,128,128]{2,1,0:T(8,128)(2,1)S(1)}, bf16[16,128,128]{2,1,0:T(8,128)(2,1)S(1)}, u32[]{:S(2)}, u32[]{:S(2)}) collective-permute-start(bf16[16,128,128]{2,1,0:T(8,128)(2,1)S(1)} %get-tuple-element.29), channel_id=1, source_target_pairs={{0,16},{1,49},{16,32},{17,1},{32,48},{33,17},{48,0},{49,33},{2,18}... | collective-permute-start | bytes 1572872 | tf_op jit(solution)/shard_map/ppermute | solution.py:314
  32.6 0.1 all-to-all-done.rows
  32.7 1.6 %scale.1 = bf16[4,128,512]{2,1,0:T(8,128)(2,1)S(1)} custom-call(s32[5]{0:T(128)S(1)} %copy-done.4, s32[16,128]{1,0:T(8,128)S(1)} %bitcast.19, bf16[16,32,512]{2,1,0:T(8,128)(2,1)S(1)} %all-to-all-done.rows, bf16[128,512]{1,0:T(8,128)(2,1)S(1)} %get-tuple-element.31.c0, bf16[128,512]{1,0:T(8,128)(2,1)S(1)} %collective-permute-done.1.c1, ...), custom_call_target="tpu_custom_call" | custom-call | flops 10000000000 | bytes 10000000 | tf_op jit(solution)/shard_map/scale/pallas_call | solution.py:103
  34.3 1.5 %collective-permute-start.14 = (bf16[512,512]{1,0:T(8,128)(2,1)S(1)}, bf16[512,512]{1,0:T(8,128)(2,1)S(1)}, u32[]{:S(2)}, u32[]{:S(2)}) collective-permute-start(bf16[512,512]{1,0:T(8,128)(2,1)S(1)} %bitcast.11), channel_id=1, source_target_pairs={{0,64},{1,193},{64,128},{65,1},{128,192},{129,65},{192,0},{193,129... | collective-permute-start | bytes 1572872 | tf_op jit(solution)/shard_map/ppermute | solution.py:311
  35.7 1.9 %collective-permute-start.9 = (bf16[512,512]{1,0:T(8,128)(2,1)S(1)}, bf16[512,512]{1,0:T(8,128)(2,1)S(1)}, u32[]{:S(2)}, u32[]{:S(2)}) collective-permute-start(bf16[512,512]{1,0:T(8,128)(2,1)S(1)} %bitcast.12), channel_id=1, source_target_pairs={{64,0},{193,1},{128,64},{1,65},{192,128},{65,129},{0,192},{129,193... | collective-permute-start | bytes 1572872 | tf_op jit(solution)/shard_map/ppermute | solution.py:312
  37.6 1.4 %collective-permute-start.7 = (bf16[12,128,128]{2,1,0:T(8,128)(2,1)S(1)}, bf16[12,128,128]{2,1,0:T(8,128)(2,1)S(1)}, u32[]{:S(2)}, u32[]{:S(2)}) collective-permute-start(bf16[12,128,128]{2,1,0:T(8,128)(2,1)S(1)} %get-tuple-element.28.refs_0_), channel_id=1, source_target_pairs={{16,0},{49,1},{32,16},{1,17},{48,32},{17,33},{0,48},{33,49},{18,2}... | collective-permute-start | bytes 1179656 | tf_op jit(solution)/shard_map/ppermute | solution.py:315
  39.0 3.8 %collective-permute-done.6.refs_1_.t1 = bf16[16,128,128]{2,1,0:T(8,128)(2,1)S(1)} collective-permute-done((bf16[16,128,128]{2,1,0:T(8,128)(2,1)S(1)}, bf16[16,128,128]{2,1,0:T(8,128)(2,1)S(1)}, u32[]{:S(2)}, u32[]{:S(2)}) %collective-permute-start.6) | collective-permute-done | bytes 524320 | tf_op jit(solution)/shard_map/ppermute | solution.py:314
  42.9 2.5 %collective-permute-start.8 = (bf16[12,128,128]{2,1,0:T(8,128)(2,1)S(1)}, bf16[12,128,128]{2,1,0:T(8,128)(2,1)S(1)}, u32[]{:S(2)}, u32[]{:S(2)}) collective-permute-start(bf16[12,128,128]{2,1,0:T(8,128)(2,1)S(1)} %slice.4), channel_id=1, source_target_pairs={{0,16},{1,49},{16,32},{17,1},{32,48},{33,17},{48,0},{49,33},{2,18}... | collective-permute-start | bytes 1179656 | tf_op jit(solution)/shard_map/ppermute | solution.py:318
  45.4 0.0 collective-permute-start.11
  45.4 3.9 %collective-permute-done.14.s1 = bf16[512,512]{1,0:T(8,128)(2,1)S(1)} collective-permute-done((bf16[512,512]{1,0:T(8,128)(2,1)S(1)}, bf16[512,512]{1,0:T(8,128)(2,1)S(1)}, u32[]{:S(2)}, u32[]{:S(2)}) %collective-permute-start.14) | collective-permute-done | bytes 524320 | tf_op jit(solution)/shard_map/ppermute | solution.py:311
  49.2 0.1 collective-permute-done.7.refs_2_.t2
  49.3 0.5 collective-permute-start.12
  49.8 1.9 %collective-permute-done.8.refs_3_.t3 = bf16[12,128,128]{2,1,0:T(8,128)(2,1)S(1)} collective-permute-done((bf16[12,128,128]{2,1,0:T(8,128)(2,1)S(1)}, bf16[12,128,128]{2,1,0:T(8,128)(2,1)S(1)}, u32[]{:S(2)}, u32[]{:S(2)}) %collective-permute-start.8) | collective-permute-done | bytes 393248 | tf_op jit(solution)/shard_map/ppermute | solution.py:318
  51.8 1.7 %collective-permute-done.13.refs_7_ = bf16[12,128,128]{2,1,0:T(8,128)(2,1)S(1)} collective-permute-done((bf16[12,128,128]{2,1,0:T(8,128)(2,1)S(1)}, bf16[12,128,128]{2,1,0:T(8,128)(2,1)S(1)}, u32[]{:S(2)}, u32[]{:S(2)}) %collective-permute-start.13) | collective-permute-done | bytes 393248 | tf_op jit(solution)/shard_map/ppermute | solution.py:321
  53.5 1.1 %turn.1.alpha = bf16[4,512,512]{2,1,0:T(8,128)(2,1)S(1)} custom-call(s32[5]{0:T(128)S(1)} %copy-done.4, bf16[12,128,128]{2,1,0:T(8,128)(2,1)S(1)} %get-tuple-element.28.refs_0_, bf16[16,128,128]{2,1,0:T(8,128)(2,1)S(1)} %collective-permute-done.6.refs_1_.t1, bf16[12,128,128]{2,1,0:T(8,128)(2,1)S(1)} %collective-permute-done.7.refs_2_.t2, ...), custom_call_target="tpu_custom_call" | custom-call | flops 1 | bytes 1 | tf_op jit(solution)/shard_map/turn/pallas_call | solution.py:180
  54.6 5.0 %collective-permute-done.15.s3 = bf16[512,512]{1,0:T(8,128)(2,1)S(1)} collective-permute-done((bf16[512,512]{1,0:T(8,128)(2,1)S(1)}, bf16[512,512]{1,0:T(8,128)(2,1)S(1)}, u32[]{:S(2)}, u32[]{:S(2)}) %collective-permute-start.15) | collective-permute-done | bytes 524320 | tf_op jit(solution)/shard_map/ppermute | solution.py:317
  59.6 2.1 %expect.1 = (f32[4,128,512]{2,1,0:T(8,128)S(1)}, f32[4,1,128]{2,1,0:T(1,128)S(1)}, bf16[128,512]{1,0:T(8,128)(2,1)S(1)}, bf16[128,512]{1,0:T(8,128)(2,1)S(1)}, bf16[128,512]{1,0:T(8,128)(2,1)S(1)}) custom-call(s32[5]{0:T(128)S(1)} %copy-done.4, bf16[4,512,512]{2,1,0:T(8,128)(2,1)S(1)} %turn.1.alpha, bf16[512,512]{1,0:T(8,128)(2,1)S(1)} %bitcast.13, ...), custom_call_target="tpu_custom_call" | custom-call | flops 1 | bytes 1 | tf_op jit(solution)/shard_map/expect/pallas_call | solution.py:217
  61.7 0.1 collective-permute-start.19
  61.8 1.1 %collective-permute-done.19 = f32[4,1,128]{2,1,0:T(1,128)S(1)} collective-permute-done((f32[4,1,128]{2,1,0:T(1,128)S(1)}, f32[4,1,128]{2,1,0:T(1,128)S(1)}, u32[]{:S(2)}, u32[]{:S(2)}) %collective-permute-start.19) | collective-permute-done | bytes 2080 | tf_op jit(solution)/shard_map/ppermute | solution.py:325
  63.0 0.6 broadcast_in_dim.16
  63.6 8.7 %all-to-all-start.1 = ((f32[32,1,128]{2,1,0:T(1,128)}), f32[32,1,128]{2,1,0:T(1,128)S(1)}, u32[]{:S(2)}, u32[]{:S(2)}) async-start(f32[32,1,128]{2,1,0:T(1,128)} %bitcast.10), calls=%async_computation.1 | async-start | bytes 32768 | tf_op jit(solution)/shard_map/all_to_all | solution.py:327
  72.2 1.5 %collective-permute-start.16 = (bf16[128,512]{1,0:T(8,128)(2,1)S(1)}, bf16[128,512]{1,0:T(8,128)(2,1)S(1)}, u32[]{:S(2)}, u32[]{:S(2)}) collective-permute-start(bf16[128,512]{1,0:T(8,128)(2,1)S(1)} %get-tuple-element.38), channel_id=1, source_target_pairs={{0,16},{16,32},{32,48},{48,0},{1,17},{17,33},{33,49},{49,1},{2,18}... | collective-permute-start | bytes 393224 | tf_op jit(solution)/shard_map/ppermute | solution.py:328
  73.8 0.8 collective-permute-start.17
  74.6 2.4 %collective-permute-start.18 = (bf16[128,512]{1,0:T(8,128)(2,1)S(1)}, bf16[128,512]{1,0:T(8,128)(2,1)S(1)}, u32[]{:S(2)}, u32[]{:S(2)}) collective-permute-start(bf16[128,512]{1,0:T(8,128)(2,1)S(1)} %get-tuple-element.40), channel_id=1, source_target_pairs={{0,48},{16,0},{32,16},{48,32},{1,49},{17,1},{33,17},{49,33},{2,50}... | collective-permute-start | bytes 393224 | tf_op jit(solution)/shard_map/ppermute | solution.py:328
  77.1 3.7 %all-to-all-done.1.sums = f32[32,1,128]{2,1,0:T(1,128)S(1)} async-done(((f32[32,1,128]{2,1,0:T(1,128)}), f32[32,1,128]{2,1,0:T(1,128)S(1)}, u32[]{:S(2)}, u32[]{:S(2)}) %all-to-all-start.1) | async-done | bytes 16416 | tf_op jit(solution)/shard_map/all_to_all | solution.py:327
  80.8 0.1 column.1.rate
  80.9 0.7 collective-permute-done.17.e2
  81.6 0.7 collective-permute-done.18.e3
  82.3 1.8 %finish.1 = (f32[128,2048]{1,0:T(8,128)}, bf16[128,2048]{1,0:T(8,128)(2,1)}) custom-call(s32[5]{0:T(128)S(1)} %copy-done.4, bf16[128,2048]{1,0:T(8,128)(2,1)S(1)} %copy-done, f32[4,128,512]{2,1,0:T(8,128)S(1)} %get-tuple-element.37.total, bf16[128,512]{1,0:T(8,128)(2,1)S(1)} %collective-permute-done.16.e1, bf16[128,512]{1,0:T(8,128)(2,1)S(1)} %collective-permute-done.17.e2, ...), custom_call_target="tpu_custom_call" | custom-call | flops 1 | bytes 1 | tf_op jit(solution)/shard_map/finish/pallas_call | solution.py:270
  (22 shorter events, 0.1 us)
Async XLA Ops:
  0.6 13.9 %copy-start.2 = (bf16[128,128]{1,0:T(8,128)(2,1)S(1)}, bf16[128,128]{1,0:T(8,128)(2,1)}, u32[]{:S(2)}) copy-start(bf16[128,128]{1,0:T(8,128)(2,1)} %param.6) | copy-start | bytes 98308
  0.7 1.0 %copy-start.1 = (bf16[128,2048]{1,0:T(8,128)(2,1)S(1)}, bf16[128,2048]{1,0:T(8,128)(2,1)}, u32[]{:S(2)}) copy-start(bf16[128,2048]{1,0:T(8,128)(2,1)} %a.1) | copy-start | bytes 1572868
  1.8 7.3 %copy-start.3 = (s32[5]{0:T(128)}, s32[5]{0:T(128)S(1)}, u32[]{:S(2)}) copy-start(s32[5]{0:T(128)S(1)} %stack.23.pos) | copy-start | bytes 64
  2.4 12.2 %collective-permute-start.1 = (bf16[128,512]{1,0:T(8,128)(2,1)S(1)}, bf16[128,512]{1,0:T(8,128)(2,1)S(1)}, u32[]{:S(2)}, u32[]{:S(2)}) collective-permute-start(bf16[128,512]{1,0:T(8,128)(2,1)S(1)} %get-tuple-element.23), channel_id=1, source_target_pairs={{0,16},{16,32},{32,48},{48,0},{1,17},{17,33},{33,49},{49,1},{2,18}... | collective-permute-start | bytes 393224 | tf_op jit(solution)/shard_map/ppermute | solution.py:302
  3.9 10.6 %collective-permute-start.2 = (bf16[128,512]{1,0:T(8,128)(2,1)S(1)}, bf16[128,512]{1,0:T(8,128)(2,1)S(1)}, u32[]{:S(2)}, u32[]{:S(2)}) collective-permute-start(bf16[128,512]{1,0:T(8,128)(2,1)S(1)} %get-tuple-element.24), channel_id=1, source_target_pairs={{0,32},{16,48},{32,0},{48,16},{1,33},{17,49},{33,1},{49,17},{2,34}... | collective-permute-start | bytes 393224 | tf_op jit(solution)/shard_map/ppermute | solution.py:302
  6.8 7.8 %collective-permute-start.3 = (bf16[128,512]{1,0:T(8,128)(2,1)S(1)}, bf16[128,512]{1,0:T(8,128)(2,1)S(1)}, u32[]{:S(2)}, u32[]{:S(2)}) collective-permute-start(bf16[128,512]{1,0:T(8,128)(2,1)S(1)} %get-tuple-element.25), channel_id=1, source_target_pairs={{0,48},{16,0},{32,16},{48,32},{1,49},{17,1},{33,17},{49,33},{2,50}... | collective-permute-start | bytes 393224 | tf_op jit(solution)/shard_map/ppermute | solution.py:302
  7.2 7.3 %collective-permute-start = (bf16[1,128,128]{2,1,0:T(8,128)(2,1)}, bf16[1,128,128]{2,1,0:T(8,128)(2,1)S(1)}, u32[]{:S(2)}, u32[]{:S(2)}) collective-permute-start(bf16[1,128,128]{2,1,0:T(8,128)(2,1)} %bitcast.14), channel_id=1, source_target_pairs={{0,2},{2,0},{4,6},{6,4},{8,10},{10,8},{12,14},{14,12},{1,3},{3,1},... | collective-permute-start | bytes 98312 | tf_op jit(solution)/shard_map/ppermute | solution.py:299
  14.6 9.3 %collective-permute-start.4 = (bf16[2,128,128]{2,1,0:T(8,128)(2,1)S(1)}, bf16[2,128,128]{2,1,0:T(8,128)(2,1)S(1)}, u32[]{:S(2)}, u32[]{:S(2)}) collective-permute-start(bf16[2,128,128]{2,1,0:T(8,128)(2,1)S(1)} %pad_maximum_fusion), channel_id=1, source_target_pairs={{0,4},{2,6},{4,0},{6,2},{8,12},{10,14},{12,8},{14,10},{1,5},{3,7},... | collective-permute-start | bytes 196616 | tf_op jit(solution)/shard_map/ppermute | solution.py:299
  17.9 14.8 %all-to-all-start = ((bf16[16,32,512]{2,1,0:T(8,128)(2,1)}), bf16[16,32,512]{2,1,0:T(8,128)(2,1)S(1)}, u32[]{:S(2)}, u32[]{:S(2)}) async-start(bf16[16,32,512]{2,1,0:T(8,128)(2,1)} %bitcast.20), calls=%async_computation | async-start | bytes 1048576 | tf_op jit(solution)/shard_map/all_to_all | solution.py:306
  23.9 6.5 %copy-start = (bf16[128,2048]{1,0:T(8,128)(2,1)S(1)}, bf16[128,2048]{1,0:T(8,128)(2,1)}, u32[]{:S(2)}) copy-start(bf16[128,2048]{1,0:T(8,128)(2,1)} %transition.5) | copy-start | bytes 1572868
  23.9 6.5 %copy-start.4 = (s32[5]{0:T(128)S(1)}, s32[5]{0:T(128)}, u32[]{:S(2)}) copy-start(s32[5]{0:T(128)} %copy-done.3) | copy-start | bytes 64
  23.9 8.8 %copy-start.5 = (s32[2048]{0:T(1024)S(1)}, s32[2048]{0:T(1024)}, u32[]{:S(2)}) copy-start(s32[2048]{0:T(1024)} %param.5) | copy-start | bytes 24580
  23.9 6.4 %collective-permute-start.5 = (bf16[4,128,128]{2,1,0:T(8,128)(2,1)S(1)}, bf16[4,128,128]{2,1,0:T(8,128)(2,1)S(1)}, u32[]{:S(2)}, u32[]{:S(2)}) collective-permute-start(bf16[4,128,128]{2,1,0:T(8,128)(2,1)S(1)} %join.1), channel_id=1, source_target_pairs={{0,14},{2,12},{4,10},{6,8},{8,6},{10,4},{12,2},{14,0},{1,15},{3,13... | collective-permute-start | bytes 393224 | tf_op jit(solution)/shard_map/ppermute | solution.py:299
  31.1 11.8 %collective-permute-start.6 = (bf16[16,128,128]{2,1,0:T(8,128)(2,1)S(1)}, bf16[16,128,128]{2,1,0:T(8,128)(2,1)S(1)}, u32[]{:S(2)}, u32[]{:S(2)}) collective-permute-start(bf16[16,128,128]{2,1,0:T(8,128)(2,1)S(1)} %get-tuple-element.29), channel_id=1, source_target_pairs={{0,16},{1,49},{16,32},{17,1},{32,48},{33,17},{48,0},{49,33},{2,18}... | collective-permute-start | bytes 1572872 | tf_op jit(solution)/shard_map/ppermute | solution.py:314
  34.3 14.9 %collective-permute-start.14 = (bf16[512,512]{1,0:T(8,128)(2,1)S(1)}, bf16[512,512]{1,0:T(8,128)(2,1)S(1)}, u32[]{:S(2)}, u32[]{:S(2)}) collective-permute-start(bf16[512,512]{1,0:T(8,128)(2,1)S(1)} %bitcast.11), channel_id=1, source_target_pairs={{0,64},{1,193},{64,128},{65,1},{128,192},{129,65},{192,0},{193,129... | collective-permute-start | bytes 1572872 | tf_op jit(solution)/shard_map/ppermute | solution.py:311
  35.7 13.6 %collective-permute-start.9 = (bf16[512,512]{1,0:T(8,128)(2,1)S(1)}, bf16[512,512]{1,0:T(8,128)(2,1)S(1)}, u32[]{:S(2)}, u32[]{:S(2)}) collective-permute-start(bf16[512,512]{1,0:T(8,128)(2,1)S(1)} %bitcast.12), channel_id=1, source_target_pairs={{64,0},{193,1},{128,64},{1,65},{192,128},{65,129},{0,192},{129,193... | collective-permute-start | bytes 1572872 | tf_op jit(solution)/shard_map/ppermute | solution.py:312
  37.6 11.7 %collective-permute-start.7 = (bf16[12,128,128]{2,1,0:T(8,128)(2,1)S(1)}, bf16[12,128,128]{2,1,0:T(8,128)(2,1)S(1)}, u32[]{:S(2)}, u32[]{:S(2)}) collective-permute-start(bf16[12,128,128]{2,1,0:T(8,128)(2,1)S(1)} %get-tuple-element.28.refs_0_), channel_id=1, source_target_pairs={{16,0},{49,1},{32,16},{1,17},{48,32},{17,33},{0,48},{33,49},{18,2}... | collective-permute-start | bytes 1179656 | tf_op jit(solution)/shard_map/ppermute | solution.py:315
  42.9 8.9 %collective-permute-start.8 = (bf16[12,128,128]{2,1,0:T(8,128)(2,1)S(1)}, bf16[12,128,128]{2,1,0:T(8,128)(2,1)S(1)}, u32[]{:S(2)}, u32[]{:S(2)}) collective-permute-start(bf16[12,128,128]{2,1,0:T(8,128)(2,1)S(1)} %slice.4), channel_id=1, source_target_pairs={{0,16},{1,49},{16,32},{17,1},{32,48},{33,17},{48,0},{49,33},{2,18}... | collective-permute-start | bytes 1179656 | tf_op jit(solution)/shard_map/ppermute | solution.py:318
  45.4 6.4 %collective-permute-start.11 = (bf16[16,128,128]{2,1,0:T(8,128)(2,1)S(1)}, bf16[16,128,128]{2,1,0:T(8,128)(2,1)S(1)}, u32[]{:S(2)}, u32[]{:S(2)}) collective-permute-start(bf16[16,128,128]{2,1,0:T(8,128)(2,1)S(1)} %collective-permute-done.6.refs_1_.t1), channel_id=1, source_target_pairs={{0,1},{1,0},{2,3},{3,2},{4,5},{5,4},{6,7},{7,6},{8,9},{9,8},{10,11... | collective-permute-start | bytes 1572872 | tf_op jit(solution)/shard_map/ppermute | solution.py:321
  49.2 10.4 %collective-permute-start.15 = (bf16[512,512]{1,0:T(8,128)(2,1)S(1)}, bf16[512,512]{1,0:T(8,128)(2,1)S(1)}, u32[]{:S(2)}, u32[]{:S(2)}) collective-permute-start(bf16[512,512]{1,0:T(8,128)(2,1)S(1)} %collective-permute-done.14.s1), channel_id=1, source_target_pairs={{0,64},{1,193},{64,128},{65,1},{128,192},{129,65},{192,0},{193,129... | collective-permute-start | bytes 1572872 | tf_op jit(solution)/shard_map/ppermute | solution.py:317
  49.3 2.4 %collective-permute-start.10 = (bf16[12,128,128]{2,1,0:T(8,128)(2,1)S(1)}, bf16[12,128,128]{2,1,0:T(8,128)(2,1)S(1)}, u32[]{:S(2)}, u32[]{:S(2)}) collective-permute-start(bf16[12,128,128]{2,1,0:T(8,128)(2,1)S(1)} %get-tuple-element.28.refs_0_), channel_id=1, source_target_pairs={{0,1},{1,0},{2,3},{3,2},{4,5},{5,4},{6,7},{7,6},{8,9},{9,8},{10,11... | collective-permute-start | bytes 1179656 | tf_op jit(solution)/shard_map/ppermute | solution.py:321
  49.3 2.4 %collective-permute-start.12 = (bf16[12,128,128]{2,1,0:T(8,128)(2,1)S(1)}, bf16[12,128,128]{2,1,0:T(8,128)(2,1)S(1)}, u32[]{:S(2)}, u32[]{:S(2)}) collective-permute-start(bf16[12,128,128]{2,1,0:T(8,128)(2,1)S(1)} %collective-permute-done.7.refs_2_.t2), channel_id=1, source_target_pairs={{0,1},{1,0},{2,3},{3,2},{4,5},{5,4},{6,7},{7,6},{8,9},{9,8},{10,11... | collective-permute-start | bytes 1179656 | tf_op jit(solution)/shard_map/ppermute | solution.py:321
  51.7 1.7 %collective-permute-start.13 = (bf16[12,128,128]{2,1,0:T(8,128)(2,1)S(1)}, bf16[12,128,128]{2,1,0:T(8,128)(2,1)S(1)}, u32[]{:S(2)}, u32[]{:S(2)}) collective-permute-start(bf16[12,128,128]{2,1,0:T(8,128)(2,1)S(1)} %collective-permute-done.8.refs_3_.t3), channel_id=1, source_target_pairs={{0,1},{1,0},{2,3},{3,2},{4,5},{5,4},{6,7},{7,6},{8,9},{9,8},{10,11... | collective-permute-start | bytes 1179656 | tf_op jit(solution)/shard_map/ppermute | solution.py:321
  61.7 1.2 %collective-permute-start.19 = (f32[4,1,128]{2,1,0:T(1,128)S(1)}, f32[4,1,128]{2,1,0:T(1,128)S(1)}, u32[]{:S(2)}, u32[]{:S(2)}) collective-permute-start(f32[4,1,128]{2,1,0:T(1,128)S(1)} %get-tuple-element.41), channel_id=1, source_target_pairs={{0,1},{1,0},{2,3},{3,2},{4,5},{5,4},{6,7},{7,6},{8,9},{9,8},{10,11... | collective-permute-start | bytes 6152 | tf_op jit(solution)/shard_map/ppermute | solution.py:325
  63.6 17.2 %all-to-all-start.1 = ((f32[32,1,128]{2,1,0:T(1,128)}), f32[32,1,128]{2,1,0:T(1,128)S(1)}, u32[]{:S(2)}, u32[]{:S(2)}) async-start(f32[32,1,128]{2,1,0:T(1,128)} %bitcast.10), calls=%async_computation.1 | async-start | bytes 32768 | tf_op jit(solution)/shard_map/all_to_all | solution.py:327
  72.2 8.7 %collective-permute-start.16 = (bf16[128,512]{1,0:T(8,128)(2,1)S(1)}, bf16[128,512]{1,0:T(8,128)(2,1)S(1)}, u32[]{:S(2)}, u32[]{:S(2)}) collective-permute-start(bf16[128,512]{1,0:T(8,128)(2,1)S(1)} %get-tuple-element.38), channel_id=1, source_target_pairs={{0,16},{16,32},{32,48},{48,0},{1,17},{17,33},{33,49},{49,1},{2,18}... | collective-permute-start | bytes 393224 | tf_op jit(solution)/shard_map/ppermute | solution.py:328
  73.8 7.8 %collective-permute-start.17 = (bf16[128,512]{1,0:T(8,128)(2,1)S(1)}, bf16[128,512]{1,0:T(8,128)(2,1)S(1)}, u32[]{:S(2)}, u32[]{:S(2)}) collective-permute-start(bf16[128,512]{1,0:T(8,128)(2,1)S(1)} %get-tuple-element.39), channel_id=1, source_target_pairs={{0,32},{16,48},{32,0},{48,16},{1,33},{17,49},{33,1},{49,17},{2,34}... | collective-permute-start | bytes 393224 | tf_op jit(solution)/shard_map/ppermute | solution.py:328
  74.6 7.7 %collective-permute-start.18 = (bf16[128,512]{1,0:T(8,128)(2,1)S(1)}, bf16[128,512]{1,0:T(8,128)(2,1)S(1)}, u32[]{:S(2)}, u32[]{:S(2)}) collective-permute-start(bf16[128,512]{1,0:T(8,128)(2,1)S(1)} %get-tuple-element.40), channel_id=1, source_target_pairs={{0,48},{16,0},{32,16},{48,32},{1,49},{17,1},{33,17},{49,33},{2,50}... | collective-permute-start | bytes 393224 | tf_op jit(solution)/shard_map/ppermute | solution.py:328

commit v4 on v3

--- a/solution.py
+++ b/solution.py
@@ -80,11 +80,9 @@
     )(pos, ids, emission)
 
 
-def scale_kernel(pos, ids, rows, c0, c1, c2, c3, out, wide):
-    wide[...] = rows[...].astype(F32)
+def moves_kernel(pos, ids, out):
     before = (iota((128, 128), 0) < iota((128, 128), 1)).astype(BF16)
-    for d, c in enumerate((c0, c1, c2, c3)):
-        block = (pos[2] - d + 4) & 3
+    for block in range(4):
         word = ids[pl.ds(pos[1] * 4 + block, 1), :]
         wordb = jnp.broadcast_to(word, (16, 128))
         owner_at = iota((16, 128), 0)
@@ -93,13 +91,31 @@
         earlier = jnp.dot(ownf.astype(BF16), before, preferred_element_type=F32)
         place = ownf * (earlier + (owner_at * 8).astype(F32))
         slot = jnp.sum(place, axis=0, keepdims=True).astype(jnp.int32)
-        move = (iota((128, 128), 0) == slot).astype(F32).astype(BF16)
+        out[block] = (iota((128, 128), 0) == slot).astype(F32).T.astype(BF16)
+
+
+def moves(pos, ids):
+    return pl.pallas_call(
+        moves_kernel,
+        in_specs=[SM, VM],
+        out_specs=VM,
+        out_shape=jax.ShapeDtypeStruct((4, 128, 128), BF16),
+        compiler_params=params(8),
+        cost_estimate=SMALL,
+        name="moves",
+    )(pos, ids)
+
+
+def scale_kernel(pos, move, rows, c0, c1, c2, c3, out, wide):
+    wide[...] = rows[...].astype(F32)
+    for d, c in enumerate((c0, c1, c2, c3)):
+        block = (pos[2] - d + 4) & 3
         given = wide[:, pl.ds(pl.multiple_of(block * 8, 8), 8), :].reshape(128, 512).astype(BF16)
-        emitted = lax.dot_general(move, given, (((0,), (0,)), ((), ())), preferred_element_type=F32)
+        emitted = jnp.dot(move[block], given, preferred_element_type=F32)
         out[block] = (emitted * c[...].astype(F32)).astype(BF16)
 
 
-def scale(pos, ids, rows, cuts):
+def scale(pos, move, rows, cuts):
     return pl.pallas_call(
         scale_kernel,
         in_specs=[SM] + [VM] * 6,
@@ -109,7 +125,7 @@
         compiler_params=params(16),
         cost_estimate=pl.CostEstimate(flops=10**10, bytes_accessed=10**7, transcendentals=0),
         name="scale",
-    )(pos, ids, rows, *cuts)
+    )(pos, move, rows, *cuts)
 
 
 def quarter(pos, transition, away):
@@ -167,9 +183,9 @@
     for c in range(2):
         core = pos[3] ^ c
         step = 1 - 2 * core
-        for n, (away, first) in enumerate(((0, 4), (-step, 4), (step, 4), (2, 0))):
+        for n, (away, first) in enumerate(((0, 4), (-step, 4 - 4 * c), (step, 4), (2, 0))):
             x = (pos[2] + away + 4) & 3
-            for m, flip in enumerate((0, 1, 2, 3, 7, 6, 5, 4)):
+            for m, flip in enumerate((0, 2, 6, 4, 1, 3, 7, 5)):
                 block = (pos[4] ^ flip) * 2 + core
                 rows = pl.ds(pl.multiple_of(x * 128, 128), 128)
                 times = pl.ds(pl.multiple_of((block & 3) * 128, 128), 128)
@@ -298,27 +314,30 @@
     together = lax.optimization_barrier
     flip = lambda a, by: lax.ppermute(a, "z", [(i, i ^ by) for i in range(8)])
 
-    line = [alpha[None], flip(alpha[None], 1)]
+    line = [alpha[None], flip(alpha[None], 2)]
     betas = [c if d == 0 else lax.ppermute(c, "x", ring(d)) for d, c in enumerate(cut(pos, beta))]
     picked = pick(pos, ids, emission)
     picked, line, betas = together((picked, line, betas))
 
     rows = lax.all_to_all(picked.reshape(16, 32, 512), ("y", "x"), 0, 0)
-    line.append(flip(jnp.concatenate(line), 2))
-    line.append(flip(join(line), 7))
-    own = scale(pos, ids, rows, betas).reshape(512, 512)
+    line.append(flip(jnp.concatenate(line), 6))
+    line.append(flip(join(line), 1))
+    ids, _ = together((ids, line[2]))
+    own = scale(pos, moves(pos, ids), rows, betas).reshape(512, 512)
 
     one = lax.ppermute(own, ("y", "k"), ahead)
     two = lax.ppermute(own, ("y", "k"), behind)
     to_a, to_b = pack(pos, line, transition)
     one_a = lax.ppermute(to_a, ("x", "k"), ahead)
-    two_a = lax.ppermute(to_b, ("x", "k"), behind)
+    later, one_a = together((to_b, one_a))
+    two_a = lax.ppermute(later, ("x", "k"), behind)
 
     far = lax.ppermute(one, ("y", "k"), ahead)
-    far_a = lax.ppermute(one_a[4:], ("x", "k"), ahead)
-    far_a, two = together((far_a, two))
+    one_c = one_a[4:]
+    far_a = lax.ppermute(one_c, ("x", "k"), ahead)
+    one_c, far_a, two = together((one_c, far_a, two))
     sources = [to_b, one_a, two_a, far_a]
-    sources += [lax.ppermute(a, "k", swap) for a in sources]
+    sources += [lax.ppermute(a, "k", swap) for a in (to_b, one_c, two_a, far_a)]
     alpha_t = turn(pos, sources)
 
     total, sums, *parts = expect(pos, alpha_t, (own, one, two, far), transition, (one_a, two_a, far_a))

time: 84.5 us -> 81.3 us (0.962)
  starting transfers between devices: 42.3 us -> 37.4 us
  waiting for transfers between devices: 25.8 us -> 27.3 us
    all_to_all x1, starting transfers between devices: 8.66 us -> 5.25 us  [per_device(): sums = lax.all_to_all(sums, ('x', 'z'), 0, 0)]
    ppermute x1, waiting for transfers between devices: 3.83 us -> 1.72 us  [per_device(): one_a = lax.ppermute(to_a, ('x', 'k'), ahead)]
    ppermute x6, starting transfers between devices: 4.4 us -> 2.62 us  [the longest x1 1.54 us: per_device(): far_a = lax.ppermute(one_c, ('x', 'k'), ahead)]
    ppermute x1, waiting for transfers between devices: 3.88 us -> 5.53 us  [per_device(): one = lax.ppermute(own, ('y', 'k'), ahead)]
    all_to_all x1, waiting for transfers between devices: 0.09 us -> 1.74 us  [per_device(): rows = lax.all_to_all(picked.reshape(16, 32, 512), ('y', 'x'), 0, 0)]
    ppermute x1, starting transfers between devices: 1.45 us -> 0.08 us  [per_device(): one = lax.ppermute(own, ('y', 'k'), ahead)]
    ppermute x1, starting transfers between devices: 1.86 us -> 3.22 us  [per_device(): two = lax.ppermute(own, ('y', 'k'), behind)]
  transfers between devices with their start and end apart: 22 -> 22, of which waited for: 12 -> 13; matrix products, arithmetic and copies ran while one was open for 0% -> 0% of each run, Pallas kernels for 11% -> 11%
where the time goes in v4:
time: 81.3 us; the launch traced here: 80.9 us
  starting transfers between devices  37.4 us (46%)
  waiting for transfers between devices  27.3 us (34%)
  Pallas kernels  13.5 us (17%)
  local copies, waits for them, and re-layouts  1.79 us (2%)
  between operations  1.01 us (1%)
    ppermute x3, starting transfers between devices, per_device(): flip = lambda a, by: lax.ppermute(a, 'z', [(i, i ^ by) for i in range(8)])  8.95 us
    all_to_all x1, starting transfers between devices, per_device(): rows = lax.all_to_all(picked.reshape(16, 32, 512), ('y', 'x'), 0, 0)  5.94 us
    ppermute x1, waiting for transfers between devices, per_device(): one = lax.ppermute(own, ('y', 'k'), ahead)  5.53 us
    pallas_call x1, Pallas kernels, pick(): pl.pallas_call(pick_kernel, in_specs=[SM, VM, pl.BlockSpec(memory_space=p...  5.38 us
    all_to_all x1, starting transfers between devices, per_device(): sums = lax.all_to_all(sums, ('x', 'z'), 0, 0)  5.25 us
    ppermute x3, starting transfers between devices, per_device(): lax.ppermute(c, 'x', ring(d))  4.83 us
    ppermute x3, starting transfers between devices, per_device(): parts = [lax.ppermute(e, 'x', ring(d)) for d, e in enumerate(parts, 1)]  4.82 us
    ppermute x1, waiting for transfers between devices, per_device(): far = lax.ppermute(one, ('y', 'k'), ahead)  4.43 us
  transfers between devices with their start and end apart: 22, of which 13 were waited for; matrix products, arithmetic and copies ran while one was open for 0% of the time, Pallas kernels for 11%

profile of v4, /device:TPU:2, one launch (start us, length us, event | category | flops | bytes accessed | tf_op | source)
XLA Modules:
  0.0 80.9 jit_solution(15712191156567454705)
XLA Ops:
  0.6 0.0 copy-start.2
  0.6 0.1 stack.23.pos
  0.7 1.0 %copy-done.1 = bf16[128,2048]{1,0:T(8,128)(2,1)S(1)} copy-done((bf16[128,2048]{1,0:T(8,128)(2,1)S(1)}, bf16[128,2048]{1,0:T(8,128)(2,1)}, u32[]{:S(2)}) %copy-start.1) | copy-done | bytes 524312
  1.8 0.6 cut.1
  2.4 1.6 %collective-permute-start.1 = (bf16[128,512]{1,0:T(8,128)(2,1)S(1)}, bf16[128,512]{1,0:T(8,128)(2,1)S(1)}, u32[]{:S(2)}, u32[]{:S(2)}) collective-permute-start(bf16[128,512]{1,0:T(8,128)(2,1)S(1)} %get-tuple-element.27), channel_id=1, source_target_pairs={{0,16},{16,32},{32,48},{48,0},{1,17},{17,33},{33,49},{49,1},{2,18}... | collective-permute-start | bytes 393224 | tf_op jit(solution)/shard_map/ppermute | solution.py:318
  3.9 2.8 %collective-permute-start.2 = (bf16[128,512]{1,0:T(8,128)(2,1)S(1)}, bf16[128,512]{1,0:T(8,128)(2,1)S(1)}, u32[]{:S(2)}, u32[]{:S(2)}) collective-permute-start(bf16[128,512]{1,0:T(8,128)(2,1)S(1)} %get-tuple-element.28), channel_id=1, source_target_pairs={{0,32},{16,48},{32,0},{48,16},{1,33},{17,49},{33,1},{49,17},{2,34}... | collective-permute-start | bytes 393224 | tf_op jit(solution)/shard_map/ppermute | solution.py:318
  6.8 0.4 collective-permute-start.3
  7.2 3.3 %collective-permute-start = (bf16[1,128,128]{2,1,0:T(8,128)(2,1)}, bf16[1,128,128]{2,1,0:T(8,128)(2,1)S(1)}, u32[]{:S(2)}, u32[]{:S(2)}) collective-permute-start(bf16[1,128,128]{2,1,0:T(8,128)(2,1)} %bitcast.14), channel_id=1, source_target_pairs={{0,4},{2,6},{4,0},{6,2},{8,12},{10,14},{12,8},{14,10},{1,5},{3,7},... | collective-permute-start | bytes 98312 | tf_op jit(solution)/shard_map/ppermute | solution.py:315
  10.5 5.4 %pick.1 = bf16[4,4,32,512]{3,2,1,0:T(8,128)(2,1)} custom-call(s32[5]{0:T(128)} %copy-done.4, s32[16,128]{1,0:T(8,128)} %bitcast.18, bf16[2000,2048]{1,0:T(8,128)(2,1)} %table.1), custom_call_target="tpu_custom_call" | custom-call | flops 1 | bytes 1 | tf_op jit(solution)/shard_map/pick/pallas_call | solution.py:71
  15.9 4.6 %collective-permute-start.4 = (bf16[2,128,128]{2,1,0:T(8,128)(2,1)S(1)}, bf16[2,128,128]{2,1,0:T(8,128)(2,1)S(1)}, u32[]{:S(2)}, u32[]{:S(2)}) collective-permute-start(bf16[2,128,128]{2,1,0:T(8,128)(2,1)S(1)} %pad_maximum_fusion), channel_id=1, source_target_pairs={{0,12},{2,14},{4,8},{6,10},{8,4},{10,6},{12,0},{14,2},{1,13},{3,15... | collective-permute-start | bytes 196616 | tf_op jit(solution)/shard_map/ppermute | solution.py:315
  20.5 5.9 %all-to-all-start = ((bf16[16,32,512]{2,1,0:T(8,128)(2,1)}), bf16[16,32,512]{2,1,0:T(8,128)(2,1)S(1)}, u32[]{:S(2)}, u32[]{:S(2)}) async-start(bf16[16,32,512]{2,1,0:T(8,128)(2,1)} %bitcast.20), calls=%async_computation | async-start | bytes 1048576 | tf_op jit(solution)/shard_map/all_to_all | solution.py:322
  26.4 0.0 copy-start.5
  26.5 0.0 copy-start
  26.5 1.1 %collective-permute-start.5 = (bf16[4,128,128]{2,1,0:T(8,128)(2,1)S(1)}, bf16[4,128,128]{2,1,0:T(8,128)(2,1)S(1)}, u32[]{:S(2)}, u32[]{:S(2)}) collective-permute-start(bf16[4,128,128]{2,1,0:T(8,128)(2,1)S(1)} %join.1), channel_id=1, source_target_pairs={{0,2},{2,0},{4,6},{6,4},{8,10},{10,8},{12,14},{14,12},{1,3},{3,1},... | collective-permute-start | bytes 393224 | tf_op jit(solution)/shard_map/ppermute | solution.py:315
  27.6 0.8 moves.1.move
  28.4 3.1 %collective-permute-done.5.l3 = bf16[4,128,128]{2,1,0:T(8,128)(2,1)S(1)} collective-permute-done((bf16[4,128,128]{2,1,0:T(8,128)(2,1)S(1)}, bf16[4,128,128]{2,1,0:T(8,128)(2,1)S(1)}, u32[]{:S(2)}, u32[]{:S(2)}) %collective-permute-start.5) | collective-permute-done | bytes 131104 | tf_op jit(solution)/shard_map/ppermute | solution.py:315
  31.6 0.7 pack.1
  32.2 1.5 %collective-permute-start.6 = (bf16[16,128,128]{2,1,0:T(8,128)(2,1)S(1)}, bf16[16,128,128]{2,1,0:T(8,128)(2,1)S(1)}, u32[]{:S(2)}, u32[]{:S(2)}) collective-permute-start(bf16[16,128,128]{2,1,0:T(8,128)(2,1)S(1)} %get-tuple-element.33), channel_id=1, source_target_pairs={{0,16},{1,49},{16,32},{17,1},{32,48},{33,17},{48,0},{49,33},{2,18}... | collective-permute-start | bytes 1572872 | tf_op jit(solution)/shard_map/ppermute | solution.py:331
  33.8 1.7 %all-to-all-done.rows = bf16[16,32,512]{2,1,0:T(8,128)(2,1)S(1)} async-done(((bf16[16,32,512]{2,1,0:T(8,128)(2,1)}), bf16[16,32,512]{2,1,0:T(8,128)(2,1)S(1)}, u32[]{:S(2)}, u32[]{:S(2)}) %all-to-all-start) | async-done | bytes 524320 | tf_op jit(solution)/shard_map/all_to_all | solution.py:322
  35.5 0.9 %scale.1 = bf16[4,128,512]{2,1,0:T(8,128)(2,1)S(1)} custom-call(s32[5]{0:T(128)S(1)} %copy-done.5, bf16[4,128,128]{2,1,0:T(8,128)(2,1)S(1)} %moves.1.move, bf16[16,32,512]{2,1,0:T(8,128)(2,1)S(1)} %all-to-all-done.rows, bf16[128,512]{1,0:T(8,128)(2,1)S(1)} %get-tuple-element.38.c0, bf16[128,512]{1,0:T(8,128)(2,1)S(1)} %collective-permute-done.1.c1, ...), custom_call_target="tpu_custom_call" | custom-call | flops 10000000000 | bytes 10000000 | tf_op jit(solution)/shard_map/scale/pallas_call | solution.py:119
  36.5 0.1 collective-permute-start.14
  36.5 3.2 %collective-permute-start.9 = (bf16[512,512]{1,0:T(8,128)(2,1)S(1)}, bf16[512,512]{1,0:T(8,128)(2,1)S(1)}, u32[]{:S(2)}, u32[]{:S(2)}) collective-permute-start(bf16[512,512]{1,0:T(8,128)(2,1)S(1)} %bitcast.12), channel_id=1, source_target_pairs={{64,0},{193,1},{128,64},{1,65},{192,128},{65,129},{0,192},{129,193... | collective-permute-start | bytes 1572872 | tf_op jit(solution)/shard_map/ppermute | solution.py:329
  39.8 1.7 %collective-permute-done.6.refs_1_.t1 = bf16[16,128,128]{2,1,0:T(8,128)(2,1)S(1)} collective-permute-done((bf16[16,128,128]{2,1,0:T(8,128)(2,1)S(1)}, bf16[16,128,128]{2,1,0:T(8,128)(2,1)S(1)}, u32[]{:S(2)}, u32[]{:S(2)}) %collective-permute-start.6) | collective-permute-done | bytes 524320 | tf_op jit(solution)/shard_map/ppermute | solution.py:331
  41.5 1.5 %collective-permute-start.8 = (bf16[12,128,128]{2,1,0:T(8,128)(2,1)S(1)}, bf16[12,128,128]{2,1,0:T(8,128)(2,1)S(1)}, u32[]{:S(2)}, u32[]{:S(2)}) collective-permute-start(bf16[12,128,128]{2,1,0:T(8,128)(2,1)S(1)} %slice.3), channel_id=1, source_target_pairs={{0,16},{1,49},{16,32},{17,1},{32,48},{33,17},{48,0},{49,33},{2,18}... | collective-permute-start | bytes 1179656 | tf_op jit(solution)/shard_map/ppermute | solution.py:337
  43.1 0.6 collective-permute-start.7
  43.6 5.5 %collective-permute-done.14.s1 = bf16[512,512]{1,0:T(8,128)(2,1)S(1)} collective-permute-done((bf16[512,512]{1,0:T(8,128)(2,1)S(1)}, bf16[512,512]{1,0:T(8,128)(2,1)S(1)}, u32[]{:S(2)}, u32[]{:S(2)}) %collective-permute-start.14) | collective-permute-done | bytes 524320 | tf_op jit(solution)/shard_map/ppermute | solution.py:328
  49.2 0.0 collective-permute-start.15
  49.2 1.9 %collective-permute-done.8.refs_3_.t3 = bf16[12,128,128]{2,1,0:T(8,128)(2,1)S(1)} collective-permute-done((bf16[12,128,128]{2,1,0:T(8,128)(2,1)S(1)}, bf16[12,128,128]{2,1,0:T(8,128)(2,1)S(1)}, u32[]{:S(2)}, u32[]{:S(2)}) %collective-permute-start.8) | collective-permute-done | bytes 393248 | tf_op jit(solution)/shard_map/ppermute | solution.py:337
  51.1 0.5 collective-permute-start.13
  51.6 0.0 collective-permute-start.12
  51.7 1.2 %collective-permute-done.11.refs_5_ = bf16[12,128,128]{2,1,0:T(8,128)(2,1)S(1)} collective-permute-done((bf16[12,128,128]{2,1,0:T(8,128)(2,1)S(1)}, bf16[12,128,128]{2,1,0:T(8,128)(2,1)S(1)}, u32[]{:S(2)}, u32[]{:S(2)}) %collective-permute-start.11) | collective-permute-done | bytes 393248 | tf_op jit(solution)/shard_map/ppermute | solution.py:340
  52.9 0.6 collective-permute-done.13.refs_7_
  53.4 0.6 collective-permute-done.12.refs_6_
  54.0 1.1 %turn.1.alpha = bf16[4,512,512]{2,1,0:T(8,128)(2,1)S(1)} custom-call(s32[5]{0:T(128)S(1)} %copy-done.5, bf16[12,128,128]{2,1,0:T(8,128)(2,1)S(1)} %get-tuple-element.35.refs_0_, bf16[16,128,128]{2,1,0:T(8,128)(2,1)S(1)} %collective-permute-done.6.refs_1_.t1, bf16[12,128,128]{2,1,0:T(8,128)(2,1)S(1)} %collective-permute-done.7.refs_2_.t2, ...), custom_call_target="tpu_custom_call" | custom-call | flops 1 | bytes 1 | tf_op jit(solution)/shard_map/turn/pallas_call | solution.py:196
  55.1 4.4 %collective-permute-done.15.s3 = bf16[512,512]{1,0:T(8,128)(2,1)S(1)} collective-permute-done((bf16[512,512]{1,0:T(8,128)(2,1)S(1)}, bf16[512,512]{1,0:T(8,128)(2,1)S(1)}, u32[]{:S(2)}, u32[]{:S(2)}) %collective-permute-start.15) | collective-permute-done | bytes 524320 | tf_op jit(solution)/shard_map/ppermute | solution.py:335
  59.5 2.1 %expect.1 = (f32[4,128,512]{2,1,0:T(8,128)S(1)}, f32[4,1,128]{2,1,0:T(1,128)S(1)}, bf16[128,512]{1,0:T(8,128)(2,1)S(1)}, bf16[128,512]{1,0:T(8,128)(2,1)S(1)}, bf16[128,512]{1,0:T(8,128)(2,1)S(1)}) custom-call(s32[5]{0:T(128)S(1)} %copy-done.5, bf16[4,512,512]{2,1,0:T(8,128)(2,1)S(1)} %turn.1.alpha, bf16[512,512]{1,0:T(8,128)(2,1)S(1)} %bitcast.13, ...), custom_call_target="tpu_custom_call" | custom-call | flops 1 | bytes 1 | tf_op jit(solution)/shard_map/expect/pallas_call | solution.py:233
  61.6 0.1 collective-permute-start.19
  61.7 1.1 %collective-permute-done.19 = f32[4,1,128]{2,1,0:T(1,128)S(1)} collective-permute-done((f32[4,1,128]{2,1,0:T(1,128)S(1)}, f32[4,1,128]{2,1,0:T(1,128)S(1)}, u32[]{:S(2)}, u32[]{:S(2)}) %collective-permute-start.19) | collective-permute-done | bytes 2080 | tf_op jit(solution)/shard_map/ppermute | solution.py:344
  62.9 0.6 broadcast_in_dim.16
  63.5 5.2 %all-to-all-start.1 = ((f32[32,1,128]{2,1,0:T(1,128)}), f32[32,1,128]{2,1,0:T(1,128)S(1)}, u32[]{:S(2)}, u32[]{:S(2)}) async-start(f32[32,1,128]{2,1,0:T(1,128)} %bitcast.10), calls=%async_computation.1 | async-start | bytes 32768 | tf_op jit(solution)/shard_map/all_to_all | solution.py:346
  68.7 1.5 %collective-permute-start.16 = (bf16[128,512]{1,0:T(8,128)(2,1)S(1)}, bf16[128,512]{1,0:T(8,128)(2,1)S(1)}, u32[]{:S(2)}, u32[]{:S(2)}) collective-permute-start(bf16[128,512]{1,0:T(8,128)(2,1)S(1)} %get-tuple-element.46), channel_id=1, source_target_pairs={{0,16},{16,32},{32,48},{48,0},{1,17},{17,33},{33,49},{49,1},{2,18}... | collective-permute-start | bytes 393224 | tf_op jit(solution)/shard_map/ppermute | solution.py:347
  70.3 0.8 %collective-permute-start.17 = (bf16[128,512]{1,0:T(8,128)(2,1)S(1)}, bf16[128,512]{1,0:T(8,128)(2,1)S(1)}, u32[]{:S(2)}, u32[]{:S(2)}) collective-permute-start(bf16[128,512]{1,0:T(8,128)(2,1)S(1)} %get-tuple-element.47), channel_id=1, source_target_pairs={{0,32},{16,48},{32,0},{48,16},{1,33},{17,49},{33,1},{49,17},{2,34}... | collective-permute-start | bytes 393224 | tf_op jit(solution)/shard_map/ppermute | solution.py:347
  71.1 2.4 %collective-permute-start.18 = (bf16[128,512]{1,0:T(8,128)(2,1)S(1)}, bf16[128,512]{1,0:T(8,128)(2,1)S(1)}, u32[]{:S(2)}, u32[]{:S(2)}) collective-permute-start(bf16[128,512]{1,0:T(8,128)(2,1)S(1)} %get-tuple-element.48), channel_id=1, source_target_pairs={{0,48},{16,0},{32,16},{48,32},{1,49},{17,1},{33,17},{49,33},{2,50}... | collective-permute-start | bytes 393224 | tf_op jit(solution)/shard_map/ppermute | solution.py:347
  73.6 3.7 %all-to-all-done.1.sums = f32[32,1,128]{2,1,0:T(1,128)S(1)} async-done(((f32[32,1,128]{2,1,0:T(1,128)}), f32[32,1,128]{2,1,0:T(1,128)S(1)}, u32[]{:S(2)}, u32[]{:S(2)}) %all-to-all-start.1) | async-done | bytes 16416 | tf_op jit(solution)/shard_map/all_to_all | solution.py:346
  77.3 0.1 column.1.rate
  77.4 0.8 %collective-permute-done.17.e2 = bf16[128,512]{1,0:T(8,128)(2,1)S(1)} collective-permute-done((bf16[128,512]{1,0:T(8,128)(2,1)S(1)}, bf16[128,512]{1,0:T(8,128)(2,1)S(1)}, u32[]{:S(2)}, u32[]{:S(2)}) %collective-permute-start.17) | collective-permute-done | bytes 131104 | tf_op jit(solution)/shard_map/ppermute | solution.py:347
  78.3 0.7 collective-permute-done.18.e3
  79.0 1.8 %finish.1 = (f32[128,2048]{1,0:T(8,128)}, bf16[128,2048]{1,0:T(8,128)(2,1)}) custom-call(s32[5]{0:T(128)S(1)} %copy-done.5, bf16[128,2048]{1,0:T(8,128)(2,1)S(1)} %copy-done, f32[4,128,512]{2,1,0:T(8,128)S(1)} %get-tuple-element.45.total, bf16[128,512]{1,0:T(8,128)(2,1)S(1)} %collective-permute-done.16.e1, bf16[128,512]{1,0:T(8,128)(2,1)S(1)} %collective-permute-done.17.e2, ...), custom_call_target="tpu_custom_call" | custom-call | flops 1 | bytes 1 | tf_op jit(solution)/shard_map/finish/pallas_call | solution.py:286
  (23 shorter events, 0.1 us)
Async XLA Ops:
  0.6 15.3 %copy-start.2 = (bf16[128,128]{1,0:T(8,128)(2,1)S(1)}, bf16[128,128]{1,0:T(8,128)(2,1)}, u32[]{:S(2)}) copy-start(bf16[128,128]{1,0:T(8,128)(2,1)} %param.6) | copy-start | bytes 98308
  0.7 1.0 %copy-start.1 = (bf16[128,2048]{1,0:T(8,128)(2,1)S(1)}, bf16[128,2048]{1,0:T(8,128)(2,1)}, u32[]{:S(2)}) copy-start(bf16[128,2048]{1,0:T(8,128)(2,1)} %a.1) | copy-start | bytes 1572868
  1.8 8.7 %copy-start.4 = (s32[5]{0:T(128)}, s32[5]{0:T(128)S(1)}, u32[]{:S(2)}) copy-start(s32[5]{0:T(128)S(1)} %stack.23.pos) | copy-start | bytes 64
  2.4 13.5 %collective-permute-start.1 = (bf16[128,512]{1,0:T(8,128)(2,1)S(1)}, bf16[128,512]{1,0:T(8,128)(2,1)S(1)}, u32[]{:S(2)}, u32[]{:S(2)}) collective-permute-start(bf16[128,512]{1,0:T(8,128)(2,1)S(1)} %get-tuple-element.27), channel_id=1, source_target_pairs={{0,16},{16,32},{32,48},{48,0},{1,17},{17,33},{33,49},{49,1},{2,18}... | collective-permute-start | bytes 393224 | tf_op jit(solution)/shard_map/ppermute | solution.py:318
  3.9 11.9 %collective-permute-start.2 = (bf16[128,512]{1,0:T(8,128)(2,1)S(1)}, bf16[128,512]{1,0:T(8,128)(2,1)S(1)}, u32[]{:S(2)}, u32[]{:S(2)}) collective-permute-start(bf16[128,512]{1,0:T(8,128)(2,1)S(1)} %get-tuple-element.28), channel_id=1, source_target_pairs={{0,32},{16,48},{32,0},{48,16},{1,33},{17,49},{33,1},{49,17},{2,34}... | collective-permute-start | bytes 393224 | tf_op jit(solution)/shard_map/ppermute | solution.py:318
  6.8 9.1 %collective-permute-start.3 = (bf16[128,512]{1,0:T(8,128)(2,1)S(1)}, bf16[128,512]{1,0:T(8,128)(2,1)S(1)}, u32[]{:S(2)}, u32[]{:S(2)}) collective-permute-start(bf16[128,512]{1,0:T(8,128)(2,1)S(1)} %get-tuple-element.29), channel_id=1, source_target_pairs={{0,48},{16,0},{32,16},{48,32},{1,49},{17,1},{33,17},{49,33},{2,50}... | collective-permute-start | bytes 393224 | tf_op jit(solution)/shard_map/ppermute | solution.py:318
  7.2 8.7 %collective-permute-start = (bf16[1,128,128]{2,1,0:T(8,128)(2,1)}, bf16[1,128,128]{2,1,0:T(8,128)(2,1)S(1)}, u32[]{:S(2)}, u32[]{:S(2)}) collective-permute-start(bf16[1,128,128]{2,1,0:T(8,128)(2,1)} %bitcast.14), channel_id=1, source_target_pairs={{0,4},{2,6},{4,0},{6,2},{8,12},{10,14},{12,8},{14,10},{1,5},{3,7},... | collective-permute-start | bytes 98312 | tf_op jit(solution)/shard_map/ppermute | solution.py:315
  15.9 10.5 %collective-permute-start.4 = (bf16[2,128,128]{2,1,0:T(8,128)(2,1)S(1)}, bf16[2,128,128]{2,1,0:T(8,128)(2,1)S(1)}, u32[]{:S(2)}, u32[]{:S(2)}) collective-permute-start(bf16[2,128,128]{2,1,0:T(8,128)(2,1)S(1)} %pad_maximum_fusion), channel_id=1, source_target_pairs={{0,12},{2,14},{4,8},{6,10},{8,4},{10,6},{12,0},{14,2},{1,13},{3,15... | collective-permute-start | bytes 196616 | tf_op jit(solution)/shard_map/ppermute | solution.py:315
  20.5 15.0 %all-to-all-start = ((bf16[16,32,512]{2,1,0:T(8,128)(2,1)}), bf16[16,32,512]{2,1,0:T(8,128)(2,1)S(1)}, u32[]{:S(2)}, u32[]{:S(2)}) async-start(bf16[16,32,512]{2,1,0:T(8,128)(2,1)} %bitcast.20), calls=%async_computation | async-start | bytes 1048576 | tf_op jit(solution)/shard_map/all_to_all | solution.py:322
  26.4 1.2 %copy-start.3 = (s32[2048]{0:T(1024)S(1)}, s32[2048]{0:T(1024)}, u32[]{:S(2)}) copy-start(s32[2048]{0:T(1024)} %param.5) | copy-start | bytes 24580
  26.4 1.2 %copy-start.5 = (s32[5]{0:T(128)S(1)}, s32[5]{0:T(128)}, u32[]{:S(2)}) copy-start(s32[5]{0:T(128)} %copy-done.4) | copy-start | bytes 64
  26.5 5.1 %copy-start = (bf16[128,2048]{1,0:T(8,128)(2,1)S(1)}, bf16[128,2048]{1,0:T(8,128)(2,1)}, u32[]{:S(2)}) copy-start(bf16[128,2048]{1,0:T(8,128)(2,1)} %transition.5) | copy-start | bytes 1572868
  26.5 5.1 %collective-permute-start.5 = (bf16[4,128,128]{2,1,0:T(8,128)(2,1)S(1)}, bf16[4,128,128]{2,1,0:T(8,128)(2,1)S(1)}, u32[]{:S(2)}, u32[]{:S(2)}) collective-permute-start(bf16[4,128,128]{2,1,0:T(8,128)(2,1)S(1)} %join.1), channel_id=1, source_target_pairs={{0,2},{2,0},{4,6},{6,4},{8,10},{10,8},{12,14},{14,12},{1,3},{3,1},... | collective-permute-start | bytes 393224 | tf_op jit(solution)/shard_map/ppermute | solution.py:315
  32.2 9.3 %collective-permute-start.6 = (bf16[16,128,128]{2,1,0:T(8,128)(2,1)S(1)}, bf16[16,128,128]{2,1,0:T(8,128)(2,1)S(1)}, u32[]{:S(2)}, u32[]{:S(2)}) collective-permute-start(bf16[16,128,128]{2,1,0:T(8,128)(2,1)S(1)} %get-tuple-element.33), channel_id=1, source_target_pairs={{0,16},{1,49},{16,32},{17,1},{32,48},{33,17},{48,0},{49,33},{2,18}... | collective-permute-start | bytes 1572872 | tf_op jit(solution)/shard_map/ppermute | solution.py:331
  36.5 12.7 %collective-permute-start.14 = (bf16[512,512]{1,0:T(8,128)(2,1)S(1)}, bf16[512,512]{1,0:T(8,128)(2,1)S(1)}, u32[]{:S(2)}, u32[]{:S(2)}) collective-permute-start(bf16[512,512]{1,0:T(8,128)(2,1)S(1)} %bitcast.11), channel_id=1, source_target_pairs={{0,64},{1,193},{64,128},{65,1},{128,192},{129,65},{192,0},{193,129... | collective-permute-start | bytes 1572872 | tf_op jit(solution)/shard_map/ppermute | solution.py:328
  36.5 12.7 %collective-permute-start.9 = (bf16[512,512]{1,0:T(8,128)(2,1)S(1)}, bf16[512,512]{1,0:T(8,128)(2,1)S(1)}, u32[]{:S(2)}, u32[]{:S(2)}) collective-permute-start(bf16[512,512]{1,0:T(8,128)(2,1)S(1)} %bitcast.12), channel_id=1, source_target_pairs={{64,0},{193,1},{128,64},{1,65},{192,128},{65,129},{0,192},{129,193... | collective-permute-start | bytes 1572872 | tf_op jit(solution)/shard_map/ppermute | solution.py:329
  41.5 9.6 %collective-permute-start.8 = (bf16[12,128,128]{2,1,0:T(8,128)(2,1)S(1)}, bf16[12,128,128]{2,1,0:T(8,128)(2,1)S(1)}, u32[]{:S(2)}, u32[]{:S(2)}) collective-permute-start(bf16[12,128,128]{2,1,0:T(8,128)(2,1)S(1)} %slice.3), channel_id=1, source_target_pairs={{0,16},{1,49},{16,32},{17,1},{32,48},{33,17},{48,0},{49,33},{2,18}... | collective-permute-start | bytes 1179656 | tf_op jit(solution)/shard_map/ppermute | solution.py:337
  43.1 8.6 %collective-permute-start.7 = (bf16[12,128,128]{2,1,0:T(8,128)(2,1)S(1)}, bf16[12,128,128]{2,1,0:T(8,128)(2,1)S(1)}, u32[]{:S(2)}, u32[]{:S(2)}) collective-permute-start(bf16[12,128,128]{2,1,0:T(8,128)(2,1)S(1)} %get-tuple-element.35.refs_0_), channel_id=1, source_target_pairs={{16,0},{49,1},{32,16},{1,17},{48,32},{17,33},{0,48},{33,49},{18,2}... | collective-permute-start | bytes 1179656 | tf_op jit(solution)/shard_map/ppermute | solution.py:333
  49.2 10.4 %collective-permute-start.15 = (bf16[512,512]{1,0:T(8,128)(2,1)S(1)}, bf16[512,512]{1,0:T(8,128)(2,1)S(1)}, u32[]{:S(2)}, u32[]{:S(2)}) collective-permute-start(bf16[512,512]{1,0:T(8,128)(2,1)S(1)} %collective-permute-done.14.s1), channel_id=1, source_target_pairs={{0,64},{1,193},{64,128},{65,1},{128,192},{129,65},{192,0},{193,129... | collective-permute-start | bytes 1572872 | tf_op jit(solution)/shard_map/ppermute | solution.py:335
  49.2 2.5 %collective-permute-start.10 = (bf16[12,128,128]{2,1,0:T(8,128)(2,1)S(1)}, bf16[12,128,128]{2,1,0:T(8,128)(2,1)S(1)}, u32[]{:S(2)}, u32[]{:S(2)}) collective-permute-start(bf16[12,128,128]{2,1,0:T(8,128)(2,1)S(1)} %get-tuple-element.35.refs_0_), channel_id=1, source_target_pairs={{0,1},{1,0},{2,3},{3,2},{4,5},{5,4},{6,7},{7,6},{8,9},{9,8},{10,11... | collective-permute-start | bytes 1179656 | tf_op jit(solution)/shard_map/ppermute | solution.py:340
  51.1 1.7 %collective-permute-start.11 = (bf16[12,128,128]{2,1,0:T(8,128)(2,1)S(1)}, bf16[12,128,128]{2,1,0:T(8,128)(2,1)S(1)}, u32[]{:S(2)}, u32[]{:S(2)}) collective-permute-start(bf16[12,128,128]{2,1,0:T(8,128)(2,1)S(1)} %slice.3), channel_id=1, source_target_pairs={{0,1},{1,0},{2,3},{3,2},{4,5},{5,4},{6,7},{7,6},{8,9},{9,8},{10,11... | collective-permute-start | bytes 1179656 | tf_op jit(solution)/shard_map/ppermute | solution.py:340
  51.1 2.3 %collective-permute-start.13 = (bf16[12,128,128]{2,1,0:T(8,128)(2,1)S(1)}, bf16[12,128,128]{2,1,0:T(8,128)(2,1)S(1)}, u32[]{:S(2)}, u32[]{:S(2)}) collective-permute-start(bf16[12,128,128]{2,1,0:T(8,128)(2,1)S(1)} %collective-permute-done.8.refs_3_.t3), channel_id=1, source_target_pairs={{0,1},{1,0},{2,3},{3,2},{4,5},{5,4},{6,7},{7,6},{8,9},{9,8},{10,11... | collective-permute-start | bytes 1179656 | tf_op jit(solution)/shard_map/ppermute | solution.py:340
  51.6 2.3 %collective-permute-start.12 = (bf16[12,128,128]{2,1,0:T(8,128)(2,1)S(1)}, bf16[12,128,128]{2,1,0:T(8,128)(2,1)S(1)}, u32[]{:S(2)}, u32[]{:S(2)}) collective-permute-start(bf16[12,128,128]{2,1,0:T(8,128)(2,1)S(1)} %collective-permute-done.7.refs_2_.t2), channel_id=1, source_target_pairs={{0,1},{1,0},{2,3},{3,2},{4,5},{5,4},{6,7},{7,6},{8,9},{9,8},{10,11... | collective-permute-start | bytes 1179656 | tf_op jit(solution)/shard_map/ppermute | solution.py:340
  61.6 1.2 %collective-permute-start.19 = (f32[4,1,128]{2,1,0:T(1,128)S(1)}, f32[4,1,128]{2,1,0:T(1,128)S(1)}, u32[]{:S(2)}, u32[]{:S(2)}) collective-permute-start(f32[4,1,128]{2,1,0:T(1,128)S(1)} %get-tuple-element.49), channel_id=1, source_target_pairs={{0,1},{1,0},{2,3},{3,2},{4,5},{5,4},{6,7},{7,6},{8,9},{9,8},{10,11... | collective-permute-start | bytes 6152 | tf_op jit(solution)/shard_map/ppermute | solution.py:344
  63.5 13.8 %all-to-all-start.1 = ((f32[32,1,128]{2,1,0:T(1,128)}), f32[32,1,128]{2,1,0:T(1,128)S(1)}, u32[]{:S(2)}, u32[]{:S(2)}) async-start(f32[32,1,128]{2,1,0:T(1,128)} %bitcast.10), calls=%async_computation.1 | async-start | bytes 32768 | tf_op jit(solution)/shard_map/all_to_all | solution.py:346
  68.7 8.7 %collective-permute-start.16 = (bf16[128,512]{1,0:T(8,128)(2,1)S(1)}, bf16[128,512]{1,0:T(8,128)(2,1)S(1)}, u32[]{:S(2)}, u32[]{:S(2)}) collective-permute-start(bf16[128,512]{1,0:T(8,128)(2,1)S(1)} %get-tuple-element.46), channel_id=1, source_target_pairs={{0,16},{16,32},{32,48},{48,0},{1,17},{17,33},{33,49},{49,1},{2,18}... | collective-permute-start | bytes 393224 | tf_op jit(solution)/shard_map/ppermute | solution.py:347
  70.3 8.0 %collective-permute-start.17 = (bf16[128,512]{1,0:T(8,128)(2,1)S(1)}, bf16[128,512]{1,0:T(8,128)(2,1)S(1)}, u32[]{:S(2)}, u32[]{:S(2)}) collective-permute-start(bf16[128,512]{1,0:T(8,128)(2,1)S(1)} %get-tuple-element.47), channel_id=1, source_target_pairs={{0,32},{16,48},{32,0},{48,16},{1,33},{17,49},{33,1},{49,17},{2,34}... | collective-permute-start | bytes 393224 | tf_op jit(solution)/shard_map/ppermute | solution.py:347
  71.1 7.9 %collective-permute-start.18 = (bf16[128,512]{1,0:T(8,128)(2,1)S(1)}, bf16[128,512]{1,0:T(8,128)(2,1)S(1)}, u32[]{:S(2)}, u32[]{:S(2)}) collective-permute-start(bf16[128,512]{1,0:T(8,128)(2,1)S(1)} %get-tuple-element.48), channel_id=1, source_target_pairs={{0,48},{16,0},{32,16},{48,32},{1,49},{17,1},{33,17},{49,33},{2,50}... | collective-permute-start | bytes 393224 | tf_op jit(solution)/shard_map/ppermute | solution.py:347

commit v5 on v4

--- a/solution.py
+++ b/solution.py
@@ -342,8 +342,8 @@
 
     total, sums, *parts = expect(pos, alpha_t, (own, one, two, far), transition, (one_a, two_a, far_a))
     sums = sums + lax.ppermute(sums, "k", swap)
-    sums = jnp.broadcast_to(sums[:, None], (4, 8, 1, 128)).reshape(32, 1, 128)
-    sums = lax.all_to_all(sums, ("x", "z"), 0, 0)
+    sums = jnp.broadcast_to(sums[None], (8, 4, 1, 128)).reshape(32, 1, 128)
+    sums = lax.all_to_all(sums, ("z", "x"), 0, 0)
     parts = [lax.ppermute(e, "x", ring(d)) for d, e in enumerate(parts, 1)]
     return finish(pos, transition, total, parts, column(sums))
 

time: 81.3 us -> 81.2 us (level)
  no operation moved by 1% of the time
where the time goes in v5:
time: 81.2 us; the launch traced here: 80.9 us
  starting transfers between devices  37.3 us (46%)
  waiting for transfers between devices  27.3 us (34%)
  Pallas kernels  13.5 us (17%)
  local copies, waits for them, and re-layouts  1.79 us (2%)
  between operations  1.01 us (1%)
    ppermute x3, starting transfers between devices, per_device(): flip = lambda a, by: lax.ppermute(a, 'z', [(i, i ^ by) for i in range(8)])  8.95 us
    all_to_all x1, starting transfers between devices, per_device(): rows = lax.all_to_all(picked.reshape(16, 32, 512), ('y', 'x'), 0, 0)  5.94 us
    ppermute x1, waiting for transfers between devices, per_device(): one = lax.ppermute(own, ('y', 'k'), ahead)  5.53 us
    pallas_call x1, Pallas kernels, pick(): pl.pallas_call(pick_kernel, in_specs=[SM, VM, pl.BlockSpec(memory_space=p...  5.38 us
    all_to_all x1, starting transfers between devices, per_device(): sums = lax.all_to_all(sums, ('z', 'x'), 0, 0)  5.24 us
    ppermute x3, starting transfers between devices, per_device(): lax.ppermute(c, 'x', ring(d))  4.83 us
    ppermute x3, starting transfers between devices, per_device(): parts = [lax.ppermute(e, 'x', ring(d)) for d, e in enumerate(parts, 1)]  4.78 us
    ppermute x1, waiting for transfers between devices, per_device(): far = lax.ppermute(one, ('y', 'k'), ahead)  4.43 us
  transfers between devices with their start and end apart: 22, of which 13 were waited for; matrix products, arithmetic and copies ran while one was open for 0% of the time, Pallas kernels for 11%

profile of v5, /device:TPU:2, one launch (start us, length us, event | category | flops | bytes accessed | tf_op | source)
XLA Modules:
  0.0 80.9 jit_solution(16232859651442655508)
XLA Ops:
  0.6 0.0 copy-start.2
  0.6 0.1 stack.23.pos
  0.7 1.0 %copy-done.1 = bf16[128,2048]{1,0:T(8,128)(2,1)S(1)} copy-done((bf16[128,2048]{1,0:T(8,128)(2,1)S(1)}, bf16[128,2048]{1,0:T(8,128)(2,1)}, u32[]{:S(2)}) %copy-start.1) | copy-done | bytes 524312
  1.8 0.6 cut.1
  2.4 1.6 %collective-permute-start.1 = (bf16[128,512]{1,0:T(8,128)(2,1)S(1)}, bf16[128,512]{1,0:T(8,128)(2,1)S(1)}, u32[]{:S(2)}, u32[]{:S(2)}) collective-permute-start(bf16[128,512]{1,0:T(8,128)(2,1)S(1)} %get-tuple-element.27), channel_id=1, source_target_pairs={{0,16},{16,32},{32,48},{48,0},{1,17},{17,33},{33,49},{49,1},{2,18}... | collective-permute-start | bytes 393224 | tf_op jit(solution)/shard_map/ppermute | solution.py:318
  3.9 2.8 %collective-permute-start.2 = (bf16[128,512]{1,0:T(8,128)(2,1)S(1)}, bf16[128,512]{1,0:T(8,128)(2,1)S(1)}, u32[]{:S(2)}, u32[]{:S(2)}) collective-permute-start(bf16[128,512]{1,0:T(8,128)(2,1)S(1)} %get-tuple-element.28), channel_id=1, source_target_pairs={{0,32},{16,48},{32,0},{48,16},{1,33},{17,49},{33,1},{49,17},{2,34}... | collective-permute-start | bytes 393224 | tf_op jit(solution)/shard_map/ppermute | solution.py:318
  6.8 0.4 collective-permute-start.3
  7.2 3.3 %collective-permute-start = (bf16[1,128,128]{2,1,0:T(8,128)(2,1)}, bf16[1,128,128]{2,1,0:T(8,128)(2,1)S(1)}, u32[]{:S(2)}, u32[]{:S(2)}) collective-permute-start(bf16[1,128,128]{2,1,0:T(8,128)(2,1)} %bitcast.14), channel_id=1, source_target_pairs={{0,4},{2,6},{4,0},{6,2},{8,12},{10,14},{12,8},{14,10},{1,5},{3,7},... | collective-permute-start | bytes 98312 | tf_op jit(solution)/shard_map/ppermute | solution.py:315
  10.5 5.4 %pick.1 = bf16[4,4,32,512]{3,2,1,0:T(8,128)(2,1)} custom-call(s32[5]{0:T(128)} %copy-done.4, s32[16,128]{1,0:T(8,128)} %bitcast.18, bf16[2000,2048]{1,0:T(8,128)(2,1)} %table.1), custom_call_target="tpu_custom_call" | custom-call | flops 1 | bytes 1 | tf_op jit(solution)/shard_map/pick/pallas_call | solution.py:71
  15.9 4.6 %collective-permute-start.4 = (bf16[2,128,128]{2,1,0:T(8,128)(2,1)S(1)}, bf16[2,128,128]{2,1,0:T(8,128)(2,1)S(1)}, u32[]{:S(2)}, u32[]{:S(2)}) collective-permute-start(bf16[2,128,128]{2,1,0:T(8,128)(2,1)S(1)} %pad_maximum_fusion), channel_id=1, source_target_pairs={{0,12},{2,14},{4,8},{6,10},{8,4},{10,6},{12,0},{14,2},{1,13},{3,15... | collective-permute-start | bytes 196616 | tf_op jit(solution)/shard_map/ppermute | solution.py:315
  20.5 5.9 %all-to-all-start = ((bf16[16,32,512]{2,1,0:T(8,128)(2,1)}), bf16[16,32,512]{2,1,0:T(8,128)(2,1)S(1)}, u32[]{:S(2)}, u32[]{:S(2)}) async-start(bf16[16,32,512]{2,1,0:T(8,128)(2,1)} %bitcast.20), calls=%async_computation | async-start | bytes 1048576 | tf_op jit(solution)/shard_map/all_to_all | solution.py:322
  26.4 0.0 copy-start.5
  26.5 0.0 copy-start
  26.5 1.1 %collective-permute-start.5 = (bf16[4,128,128]{2,1,0:T(8,128)(2,1)S(1)}, bf16[4,128,128]{2,1,0:T(8,128)(2,1)S(1)}, u32[]{:S(2)}, u32[]{:S(2)}) collective-permute-start(bf16[4,128,128]{2,1,0:T(8,128)(2,1)S(1)} %join.1), channel_id=1, source_target_pairs={{0,2},{2,0},{4,6},{6,4},{8,10},{10,8},{12,14},{14,12},{1,3},{3,1},... | collective-permute-start | bytes 393224 | tf_op jit(solution)/shard_map/ppermute | solution.py:315
  27.6 0.8 moves.1.move
  28.4 3.1 %collective-permute-done.5.l3 = bf16[4,128,128]{2,1,0:T(8,128)(2,1)S(1)} collective-permute-done((bf16[4,128,128]{2,1,0:T(8,128)(2,1)S(1)}, bf16[4,128,128]{2,1,0:T(8,128)(2,1)S(1)}, u32[]{:S(2)}, u32[]{:S(2)}) %collective-permute-start.5) | collective-permute-done | bytes 131104 | tf_op jit(solution)/shard_map/ppermute | solution.py:315
  31.6 0.7 pack.1
  32.2 1.5 %collective-permute-start.6 = (bf16[16,128,128]{2,1,0:T(8,128)(2,1)S(1)}, bf16[16,128,128]{2,1,0:T(8,128)(2,1)S(1)}, u32[]{:S(2)}, u32[]{:S(2)}) collective-permute-start(bf16[16,128,128]{2,1,0:T(8,128)(2,1)S(1)} %get-tuple-element.33), channel_id=1, source_target_pairs={{0,16},{1,49},{16,32},{17,1},{32,48},{33,17},{48,0},{49,33},{2,18}... | collective-permute-start | bytes 1572872 | tf_op jit(solution)/shard_map/ppermute | solution.py:331
  33.8 1.7 %all-to-all-done.rows = bf16[16,32,512]{2,1,0:T(8,128)(2,1)S(1)} async-done(((bf16[16,32,512]{2,1,0:T(8,128)(2,1)}), bf16[16,32,512]{2,1,0:T(8,128)(2,1)S(1)}, u32[]{:S(2)}, u32[]{:S(2)}) %all-to-all-start) | async-done | bytes 524320 | tf_op jit(solution)/shard_map/all_to_all | solution.py:322
  35.5 0.9 %scale.1 = bf16[4,128,512]{2,1,0:T(8,128)(2,1)S(1)} custom-call(s32[5]{0:T(128)S(1)} %copy-done.5, bf16[4,128,128]{2,1,0:T(8,128)(2,1)S(1)} %moves.1.move, bf16[16,32,512]{2,1,0:T(8,128)(2,1)S(1)} %all-to-all-done.rows, bf16[128,512]{1,0:T(8,128)(2,1)S(1)} %get-tuple-element.38.c0, bf16[128,512]{1,0:T(8,128)(2,1)S(1)} %collective-permute-done.1.c1, ...), custom_call_target="tpu_custom_call" | custom-call | flops 10000000000 | bytes 10000000 | tf_op jit(solution)/shard_map/scale/pallas_call | solution.py:119
  36.5 0.1 collective-permute-start.14
  36.5 3.2 %collective-permute-start.9 = (bf16[512,512]{1,0:T(8,128)(2,1)S(1)}, bf16[512,512]{1,0:T(8,128)(2,1)S(1)}, u32[]{:S(2)}, u32[]{:S(2)}) collective-permute-start(bf16[512,512]{1,0:T(8,128)(2,1)S(1)} %bitcast.12), channel_id=1, source_target_pairs={{64,0},{193,1},{128,64},{1,65},{192,128},{65,129},{0,192},{129,193... | collective-permute-start | bytes 1572872 | tf_op jit(solution)/shard_map/ppermute | solution.py:329
  39.8 1.7 %collective-permute-done.6.refs_1_.t1 = bf16[16,128,128]{2,1,0:T(8,128)(2,1)S(1)} collective-permute-done((bf16[16,128,128]{2,1,0:T(8,128)(2,1)S(1)}, bf16[16,128,128]{2,1,0:T(8,128)(2,1)S(1)}, u32[]{:S(2)}, u32[]{:S(2)}) %collective-permute-start.6) | collective-permute-done | bytes 524320 | tf_op jit(solution)/shard_map/ppermute | solution.py:331
  41.5 1.5 %collective-permute-start.8 = (bf16[12,128,128]{2,1,0:T(8,128)(2,1)S(1)}, bf16[12,128,128]{2,1,0:T(8,128)(2,1)S(1)}, u32[]{:S(2)}, u32[]{:S(2)}) collective-permute-start(bf16[12,128,128]{2,1,0:T(8,128)(2,1)S(1)} %slice.3), channel_id=1, source_target_pairs={{0,16},{1,49},{16,32},{17,1},{32,48},{33,17},{48,0},{49,33},{2,18}... | collective-permute-start | bytes 1179656 | tf_op jit(solution)/shard_map/ppermute | solution.py:337
  43.1 0.6 collective-permute-start.7
  43.6 5.5 %collective-permute-done.14.s1 = bf16[512,512]{1,0:T(8,128)(2,1)S(1)} collective-permute-done((bf16[512,512]{1,0:T(8,128)(2,1)S(1)}, bf16[512,512]{1,0:T(8,128)(2,1)S(1)}, u32[]{:S(2)}, u32[]{:S(2)}) %collective-permute-start.14) | collective-permute-done | bytes 524320 | tf_op jit(solution)/shard_map/ppermute | solution.py:328
  49.2 0.0 collective-permute-start.15
  49.2 1.9 %collective-permute-done.8.refs_3_.t3 = bf16[12,128,128]{2,1,0:T(8,128)(2,1)S(1)} collective-permute-done((bf16[12,128,128]{2,1,0:T(8,128)(2,1)S(1)}, bf16[12,128,128]{2,1,0:T(8,128)(2,1)S(1)}, u32[]{:S(2)}, u32[]{:S(2)}) %collective-permute-start.8) | collective-permute-done | bytes 393248 | tf_op jit(solution)/shard_map/ppermute | solution.py:337
  51.1 0.5 collective-permute-start.13
  51.6 0.0 collective-permute-start.12
  51.7 1.2 %collective-permute-done.11.refs_5_ = bf16[12,128,128]{2,1,0:T(8,128)(2,1)S(1)} collective-permute-done((bf16[12,128,128]{2,1,0:T(8,128)(2,1)S(1)}, bf16[12,128,128]{2,1,0:T(8,128)(2,1)S(1)}, u32[]{:S(2)}, u32[]{:S(2)}) %collective-permute-start.11) | collective-permute-done | bytes 393248 | tf_op jit(solution)/shard_map/ppermute | solution.py:340
  52.9 0.6 collective-permute-done.13.refs_7_
  53.4 0.6 collective-permute-done.12.refs_6_
  54.0 1.1 %turn.1.alpha = bf16[4,512,512]{2,1,0:T(8,128)(2,1)S(1)} custom-call(s32[5]{0:T(128)S(1)} %copy-done.5, bf16[12,128,128]{2,1,0:T(8,128)(2,1)S(1)} %get-tuple-element.35.refs_0_, bf16[16,128,128]{2,1,0:T(8,128)(2,1)S(1)} %collective-permute-done.6.refs_1_.t1, bf16[12,128,128]{2,1,0:T(8,128)(2,1)S(1)} %collective-permute-done.7.refs_2_.t2, ...), custom_call_target="tpu_custom_call" | custom-call | flops 1 | bytes 1 | tf_op jit(solution)/shard_map/turn/pallas_call | solution.py:196
  55.1 4.4 %collective-permute-done.15.s3 = bf16[512,512]{1,0:T(8,128)(2,1)S(1)} collective-permute-done((bf16[512,512]{1,0:T(8,128)(2,1)S(1)}, bf16[512,512]{1,0:T(8,128)(2,1)S(1)}, u32[]{:S(2)}, u32[]{:S(2)}) %collective-permute-start.15) | collective-permute-done | bytes 524320 | tf_op jit(solution)/shard_map/ppermute | solution.py:335
  59.5 2.1 %expect.1 = (f32[4,128,512]{2,1,0:T(8,128)S(1)}, f32[4,1,128]{2,1,0:T(1,128)S(1)}, bf16[128,512]{1,0:T(8,128)(2,1)S(1)}, bf16[128,512]{1,0:T(8,128)(2,1)S(1)}, bf16[128,512]{1,0:T(8,128)(2,1)S(1)}) custom-call(s32[5]{0:T(128)S(1)} %copy-done.5, bf16[4,512,512]{2,1,0:T(8,128)(2,1)S(1)} %turn.1.alpha, bf16[512,512]{1,0:T(8,128)(2,1)S(1)} %bitcast.13, ...), custom_call_target="tpu_custom_call" | custom-call | flops 1 | bytes 1 | tf_op jit(solution)/shard_map/expect/pallas_call | solution.py:233
  61.6 0.1 collective-permute-start.19
  61.7 1.1 %collective-permute-done.19 = f32[4,1,128]{2,1,0:T(1,128)S(1)} collective-permute-done((f32[4,1,128]{2,1,0:T(1,128)S(1)}, f32[4,1,128]{2,1,0:T(1,128)S(1)}, u32[]{:S(2)}, u32[]{:S(2)}) %collective-permute-start.19) | collective-permute-done | bytes 2080 | tf_op jit(solution)/shard_map/ppermute | solution.py:344
  62.9 0.6 broadcast_in_dim.16
  63.5 5.2 %all-to-all-start.1 = ((f32[32,1,128]{2,1,0:T(1,128)}), f32[32,1,128]{2,1,0:T(1,128)S(1)}, u32[]{:S(2)}, u32[]{:S(2)}) async-start(f32[32,1,128]{2,1,0:T(1,128)} %bitcast.10), calls=%async_computation.1 | async-start | bytes 32768 | tf_op jit(solution)/shard_map/all_to_all | solution.py:346
  68.7 1.5 %collective-permute-start.16 = (bf16[128,512]{1,0:T(8,128)(2,1)S(1)}, bf16[128,512]{1,0:T(8,128)(2,1)S(1)}, u32[]{:S(2)}, u32[]{:S(2)}) collective-permute-start(bf16[128,512]{1,0:T(8,128)(2,1)S(1)} %get-tuple-element.46), channel_id=1, source_target_pairs={{0,16},{16,32},{32,48},{48,0},{1,17},{17,33},{33,49},{49,1},{2,18}... | collective-permute-start | bytes 393224 | tf_op jit(solution)/shard_map/ppermute | solution.py:347
  70.3 0.8 %collective-permute-start.17 = (bf16[128,512]{1,0:T(8,128)(2,1)S(1)}, bf16[128,512]{1,0:T(8,128)(2,1)S(1)}, u32[]{:S(2)}, u32[]{:S(2)}) collective-permute-start(bf16[128,512]{1,0:T(8,128)(2,1)S(1)} %get-tuple-element.47), channel_id=1, source_target_pairs={{0,32},{16,48},{32,0},{48,16},{1,33},{17,49},{33,1},{49,17},{2,34}... | collective-permute-start | bytes 393224 | tf_op jit(solution)/shard_map/ppermute | solution.py:347
  71.1 2.4 %collective-permute-start.18 = (bf16[128,512]{1,0:T(8,128)(2,1)S(1)}, bf16[128,512]{1,0:T(8,128)(2,1)S(1)}, u32[]{:S(2)}, u32[]{:S(2)}) collective-permute-start(bf16[128,512]{1,0:T(8,128)(2,1)S(1)} %get-tuple-element.48), channel_id=1, source_target_pairs={{0,48},{16,0},{32,16},{48,32},{1,49},{17,1},{33,17},{49,33},{2,50}... | collective-permute-start | bytes 393224 | tf_op jit(solution)/shard_map/ppermute | solution.py:347
  73.5 3.7 %all-to-all-done.1.sums = f32[32,1,128]{2,1,0:T(1,128)S(1)} async-done(((f32[32,1,128]{2,1,0:T(1,128)}), f32[32,1,128]{2,1,0:T(1,128)S(1)}, u32[]{:S(2)}, u32[]{:S(2)}) %all-to-all-start.1) | async-done | bytes 16416 | tf_op jit(solution)/shard_map/all_to_all | solution.py:346
  77.2 0.1 column.1.rate
  77.3 0.8 %collective-permute-done.17.e2 = bf16[128,512]{1,0:T(8,128)(2,1)S(1)} collective-permute-done((bf16[128,512]{1,0:T(8,128)(2,1)S(1)}, bf16[128,512]{1,0:T(8,128)(2,1)S(1)}, u32[]{:S(2)}, u32[]{:S(2)}) %collective-permute-start.17) | collective-permute-done | bytes 131104 | tf_op jit(solution)/shard_map/ppermute | solution.py:347
  78.2 0.8 %collective-permute-done.18.e3 = bf16[128,512]{1,0:T(8,128)(2,1)S(1)} collective-permute-done((bf16[128,512]{1,0:T(8,128)(2,1)S(1)}, bf16[128,512]{1,0:T(8,128)(2,1)S(1)}, u32[]{:S(2)}, u32[]{:S(2)}) %collective-permute-start.18) | collective-permute-done | bytes 131104 | tf_op jit(solution)/shard_map/ppermute | solution.py:347
  79.0 1.8 %finish.1 = (f32[128,2048]{1,0:T(8,128)}, bf16[128,2048]{1,0:T(8,128)(2,1)}) custom-call(s32[5]{0:T(128)S(1)} %copy-done.5, bf16[128,2048]{1,0:T(8,128)(2,1)S(1)} %copy-done, f32[4,128,512]{2,1,0:T(8,128)S(1)} %get-tuple-element.45.total, bf16[128,512]{1,0:T(8,128)(2,1)S(1)} %collective-permute-done.16.e1, bf16[128,512]{1,0:T(8,128)(2,1)S(1)} %collective-permute-done.17.e2, ...), custom_call_target="tpu_custom_call" | custom-call | flops 1 | bytes 1 | tf_op jit(solution)/shard_map/finish/pallas_call | solution.py:286
  (23 shorter events, 0.1 us)
Async XLA Ops:
  0.6 15.3 %copy-start.2 = (bf16[128,128]{1,0:T(8,128)(2,1)S(1)}, bf16[128,128]{1,0:T(8,128)(2,1)}, u32[]{:S(2)}) copy-start(bf16[128,128]{1,0:T(8,128)(2,1)} %param.6) | copy-start | bytes 98308
  0.7 1.0 %copy-start.1 = (bf16[128,2048]{1,0:T(8,128)(2,1)S(1)}, bf16[128,2048]{1,0:T(8,128)(2,1)}, u32[]{:S(2)}) copy-start(bf16[128,2048]{1,0:T(8,128)(2,1)} %a.1) | copy-start | bytes 1572868
  1.8 8.7 %copy-start.4 = (s32[5]{0:T(128)}, s32[5]{0:T(128)S(1)}, u32[]{:S(2)}) copy-start(s32[5]{0:T(128)S(1)} %stack.23.pos) | copy-start | bytes 64
  2.4 13.5 %collective-permute-start.1 = (bf16[128,512]{1,0:T(8,128)(2,1)S(1)}, bf16[128,512]{1,0:T(8,128)(2,1)S(1)}, u32[]{:S(2)}, u32[]{:S(2)}) collective-permute-start(bf16[128,512]{1,0:T(8,128)(2,1)S(1)} %get-tuple-element.27), channel_id=1, source_target_pairs={{0,16},{16,32},{32,48},{48,0},{1,17},{17,33},{33,49},{49,1},{2,18}... | collective-permute-start | bytes 393224 | tf_op jit(solution)/shard_map/ppermute | solution.py:318
  3.9 11.9 %collective-permute-start.2 = (bf16[128,512]{1,0:T(8,128)(2,1)S(1)}, bf16[128,512]{1,0:T(8,128)(2,1)S(1)}, u32[]{:S(2)}, u32[]{:S(2)}) collective-permute-start(bf16[128,512]{1,0:T(8,128)(2,1)S(1)} %get-tuple-element.28), channel_id=1, source_target_pairs={{0,32},{16,48},{32,0},{48,16},{1,33},{17,49},{33,1},{49,17},{2,34}... | collective-permute-start | bytes 393224 | tf_op jit(solution)/shard_map/ppermute | solution.py:318
  6.8 9.1 %collective-permute-start.3 = (bf16[128,512]{1,0:T(8,128)(2,1)S(1)}, bf16[128,512]{1,0:T(8,128)(2,1)S(1)}, u32[]{:S(2)}, u32[]{:S(2)}) collective-permute-start(bf16[128,512]{1,0:T(8,128)(2,1)S(1)} %get-tuple-element.29), channel_id=1, source_target_pairs={{0,48},{16,0},{32,16},{48,32},{1,49},{17,1},{33,17},{49,33},{2,50}... | collective-permute-start | bytes 393224 | tf_op jit(solution)/shard_map/ppermute | solution.py:318
  7.2 8.7 %collective-permute-start = (bf16[1,128,128]{2,1,0:T(8,128)(2,1)}, bf16[1,128,128]{2,1,0:T(8,128)(2,1)S(1)}, u32[]{:S(2)}, u32[]{:S(2)}) collective-permute-start(bf16[1,128,128]{2,1,0:T(8,128)(2,1)} %bitcast.14), channel_id=1, source_target_pairs={{0,4},{2,6},{4,0},{6,2},{8,12},{10,14},{12,8},{14,10},{1,5},{3,7},... | collective-permute-start | bytes 98312 | tf_op jit(solution)/shard_map/ppermute | solution.py:315
  15.9 10.5 %collective-permute-start.4 = (bf16[2,128,128]{2,1,0:T(8,128)(2,1)S(1)}, bf16[2,128,128]{2,1,0:T(8,128)(2,1)S(1)}, u32[]{:S(2)}, u32[]{:S(2)}) collective-permute-start(bf16[2,128,128]{2,1,0:T(8,128)(2,1)S(1)} %pad_maximum_fusion), channel_id=1, source_target_pairs={{0,12},{2,14},{4,8},{6,10},{8,4},{10,6},{12,0},{14,2},{1,13},{3,15... | collective-permute-start | bytes 196616 | tf_op jit(solution)/shard_map/ppermute | solution.py:315
  20.5 15.0 %all-to-all-start = ((bf16[16,32,512]{2,1,0:T(8,128)(2,1)}), bf16[16,32,512]{2,1,0:T(8,128)(2,1)S(1)}, u32[]{:S(2)}, u32[]{:S(2)}) async-start(bf16[16,32,512]{2,1,0:T(8,128)(2,1)} %bitcast.20), calls=%async_computation | async-start | bytes 1048576 | tf_op jit(solution)/shard_map/all_to_all | solution.py:322
  26.4 1.2 %copy-start.3 = (s32[2048]{0:T(1024)S(1)}, s32[2048]{0:T(1024)}, u32[]{:S(2)}) copy-start(s32[2048]{0:T(1024)} %param.5) | copy-start | bytes 24580
  26.4 1.2 %copy-start.5 = (s32[5]{0:T(128)S(1)}, s32[5]{0:T(128)}, u32[]{:S(2)}) copy-start(s32[5]{0:T(128)} %copy-done.4) | copy-start | bytes 64
  26.5 5.1 %copy-start = (bf16[128,2048]{1,0:T(8,128)(2,1)S(1)}, bf16[128,2048]{1,0:T(8,128)(2,1)}, u32[]{:S(2)}) copy-start(bf16[128,2048]{1,0:T(8,128)(2,1)} %transition.5) | copy-start | bytes 1572868
  26.5 5.1 %collective-permute-start.5 = (bf16[4,128,128]{2,1,0:T(8,128)(2,1)S(1)}, bf16[4,128,128]{2,1,0:T(8,128)(2,1)S(1)}, u32[]{:S(2)}, u32[]{:S(2)}) collective-permute-start(bf16[4,128,128]{2,1,0:T(8,128)(2,1)S(1)} %join.1), channel_id=1, source_target_pairs={{0,2},{2,0},{4,6},{6,4},{8,10},{10,8},{12,14},{14,12},{1,3},{3,1},... | collective-permute-start | bytes 393224 | tf_op jit(solution)/shard_map/ppermute | solution.py:315
  32.2 9.3 %collective-permute-start.6 = (bf16[16,128,128]{2,1,0:T(8,128)(2,1)S(1)}, bf16[16,128,128]{2,1,0:T(8,128)(2,1)S(1)}, u32[]{:S(2)}, u32[]{:S(2)}) collective-permute-start(bf16[16,128,128]{2,1,0:T(8,128)(2,1)S(1)} %get-tuple-element.33), channel_id=1, source_target_pairs={{0,16},{1,49},{16,32},{17,1},{32,48},{33,17},{48,0},{49,33},{2,18}... | collective-permute-start | bytes 1572872 | tf_op jit(solution)/shard_map/ppermute | solution.py:331
  36.5 12.7 %collective-permute-start.14 = (bf16[512,512]{1,0:T(8,128)(2,1)S(1)}, bf16[512,512]{1,0:T(8,128)(2,1)S(1)}, u32[]{:S(2)}, u32[]{:S(2)}) collective-permute-start(bf16[512,512]{1,0:T(8,128)(2,1)S(1)} %bitcast.11), channel_id=1, source_target_pairs={{0,64},{1,193},{64,128},{65,1},{128,192},{129,65},{192,0},{193,129... | collective-permute-start | bytes 1572872 | tf_op jit(solution)/shard_map/ppermute | solution.py:328
  36.5 12.7 %collective-permute-start.9 = (bf16[512,512]{1,0:T(8,128)(2,1)S(1)}, bf16[512,512]{1,0:T(8,128)(2,1)S(1)}, u32[]{:S(2)}, u32[]{:S(2)}) collective-permute-start(bf16[512,512]{1,0:T(8,128)(2,1)S(1)} %bitcast.12), channel_id=1, source_target_pairs={{64,0},{193,1},{128,64},{1,65},{192,128},{65,129},{0,192},{129,193... | collective-permute-start | bytes 1572872 | tf_op jit(solution)/shard_map/ppermute | solution.py:329
  41.5 9.6 %collective-permute-start.8 = (bf16[12,128,128]{2,1,0:T(8,128)(2,1)S(1)}, bf16[12,128,128]{2,1,0:T(8,128)(2,1)S(1)}, u32[]{:S(2)}, u32[]{:S(2)}) collective-permute-start(bf16[12,128,128]{2,1,0:T(8,128)(2,1)S(1)} %slice.3), channel_id=1, source_target_pairs={{0,16},{1,49},{16,32},{17,1},{32,48},{33,17},{48,0},{49,33},{2,18}... | collective-permute-start | bytes 1179656 | tf_op jit(solution)/shard_map/ppermute | solution.py:337
  43.1 8.6 %collective-permute-start.7 = (bf16[12,128,128]{2,1,0:T(8,128)(2,1)S(1)}, bf16[12,128,128]{2,1,0:T(8,128)(2,1)S(1)}, u32[]{:S(2)}, u32[]{:S(2)}) collective-permute-start(bf16[12,128,128]{2,1,0:T(8,128)(2,1)S(1)} %get-tuple-element.35.refs_0_), channel_id=1, source_target_pairs={{16,0},{49,1},{32,16},{1,17},{48,32},{17,33},{0,48},{33,49},{18,2}... | collective-permute-start | bytes 1179656 | tf_op jit(solution)/shard_map/ppermute | solution.py:333
  49.2 10.4 %collective-permute-start.15 = (bf16[512,512]{1,0:T(8,128)(2,1)S(1)}, bf16[512,512]{1,0:T(8,128)(2,1)S(1)}, u32[]{:S(2)}, u32[]{:S(2)}) collective-permute-start(bf16[512,512]{1,0:T(8,128)(2,1)S(1)} %collective-permute-done.14.s1), channel_id=1, source_target_pairs={{0,64},{1,193},{64,128},{65,1},{128,192},{129,65},{192,0},{193,129... | collective-permute-start | bytes 1572872 | tf_op jit(solution)/shard_map/ppermute | solution.py:335
  49.2 2.5 %collective-permute-start.10 = (bf16[12,128,128]{2,1,0:T(8,128)(2,1)S(1)}, bf16[12,128,128]{2,1,0:T(8,128)(2,1)S(1)}, u32[]{:S(2)}, u32[]{:S(2)}) collective-permute-start(bf16[12,128,128]{2,1,0:T(8,128)(2,1)S(1)} %get-tuple-element.35.refs_0_), channel_id=1, source_target_pairs={{0,1},{1,0},{2,3},{3,2},{4,5},{5,4},{6,7},{7,6},{8,9},{9,8},{10,11... | collective-permute-start | bytes 1179656 | tf_op jit(solution)/shard_map/ppermute | solution.py:340
  51.1 1.7 %collective-permute-start.11 = (bf16[12,128,128]{2,1,0:T(8,128)(2,1)S(1)}, bf16[12,128,128]{2,1,0:T(8,128)(2,1)S(1)}, u32[]{:S(2)}, u32[]{:S(2)}) collective-permute-start(bf16[12,128,128]{2,1,0:T(8,128)(2,1)S(1)} %slice.3), channel_id=1, source_target_pairs={{0,1},{1,0},{2,3},{3,2},{4,5},{5,4},{6,7},{7,6},{8,9},{9,8},{10,11... | collective-permute-start | bytes 1179656 | tf_op jit(solution)/shard_map/ppermute | solution.py:340
  51.1 2.3 %collective-permute-start.13 = (bf16[12,128,128]{2,1,0:T(8,128)(2,1)S(1)}, bf16[12,128,128]{2,1,0:T(8,128)(2,1)S(1)}, u32[]{:S(2)}, u32[]{:S(2)}) collective-permute-start(bf16[12,128,128]{2,1,0:T(8,128)(2,1)S(1)} %collective-permute-done.8.refs_3_.t3), channel_id=1, source_target_pairs={{0,1},{1,0},{2,3},{3,2},{4,5},{5,4},{6,7},{7,6},{8,9},{9,8},{10,11... | collective-permute-start | bytes 1179656 | tf_op jit(solution)/shard_map/ppermute | solution.py:340
  51.6 2.3 %collective-permute-start.12 = (bf16[12,128,128]{2,1,0:T(8,128)(2,1)S(1)}, bf16[12,128,128]{2,1,0:T(8,128)(2,1)S(1)}, u32[]{:S(2)}, u32[]{:S(2)}) collective-permute-start(bf16[12,128,128]{2,1,0:T(8,128)(2,1)S(1)} %collective-permute-done.7.refs_2_.t2), channel_id=1, source_target_pairs={{0,1},{1,0},{2,3},{3,2},{4,5},{5,4},{6,7},{7,6},{8,9},{9,8},{10,11... | collective-permute-start | bytes 1179656 | tf_op jit(solution)/shard_map/ppermute | solution.py:340
  61.6 1.2 %collective-permute-start.19 = (f32[4,1,128]{2,1,0:T(1,128)S(1)}, f32[4,1,128]{2,1,0:T(1,128)S(1)}, u32[]{:S(2)}, u32[]{:S(2)}) collective-permute-start(f32[4,1,128]{2,1,0:T(1,128)S(1)} %get-tuple-element.49), channel_id=1, source_target_pairs={{0,1},{1,0},{2,3},{3,2},{4,5},{5,4},{6,7},{7,6},{8,9},{9,8},{10,11... | collective-permute-start | bytes 6152 | tf_op jit(solution)/shard_map/ppermute | solution.py:344
  63.5 13.7 %all-to-all-start.1 = ((f32[32,1,128]{2,1,0:T(1,128)}), f32[32,1,128]{2,1,0:T(1,128)S(1)}, u32[]{:S(2)}, u32[]{:S(2)}) async-start(f32[32,1,128]{2,1,0:T(1,128)} %bitcast.10), calls=%async_computation.1 | async-start | bytes 32768 | tf_op jit(solution)/shard_map/all_to_all | solution.py:346
  68.7 8.6 %collective-permute-start.16 = (bf16[128,512]{1,0:T(8,128)(2,1)S(1)}, bf16[128,512]{1,0:T(8,128)(2,1)S(1)}, u32[]{:S(2)}, u32[]{:S(2)}) collective-permute-start(bf16[128,512]{1,0:T(8,128)(2,1)S(1)} %get-tuple-element.46), channel_id=1, source_target_pairs={{0,16},{16,32},{32,48},{48,0},{1,17},{17,33},{33,49},{49,1},{2,18}... | collective-permute-start | bytes 393224 | tf_op jit(solution)/shard_map/ppermute | solution.py:347
  70.3 7.9 %collective-permute-start.17 = (bf16[128,512]{1,0:T(8,128)(2,1)S(1)}, bf16[128,512]{1,0:T(8,128)(2,1)S(1)}, u32[]{:S(2)}, u32[]{:S(2)}) collective-permute-start(bf16[128,512]{1,0:T(8,128)(2,1)S(1)} %get-tuple-element.47), channel_id=1, source_target_pairs={{0,32},{16,48},{32,0},{48,16},{1,33},{17,49},{33,1},{49,17},{2,34}... | collective-permute-start | bytes 393224 | tf_op jit(solution)/shard_map/ppermute | solution.py:347
  71.1 7.9 %collective-permute-start.18 = (bf16[128,512]{1,0:T(8,128)(2,1)S(1)}, bf16[128,512]{1,0:T(8,128)(2,1)S(1)}, u32[]{:S(2)}, u32[]{:S(2)}) collective-permute-start(bf16[128,512]{1,0:T(8,128)(2,1)S(1)} %get-tuple-element.48), channel_id=1, source_target_pairs={{0,48},{16,0},{32,16},{48,32},{1,49},{17,1},{33,17},{49,33},{2,50}... | collective-permute-start | bytes 393224 | tf_op jit(solution)/shard_map/ppermute | solution.py:347
